TPU v7x, 32 devices: a whole 2x2x4 slice. The times are simulated.
32 devices in a mesh: groups: 2 (over x), dp: 16 (over z, y, core).
Axes of the slice: x: 2, y: 2, z: 4, core: 2. Of those that a mesh axis runs over, the one named last changes fastest.
Arguments:
- tokens: bfloat16 [8192, 8192], P(('groups', 'dp')), parts along dimension 0, may hold values from -6 to 6
- output_gradient: bfloat16 [8192, 1024], P(('groups', 'dp')), parts along dimension 0, may hold values from -6 to 6
- adapter_hidden_state: bfloat16 [8192, 64], P(('groups', 'dp')), parts along dimension 0, may hold values from -6 to 6
- frozen_value_weight: bfloat16 [8192, 1024], P('dp'), may hold values from -0.1875 to 0.1875
- adapter_down_maps: bfloat16 [16384, 256], P(('groups', 'dp')), parts along dimension 0, may hold values from -0.75 to 0.75
- adapter_up_maps: bfloat16 [512, 1024], P('groups'), parts along dimension 0, may hold values from -0.1875 to 0.1875
- members: int32 [64], P('groups'), parts along dimension 0, may hold values from 0 to 3, never falling along the last dimension, each value on 1 to 16 neighbouring positions
Outputs:
- layer_input_gradient: bfloat16 [8192, 8192], P(('groups', 'dp')), parts along dimension 0
- down_grad: float32 [16384, 256], P(('groups', 'dp')), parts along dimension 0
- up_map_gradient: float32 [512, 1024], P('groups'), parts along dimension 0
There are 2 independent parts, one for each index of `groups`. A program takes and returns all parts, laid end to end along the dimension named above; an argument that names none is the same for every part. Nothing has to cross between parts.
Inputs may be any that keep to these rules, and one draw needn't show every extreme that they name: members never falls from one block to the next, and every member owns at least one block.
All inputs are finite; a program needn't handle non-finite values.
Results may differ from a plain program's by a relative error of at most 0.008.
Values may be sent and summed in bfloat16 or wider, within the bound.
No kernel may reach another device: no remote copies, remote signals or barrier semaphores. Data moves between devices by JAX's collectives and lax.ppermute only.
A program may use at most 128 MiB of HBM per device.

v0:
```python
import jax
import jax.numpy as jnp
from jax import lax
from jax.sharding import PartitionSpec as P

ADAPTER_RANK = 64
MEMBER_COUNT = 4
BLOCK = 128


adapter_scale = 2.0


def member_mask(members, dtype):
    return (members[:, None] == jnp.arange(MEMBER_COUNT, dtype=jnp.int32)[None, :]).astype(dtype)


def expand(members, values):
    blocks = members.shape[0]
    onehot = member_mask(members, values.dtype)
    shaped = values.reshape(blocks, BLOCK, 1, ADAPTER_RANK)
    expanded_rows = shaped * onehot[:, None, :, None]
    return expanded_rows.reshape(blocks * BLOCK, MEMBER_COUNT * ADAPTER_RANK)


def member_selector(members, widened_gradient):
    blocks = members.shape[0]
    onehot = member_mask(members, widened_gradient.dtype)
    shaped = widened_gradient.reshape(blocks, BLOCK, MEMBER_COUNT, ADAPTER_RANK)
    return jnp.sum(shaped * onehot[:, None, :, None], axis=2).reshape(blocks * BLOCK, ADAPTER_RANK)


def local(
    tokens,
    output_gradient,
    adapter_hidden_state,
    frozen_value_weight,
    adapter_down_maps,
    adapter_up_maps,
    members,
):
    local_rows = tokens.shape[0]
    local_blocks = local_rows // BLOCK
    offset = lax.axis_index("dp") * local_blocks
    member_ownership = lax.dynamic_slice_in_dim(members, offset, local_blocks)
    widened_gradient = jnp.dot(
        output_gradient, adapter_up_maps.T, preferred_element_type=jnp.float32
    )
    adapter_gradient = (adapter_scale * member_selector(member_ownership, widened_gradient)).astype(
        jnp.bfloat16
    )
    expanded_rows = expand(member_ownership, adapter_gradient)
    frozen_output = jnp.dot(
        output_gradient,
        lax.all_gather(frozen_value_weight, "dp", axis=0, tiled=True).T,
        preferred_element_type=jnp.float32,
    )
    adapter_contribution = jnp.dot(
        expanded_rows,
        lax.all_gather(adapter_down_maps, "dp", axis=0, tiled=True).T,
        preferred_element_type=jnp.float32,
    ).astype(jnp.bfloat16)
    down_grad = lax.psum_scatter(
        jnp.dot(tokens.T, expanded_rows, preferred_element_type=jnp.float32),
        "dp",
        scatter_dimension=0,
        tiled=True,
    )
    adapter_contribution = lax.optimization_barrier(adapter_contribution)
    layer_input_gradient = (frozen_output + adapter_contribution.astype(jnp.float32)).astype(
        jnp.bfloat16
    )
    hidden_state_expanded = expand(member_ownership, adapter_hidden_state)
    partial_up_gradient = adapter_scale * jnp.dot(
        hidden_state_expanded.T, output_gradient, preferred_element_type=jnp.float32
    )
    up_map_gradient = lax.psum(partial_up_gradient, "dp")
    return (layer_input_gradient, down_grad, up_map_gradient)


def solution(mesh):
    in_specs = (
        P(("groups", "dp"), None),
        P(("groups", "dp"), None),
        P(("groups", "dp"), None),
        P("dp", None),
        P(("groups", "dp"), None),
        P("groups", None),
        P("groups"),
    )
    out_specs = (P(("groups", "dp"), None), P(("groups", "dp"), None), P("groups", None))
    return jax.shard_map(local, mesh=mesh, in_specs=in_specs, out_specs=out_specs, check_vma=False)
```

profile of v0, /device:TPU:0, one launch (start us, length us, event | category | flops | bytes accessed | tf_op | source)
XLA Modules:
  0.0 404.0 jit_solution(6583863228047465599)
XLA Ops:
  7.2 0.0 copy-start
  7.2 0.0 all-gather.5.cloned.1.call-start
  7.2 0.7 all-gather.5.cloned.1.call-update
  7.9 0.0 reduce-scatter.2.cloned.1.call-start
  8.0 0.8 mul.70
  8.7 0.0 copy-done
  8.7 1.4 fusion.9
  10.1 0.1 reshape.63
  10.3 0.7 dynamic_slice.3
  11.0 0.2 multiply_reduce_fusion
  11.3 0.3 broadcast_multiply_fusion
  11.5 6.7 %convolution_bitcast_fusion = f32[8192,256]{0,1:T(8,128)} fusion(bf16[256,8192]{1,0:T(8,128)(2,1)} %param.7, bf16[32,8,2,128]{3,2,1,0:T(2,128)(2,1)S(1)} %bitcast.29), kind=kOutput, calls=%fused_computation | convolution fusion | flops 1073741824 | bytes 12713984 | tf_op jit(solution)/shard_map/dot_general | solution.py:64
  18.2 0.0 reduce-scatter.2.cloned.1.call-update
  18.2 0.0 all-gather.3.cloned.1.call-start
  18.3 0.7 all-gather.3.cloned.1.call-update
  19.0 0.0 all-reduce.2.cloned.1.call-start
  19.0 1.3 convolution_multiply_fusion
  20.3 0.0 all-reduce.2.cloned.1.call-update
  20.3 43.2 %all-gather.5.cloned.1.call-done = bf16[8192,256]{1,0:T(8,128)(2,1)} async-done(((bf16[512,256]{1,0:T(8,128)(2,1)}), bf16[8192,256]{1,0:T(8,128)(2,1)}) %all-gather.5.cloned.1.call-update) | async-done | bytes 4194320 | tf_op jit(solution)/shard_map/all_gather | solution.py:60
  63.5 5.5 %convolution_convert_fusion = bf16[256,8192]{1,0:T(8,128)(2,1)} fusion(bf16[8192,256]{1,0:T(8,128)(2,1)} %all-gather.5.cloned.1.call-done, bf16[32,8,2,128]{3,2,1,0:T(2,128)(2,1)S(1)} %bitcast.30), kind=kOutput, calls=%fused_computation.2 | convolution fusion | flops 1075838976 | bytes 8519680 | tf_op jit(solution)/shard_map/dot_general | solution.py:58
  69.0 101.9 %reduce-scatter.2.cloned.1.call-done = f32[512,256]{0,1:T(8,128)} async-done(((f32[8192,256]{0,1:T(8,128)}), f32[512,256]{0,1:T(8,128)}) %reduce-scatter.2.cloned.1.call-update) | async-done | bytes 524304 | tf_op jit(solution)/shard_map/reduce_scatter | solution.py:63
  170.9 2.0 copy.13
  172.9 126.8 %all-gather.3.cloned.1.call-done = bf16[8192,1024]{1,0:T(8,128)(2,1)} async-done(((bf16[512,1024]{1,0:T(8,128)(2,1)}), bf16[8192,1024]{1,0:T(8,128)(2,1)}) %all-gather.3.cloned.1.call-update) | async-done | bytes 16777232 | tf_op jit(solution)/shard_map/all_gather | solution.py:55
  299.8 10.7 %fusion = bf16[256,8192]{1,0:T(8,128)(2,1)} fusion(bf16[256,1024]{1,0:T(8,128)(2,1)S(1)} %copy-done, bf16[8192,1024]{1,0:T(8,128)(2,1)} %all-gather.3.cloned.1.call-done, bf16[256,8192]{1,0:T(8,128)(2,1)} %convolution_convert_fusion), kind=kOutput, calls=%fused_computation.3 | convolution fusion | flops 4301258752 | bytes 25690112 | tf_op jit(solution)/shard_map/dot_general | solution.py:53
  310.4 84.8 %all-reduce.2.cloned.1.call-done = f32[256,1024]{1,0:T(8,128)} async-done(((f32[256,1024]{1,0:T(8,128)}), f32[256,1024]{1,0:T(8,128)}) %all-reduce.2.cloned.1.call-update) | async-done | bytes 1048592 | tf_op jit(solution)/shard_map/psum | solution.py:77
  395.2 2.3 copy.30
  (2 shorter events, 0.0 us)
Async XLA Ops:
  7.2 1.6 copy-start
  7.2 56.3 %all-gather.5.cloned.1.call-start = ((), (), s32[]{:S(2)}) async-start(), calls=%async_computation.2 | async-start | bytes 4456448 | tf_op jit(solution)/shard_map/all_gather | solution.py:60
  7.9 163.0 %reduce-scatter.2.cloned.1.call-start = ((), (), s32[]{:S(2)}) async-start(), calls=%async_computation.3 | async-start | bytes 8912896 | tf_op jit(solution)/shard_map/reduce_scatter | solution.py:63
  18.2 281.6 %all-gather.3.cloned.1.call-start = ((), (), s32[]{:S(2)}) async-start(), calls=%async_computation.1 | async-start | bytes 17825792 | tf_op jit(solution)/shard_map/all_gather | solution.py:55
  19.0 376.2 %all-reduce.2.cloned.1.call-start = ((), (), s32[]{:S(2)}) async-start(), calls=%async_computation.4 | async-start | bytes 2097152 | tf_op jit(solution)/shard_map/psum | solution.py:77
Sparse Core Ops, SparseCore 0:
  10.2 53.2 all-gather.4
  67.5 103.3 reduce-scatter.1
  173.1 126.6 all-gather.2
  303.7 91.4 all-reduce.1
where the time goes:
time: 404 us
  waiting for transfers between devices  358 us (89%)
  matrix products  25.5 us (6%)
  between operations  13.8 us (3%)
  local copies, waits for them, and re-layouts  6 us (1%)
    all_gather x1, waiting for transfers between devices, local(): lax.all_gather(frozen_value_weight, 'dp', axis=0, tiled=True)  127 us
    reduce_scatter x1, waiting for transfers between devices, local(): lax.psum_scatter(jnp.dot(tokens.T, expanded_rows, preferred_element_type=...  102 us
    psum x1, waiting for transfers between devices, local(): up_map_gradient = lax.psum(partial_up_gradient, 'dp')  84.8 us
    all_gather x1, waiting for transfers between devices, local(): lax.all_gather(adapter_down_maps, 'dp', axis=0, tiled=True)  43.2 us
    dot_general x1, matrix products, local(): jnp.dot(output_gradient, lax.all_gather(frozen_value_weight, 'dp', axis=0...  10.7 us
  transfers between devices with their start and end apart: 4, of which 4 were waited for; matrix products, arithmetic and copies ran while one was open for 7% of the time, Pallas kernels for 0%

commit v1 on v0

v1 whole, which is shorter than its diff:
```python
import functools

import jax
import jax.numpy as jnp
import numpy as np
from jax import lax
from jax.experimental import pallas as pl
from jax.experimental.pallas import tpu as pltpu
from jax.sharding import PartitionSpec as P

ADAPTER_RANK = 64
MEMBER_COUNT = 4
BLOCK = 128
INNER = 4

adapter_scale = 2.0

F32 = jnp.float32
BF16 = jnp.bfloat16
VMEM = pl.BlockSpec(memory_space=pltpu.VMEM)
SMEM = pl.BlockSpec(memory_space=pltpu.SMEM)
ANY = pl.BlockSpec(memory_space=pl.ANY)


def nt(a, b):
    return lax.dot_general(a, b, (((1,), (1,)), ((), ())), preferred_element_type=F32)


def tn(a, b):
    return lax.dot_general(a, b, (((0,), (0,)), ((), ())), preferred_element_type=F32)


def params(nbytes, **kw):
    return pltpu.CompilerParams(vmem_limit_bytes=nbytes, **kw)


def cost(flops, nbytes):
    return pl.CostEstimate(flops=flops, bytes_accessed=nbytes, transcendentals=0)


def where_am_i():
    me = lax.axis_index("dp")
    return me // INNER, me % INNER


def member_of_rows(members_ref, first_block, shape, dim):
    position = lax.broadcasted_iota(jnp.int32, shape, dim) // BLOCK
    result = jnp.zeros(shape, jnp.int32)
    for b in range(shape[dim] // BLOCK):
        result = jnp.where(position == b, members_ref[first_block + b], result)
    return result


def down_kernel(members, g, b, tok_send, tok_keep, send, keep, spread_t):
    rows = g.shape[0]
    width = b.shape[0]

    @pl.when(pl.program_id(0) == 0)
    def _():
        wide = nt(b[...], g[...])
        first = lax.axis_index("dp") * (rows // BLOCK)
        owner = member_of_rows(members, first, (width, rows), 1)
        column = lax.broadcasted_iota(jnp.int32, (width, rows), 0) // ADAPTER_RANK
        spread_t[...] = jnp.where(owner == column, adapter_scale * wide, 0.0).astype(BF16)

    left = spread_t[...]
    send[0] = jnp.dot(left, tok_send[...], preferred_element_type=F32).astype(BF16)
    keep[0] = jnp.dot(left, tok_keep[...], preferred_element_type=F32).astype(BF16)


def down_partials(members, g, b, tokens, per, n):
    rows, width = g.shape[0], b.shape[0]
    whole = lambda shape: pl.BlockSpec(shape, lambda i: (0, 0))
    out = pl.BlockSpec((1, width, per), lambda i: (i, 0, 0))
    shape = jax.ShapeDtypeStruct((n // 2, width, per), BF16)
    return pl.pallas_call(
        down_kernel,
        out_shape=(shape, shape),
        grid=(n // 2,),
        in_specs=[
            SMEM,
            whole(g.shape),
            whole(b.shape),
            pl.BlockSpec((rows, per), lambda i: (0, 2 * i + 1 - lax.axis_index("dp") % 2)),
            pl.BlockSpec((rows, per), lambda i: (0, 2 * i + lax.axis_index("dp") % 2)),
        ],
        out_specs=[out, out],
        scratch_shapes=[pltpu.VMEM((width, rows), BF16)],
        compiler_params=params(32 << 20),
        cost_estimate=cost(0, 0),
        name="down_partials",
    )(members, g, b, tokens, tokens)


def spread_kernel(members, b, *refs):
    gs, spread, up = refs[:INNER], refs[INNER], refs[INNER + 1]
    width, depth = b.shape
    rows = gs[0].shape[0]
    half, cols = up.shape
    z, q = where_am_i()
    total = jnp.zeros(up.shape, F32)
    for j in range(INNER):
        first = (z * INNER + (q ^ j)) * (rows // BLOCK)
        wide = nt(gs[j][:, :depth], b[...])
        owner = member_of_rows(members, first, (rows, width), 0)
        column = lax.broadcasted_iota(jnp.int32, (rows, width), 1) // ADAPTER_RANK
        spread[j] = jnp.where(owner == column, adapter_scale * wide, 0.0).astype(BF16)
        hidden = gs[j][:, depth:]
        hidden = jnp.concatenate([hidden] * (half // ADAPTER_RANK), axis=1)
        column = column[:, :half] + (q // 2) * (half // ADAPTER_RANK)
        hidden = jnp.where(owner[:, :half] == column, hidden, jnp.zeros_like(hidden))
        total = total + tn(hidden, gs[j][:, pl.ds(pl.multiple_of((q % 2) * cols, cols), cols)])
    up[...] = (adapter_scale * total).astype(BF16)


def spread_rows(members, b, gs):
    rows, (width, depth) = gs[0].shape[0], b.shape
    return pl.pallas_call(
        spread_kernel,
        out_shape=(
            jax.ShapeDtypeStruct((INNER, rows, width), BF16),
            jax.ShapeDtypeStruct((width // 2, depth // 2), BF16),
        ),
        in_specs=[SMEM] + [VMEM] * (1 + INNER),
        out_specs=[VMEM, VMEM],
        compiler_params=params(32 << 20),
        cost_estimate=cost(0, 0),
        name="spread_rows",
    )(members, b, *gs)


def multiply(gs, spread, w, a, outs, at):
    depth = w.shape[1]
    rows = gs[0].shape[0]
    for j in (2, 3, 1, 0):
        value = (nt(gs[j][:, :depth], w[...]) + nt(spread[j], a)).astype(BF16)
        if j < 2:
            outs[j][:, at] = value
        else:
            outs[2][(j - 2) * rows : (j - 1) * rows, at] = value


def own_kernel(w, a, spread, *refs):
    multiply(refs[:INNER], spread, w, a[...], refs[INNER:], slice(None))


def shard_kernel(turn, mine, theirs, a, spread, *refs):
    half = mine.shape[0]
    z, _ = where_am_i()
    parity = lax.axis_index("groups") % 2
    start = shard_of(turn, z) * (2 * half)
    for w, which in ((mine, parity), (theirs, 1 - parity)):
        at = pl.multiple_of(which * half, half)
        rows = pl.ds(pl.multiple_of(start + at, half), half)
        multiply(refs[:INNER], spread, w, a[rows, :], refs[INNER:], pl.ds(at, half))


def joined_kernel(turn, w, a, spread, *refs):
    per = w.shape[0]
    z, _ = where_am_i()
    rows = pl.ds(pl.multiple_of(shard_of(turn, z) * per, per), per)
    multiply(refs[:INNER], spread, w, a[rows, :], refs[INNER:], slice(None))


def product(kernel, per, gs, args, name):
    rows = gs[0].shape[0]
    shape = jax.ShapeDtypeStruct((rows, per), BF16)
    pair = jax.ShapeDtypeStruct((2 * rows, per), BF16)
    return pl.pallas_call(
        kernel,
        out_shape=(shape, shape, pair),
        in_specs=[VMEM] * (len(args) + INNER),
        out_specs=[VMEM] * 3,
        compiler_params=params(32 << 20),
        cost_estimate=cost(0, 0),
        name=name,
    )(*args, *gs)


def place_kernel(turn, own, core, across, both, *refs):
    out, sem = refs[-2], refs[-1]
    rows, per = own.shape
    z, q = where_am_i()
    shard = shard_of(turn, z)
    copies = []
    for j, piece in enumerate((own, core, across.at[:rows], both)):
        at = pl.ds(pl.multiple_of((shard * INNER + (q ^ j)) * per, per), per)
        copies.append(pltpu.make_async_copy(piece, out.at[:, at], sem.at[j]))
        copies[-1].start()
    for copy in copies:
        copy.wait()


def place(turn, pieces, out, shape):
    args = [*pieces] + ([out] if turn else [])
    return pl.pallas_call(
        functools.partial(place_kernel, turn),
        out_shape=shape,
        in_specs=[VMEM] * INNER + [ANY] * (len(args) - INNER),
        out_specs=ANY,
        scratch_shapes=[pltpu.SemaphoreType.DMA((INNER,))],
        input_output_aliases={len(args) - 1: 0} if turn else {},
        compiler_params=params(32 << 20),
        cost_estimate=cost(0, 0),
        name="place",
    )(*args)


def source(turn, z, planes):
    both = min(z, planes - 1 - z)
    if turn <= 2 * both:
        return (turn + 1) // 2, 1 - turn % 2
    even_is_far = (z % 2 == 0) == (z < planes // 2)
    return turn - both, 0 if even_is_far else 1


def far_plane(z, step, link):
    return z + step if z % 2 == link else z - step


def shard_of(turn, z):
    planes = lax.axis_size("dp") // INNER
    result = z
    if turn:
        for plane in range(planes):
            step, link = source(turn, plane, planes)
            result = jnp.where(z == plane, far_plane(plane, step, link), result)
    return result


def edges(step, link, planes):
    pairs = []
    for z in range(planes):
        right = z % 2 == link
        origin, to = (z - step + 1, z + 1) if right else (z + step - 1, z - 1)
        if 0 <= origin < planes and 0 <= to < planes:
            pairs.append((z, to))
    return pairs


def local(tokens, output_gradient, hidden, frozen, down_maps, up_maps, members):
    n = lax.axis_size("dp")
    groups = lax.axis_size("groups")
    planes = n // INNER
    me = lax.axis_index("dp")
    z, q = me // INNER, me % INNER
    parity = lax.axis_index("groups") % 2
    per = frozen.shape[0]
    width, depth = up_maps.shape

    def inner(x, bit):
        return lax.ppermute(x, "dp", [(i, i ^ bit) for i in range(n)])

    def along(x, pairs):
        return lax.ppermute(
            x, "dp", [(s * INNER + i, t * INNER + i) for s, t in pairs for i in range(INNER)]
        )

    def twin(x):
        return lax.ppermute(x, "groups", [(i, i ^ 1) for i in range(groups)])

    maps = lax.all_gather(
        down_maps,
        "dp",
        axis=0,
        tiled=True,
        axis_index_groups=[[p * INNER + i for p in range(planes)] for i in range(INNER)],
    )
    half = per // 2
    part = lax.dynamic_slice_in_dim(frozen, parity * half, half)
    packed = jnp.concatenate([output_gradient, hidden], axis=1)
    g2 = inner(packed, 2)
    held = {(0, 0): part, (0, 1): part}
    for k in range(1, planes):
        for link in (0, 1):
            pairs = edges(k, link, planes)
            if pairs:
                held[k, link] = along(held[k - 1, 1 - link], pairs)

    g1 = inner(packed, 1)
    g3 = inner(g2, 1)
    gs = [packed, g1, g2, g3]

    send, keep = down_partials(members, output_gradient, up_maps, tokens, per, n)
    got = inner(send, 1)
    spread, up = spread_rows(members, up_maps, gs)

    out_shape = jax.ShapeDtypeStruct(tokens.shape, BF16)
    rows = tokens.shape[0]

    def exchange(own, sibling, pair):
        across = inner(pair, 2)
        return own, inner(sibling, 1), across, inner(across[rows:], 1)

    blocks = product(own_kernel, per, gs, (frozen, down_maps, spread), "own_shard")
    result = place(0, exchange(*blocks), None, out_shape)
    for turn in range(1, planes):
        where = [source(turn, p, planes) for p in range(planes)]
        mine = held[where[0]]
        for option in sorted(set(where) - {where[0]}):
            hit = functools.reduce(
                jnp.logical_or, [z == p for p in range(planes) if where[p] == option]
            )
            mine = jnp.where(hit, held[option], mine)
        theirs = twin(mine)
        if half % 128:
            low, high = jnp.where(parity == 0, mine, theirs), jnp.where(parity == 0, theirs, mine)
            args = (jnp.concatenate([low, high]), maps, spread)
            kernel = functools.partial(joined_kernel, turn)
        else:
            args = (mine, theirs, maps, spread)
            kernel = functools.partial(shard_kernel, turn)
        blocks = product(kernel, per, gs, args, "shard")
        result = place(turn, exchange(*blocks), result, out_shape)

    keep = keep.reshape(planes, 2 * width, per)
    got = got.reshape(planes, 2 * width, per)
    up = up.reshape(planes, up.size // planes // per, per)

    def term(t):
        t = jnp.clip(t, 0, planes - 1)
        down = lax.dynamic_index_in_dim(keep, t, keepdims=False).astype(F32)
        down = down + lax.dynamic_index_in_dim(got, t, keepdims=False).astype(F32)
        return jnp.concatenate([down, lax.dynamic_index_in_dim(up, t, keepdims=False).astype(F32)])

    came = {}
    for k in range(planes - 1, 0, -1):
        for link in (0, 1):
            pairs = [(t, s) for s, t in edges(k, link, planes)]
            if pairs:
                value = term(jnp.where(z % 2 == link, z + k, z - k))
                if (k + 1, 1 - link) in came:
                    value = value + came[k + 1, 1 - link].astype(F32)
                came[k, link] = along(value.astype(BF16), pairs)
    total = term(z)
    for link in (0, 1):
        if (1, link) in came:
            total = total + came[1, link].astype(F32)
    y = q // 2
    down = total[: 2 * width].reshape(2, width, per)
    other = inner(lax.dynamic_index_in_dim(down, 1 - y, keepdims=False).astype(BF16), 2)
    down = lax.dynamic_index_in_dim(down, y, keepdims=False) + other.astype(F32)
    down_grad = down.T

    piece = total[2 * width :].astype(BF16)
    pieces = jnp.zeros((planes,) + piece.shape, BF16)
    pieces = lax.dynamic_update_index_in_dim(pieces, piece, z, 0)
    for k in range(1, planes):
        moved = along(piece, [(s, (s + k) % planes) for s in range(planes)])
        pieces = lax.dynamic_update_index_in_dim(pieces, moved, (z - k) % planes, 0)
    mine = pieces.reshape(width // 2, depth // 2)
    theirs = inner(mine, 2)
    mine = jnp.concatenate([jnp.where(y == 0, mine, theirs), jnp.where(y == 0, theirs, mine)])
    theirs = inner(mine, 1)
    c = q % 2
    up_grad = jnp.concatenate(
        [jnp.where(c == 0, mine, theirs), jnp.where(c == 0, theirs, mine)], axis=1
    ).astype(F32)
    return result, down_grad, up_grad


def solution(mesh):
    in_specs = (
        P(("groups", "dp"), None),
        P(("groups", "dp"), None),
        P(("groups", "dp"), None),
        P("dp", None),
        P(("groups", "dp"), None),
        P("groups", None),
        P("groups"),
    )
    out_specs = (P(("groups", "dp"), None), P(("groups", "dp"), None), P("groups", None))
    return jax.shard_map(local, mesh=mesh, in_specs=in_specs, out_specs=out_specs, check_vma=False)
```

time: 404 us -> 198 us (0.49)
  waiting for transfers between devices: 358 us -> 41.6 us
  starting transfers between devices: 0.16 us -> 69.2 us
  Pallas kernels: 0 us -> 25.6 us
  matrix products: 25.5 us -> 0 us
  local copies, waits for them, and re-layouts: 6 us -> 26.9 us
  other arithmetic: 0.49 us -> 19.1 us
    all_gather x2 -> x1, waiting for transfers between devices: 170 us -> 0.01 us  [local(): lax.all_gather(down_maps, 'dp', axis=0, tiled=True, axis_index_groups=[[p...]
    reduce_scatter x1 -> x0, waiting for transfers between devices: 102 us -> none  [local(): lax.psum_scatter(jnp.dot(tokens.T, expanded_rows, preferred_element_type=...]
    psum x1 -> x0, waiting for transfers between devices: 84.8 us -> none  [local(): up_map_gradient = lax.psum(partial_up_gradient, 'dp')]
    ppermute x0 -> x35, starting transfers between devices: none -> 69.1 us  [the longest x13 53.4 us: along(): lax.ppermute(x, 'dp', [(s * INNER + i, t * INNER + i) for s, t in pairs f...]
    ppermute x0 -> x35, waiting for transfers between devices: none -> 41.5 us  [the longest x19 18.6 us: inner(): return lax.ppermute(x, 'dp', [(i, i ^ bit) for i in range(n)])]
    pallas_call x0 -> x10, Pallas kernels: none -> 25.6 us  [the longest x4 11.6 us: product(): pl.pallas_call(kernel, out_shape=(shape, shape, pair), in_specs=[VMEM] *...]
    dot_general x5 -> x0, matrix products: 25.5 us -> none  [the longest x1 10.7 us: local(): jnp.dot(output_gradient, lax.all_gather(frozen_value_weight, 'dp', axis=0...]
    unnamed x4 -> x72, local copies, waits for them, and re-layouts: 4.35 us -> 15.6 us
  transfers between devices with their start and end apart: 4 -> 36, of which waited for: 4 -> 9; matrix products, arithmetic and copies ran while one was open for 7% -> 15% of each run, Pallas kernels for 0% -> 10%
where the time goes in v1:
time: 198 us; the launch traced here: 197 us
  starting transfers between devices  69.2 us (35%)
  waiting for transfers between devices  41.6 us (21%)
  local copies, waits for them, and re-layouts  26.9 us (14%)
  Pallas kernels  25.6 us (13%)
  other arithmetic  19.1 us (10%)
  between operations  14.5 us (7%)
    ppermute x13, starting transfers between devices, along(): lax.ppermute(x, 'dp', [(s * INNER + i, t * INNER + i) for s, t in pairs f...  53.4 us
    ppermute x19, waiting for transfers between devices, inner(): return lax.ppermute(x, 'dp', [(i, i ^ bit) for i in range(n)])  18.6 us
    unnamed x72, local copies, waits for them, and re-layouts  15.6 us
    ppermute x13, waiting for transfers between devices, along(): lax.ppermute(x, 'dp', [(s * INNER + i, t * INNER + i) for s, t in pairs f...  13 us
    ppermute x19, starting transfers between devices, inner(): return lax.ppermute(x, 'dp', [(i, i ^ bit) for i in range(n)])  12.1 us
    pallas_call x4, Pallas kernels, product(): pl.pallas_call(kernel, out_shape=(shape, shape, pair), in_specs=[VMEM] *...  11.6 us
    ppermute x3, waiting for transfers between devices, twin(): return lax.ppermute(x, 'groups', [(i, i ^ 1) for i in range(groups)])  9.87 us
    pallas_call x4, Pallas kernels, place(): pl.pallas_call(functools.partial(place_kernel, turn), out_shape=shape, in...  7.34 us
  transfers between devices with their start and end apart: 36, of which 9 were waited for; matrix products, arithmetic and copies ran while one was open for 15% of the time, Pallas kernels for 10%

profile of v1, /device:TPU:0, one launch (start us, length us, event | category | flops | bytes accessed | tf_op | source)
XLA Modules:
  0.0 196.9 jit_solution(6825089032356165407)
XLA Ops:
  7.2 2.2 %copy-done = bf16[256,8192]{1,0:T(8,128)(2,1)S(1)} copy-done((bf16[256,8192]{1,0:T(8,128)(2,1)S(1)}, bf16[256,8192]{1,0:T(8,128)(2,1)}, u32[]{:S(2)}) %copy-start) | copy-done | bytes 4194328
  9.4 1.0 copy-done.9
  10.4 1.0 copy-done.11
  12.1 5.2 %down_partials.1 = (bf16[8,256,512]{2,1,0:T(8,128)(2,1)}, bf16[8,256,512]{2,1,0:T(8,128)(2,1)S(1)}) custom-call(s32[32]{0:T(128)S(1)} %copy-done.22, bf16[256,1024]{1,0:T(8,128)(2,1)S(1)} %copy-done.9, bf16[256,1024]{1,0:T(8,128)(2,1)S(1)} %copy-done.11, bf16[256,8192]{1,0:T(8,128)(2,1)S(1)} %copy-done, bf16[256,8192]{1,0:T(8,128)(2,1)S(1)} %copy-done), custom_call_target="tpu_custom_call" | custom-call | tf_op jit(solution)/shard_map/down_partials/pallas_call | solution.py:76
  17.4 1.3 copy-done.5
  19.6 2.6 %collective-permute-start.5 = (bf16[256,1088]{0,1:T(8,128)(2,1)S(1)}, bf16[256,1088]{0,1:T(8,128)(2,1)S(1)}, u32[]{:S(2)}, u32[]{:S(2)}) collective-permute-start(bf16[256,1088]{0,1:T(8,128)(2,1)S(1)} %copy.17), channel_id=1, source_target_pairs={{0,2},{1,3},{2,0},{3,1},{4,6},{5,7},{6,4},{7,5},{8,10},{9,11},{10,... | collective-permute-start | bytes 1671176 | tf_op jit(solution)/shard_map/ppermute | solution.py:252
  22.4 13.1 %collective-permute-done.5 = bf16[256,1088]{0,1:T(8,128)(2,1)S(1)} collective-permute-done((bf16[256,1088]{0,1:T(8,128)(2,1)S(1)}, bf16[256,1088]{0,1:T(8,128)(2,1)S(1)}, u32[]{:S(2)}, u32[]{:S(2)}) %collective-permute-start.5) | collective-permute-done | bytes 557088 | tf_op jit(solution)/shard_map/ppermute | solution.py:252
  36.3 1.8 collective-permute-start
  38.4 1.4 copy.19.refs_1_
  39.8 1.3 copy.21.refs_3_
  41.2 1.4 spread_rows.1
  43.4 4.2 %fusion.4 = (bf16[512,512]{1,0:T(8,128)(2,1)S(1)}, bf16[512,512]{1,0:T(8,128)(2,1)S(1)}, f32[512,512]{1,0:T(8,128)}, f32[512,512]{1,0:T(8,128)S(1)}, f32[512,512]{1,0:T(8,128)}, /*index=5*/f32[512,512]{1,0:T(8,128)}) fusion(bf16[4,512,512]{2,1,0:T(8,128)(2,1)} %bitcast.1, s32[]{:T(128)S(6)} %min.22, bf16[4,512,512]{2,1,0:T(8,128)(2,1)S(1)} %bitcast.51, ...), kind=kLoop, calls=%fused_computation.17 | loop fusion | flops 5242880 | bytes 11534360 | tf_op jit(solution)/shard_map/add | solution.py:323
  47.7 2.2 %collective-permute-start.24 = (bf16[544,512]{1,0:T(8,128)(2,1)S(1)}, bf16[544,512]{1,0:T(8,128)(2,1)S(1)}, u32[]{:S(2)}, u32[]{:S(2)}) collective-permute-start(bf16[544,512]{1,0:T(8,128)(2,1)S(1)} %pad_maximum_fusion.1), channel_id=1, source_target_pairs={{0,4},{1,5},{2,6},{3,7},{12,8},{13,9},{14,10},{15,11},{16,20},{17,... | collective-permute-start | bytes 1671176 | tf_op jit(solution)/shard_map/ppermute | solution.py:255
  49.9 1.5 collective-permute-start.10
  51.3 1.5 collective-permute-start.1
  52.8 0.9 pad_maximum_fusion.2
  53.7 5.3 %collective-permute-start.27 = (bf16[544,512]{1,0:T(8,128)(2,1)}, bf16[544,512]{1,0:T(8,128)(2,1)S(1)}, u32[]{:S(2)}, u32[]{:S(2)}) collective-permute-start(bf16[544,512]{1,0:T(8,128)(2,1)} %pad_maximum_fusion.2), channel_id=1, source_target_pairs={{0,4},{1,5},{2,6},{3,7},{12,8},{13,9},{14,10},{15,11},{16,20},{17,... | collective-permute-start | bytes 1671176 | tf_op jit(solution)/shard_map/ppermute | solution.py:255
  59.0 3.8 %collective-permute-done.24 = bf16[544,512]{1,0:T(8,128)(2,1)S(1)} collective-permute-done((bf16[544,512]{1,0:T(8,128)(2,1)S(1)}, bf16[544,512]{1,0:T(8,128)(2,1)S(1)}, u32[]{:S(2)}, u32[]{:S(2)}) %collective-permute-start.24) | collective-permute-done | bytes 557088 | tf_op jit(solution)/shard_map/ppermute | solution.py:255
  62.8 1.1 fusion.2
  63.9 1.5 collective-permute-start.25
  65.4 1.3 collective-permute-start.11
  66.7 1.3 collective-permute-start.2
  68.0 6.2 %collective-permute-done.27 = bf16[544,512]{1,0:T(8,128)(2,1)S(1)} collective-permute-done((bf16[544,512]{1,0:T(8,128)(2,1)}, bf16[544,512]{1,0:T(8,128)(2,1)S(1)}, u32[]{:S(2)}, u32[]{:S(2)}) %collective-permute-start.27) | collective-permute-done | bytes 557088 | tf_op jit(solution)/shard_map/ppermute | solution.py:255
  74.2 2.3 %fusion.3 = bf16[544,512]{1,0:T(8,128)(2,1)} fusion(f32[32,512]{1,0:T(8,128)} %get-tuple-element.55, f32[512,512]{1,0:T(8,128)} %get-tuple-element.45, bf16[544,512]{1,0:T(8,128)(2,1)S(1)} %collective-permute-done.27), kind=kLoop, calls=%fused_computation.7 | loop fusion | flops 1114112 | bytes 2228224 | tf_op jit(solution)/shard_map/convert_element_type | solution.py:334
  76.5 1.5 collective-permute-start.28
  78.0 2.1 %fusion.1 = bf16[544,512]{1,0:T(8,128)(2,1)} fusion(f32[32,512]{1,0:T(8,128)S(1)} %copy-done.33, f32[512,512]{1,0:T(8,128)S(1)} %copy-done.30, bf16[544,512]{1,0:T(8,128)(2,1)} %collective-permute-done.25), kind=kLoop, calls=%fused_computation.3 | loop fusion | flops 1114112 | bytes 2228224 | tf_op jit(solution)/shard_map/convert_element_type | solution.py:334
  80.1 29.1 %collective-permute-start.26 = (bf16[544,512]{1,0:T(8,128)(2,1)}, bf16[544,512]{1,0:T(8,128)(2,1)}, u32[]{:S(2)}, u32[]{:S(2)}) collective-permute-start(bf16[544,512]{1,0:T(8,128)(2,1)} %fusion.1), channel_id=1, source_target_pairs={{4,0},{5,1},{6,2},{7,3},{0,4},{1,5},{2,6},{3,7},{12,8},{13,9},{14,... | collective-permute-start | bytes 1671176 | tf_op jit(solution)/shard_map/ppermute | solution.py:255
  109.2 1.1 broadcast_select_fusion.mine
  110.3 1.5 collective-permute-start.12
  112.4 1.2 copy-done.8
  113.6 0.9 copy-done.13
  114.6 2.0 %own_shard.1 = (bf16[256,512]{1,0:T(8,128)(2,1)S(1)}, bf16[256,512]{1,0:T(8,128)(2,1)S(1)}, bf16[512,512]{1,0:T(8,128)(2,1)}) custom-call(bf16[512,1024]{1,0:T(8,128)(2,1)S(1)} %copy-done.8, bf16[512,256]{1,0:T(8,128)(2,1)S(1)} %copy-done.13, bf16[4,256,256]{2,1,0:T(8,128)(2,1)S(1)} %get-tuple-element.19.spread, ...), custom_call_target="tpu_custom_call" | custom-call | tf_op jit(solution)/shard_map/own_shard/pallas_call | solution.py:169
  116.6 1.5 collective-permute-start.21
  118.1 1.9 broadcast_select_fusion.1.mine
  120.0 5.4 %collective-permute-done.12.theirs = bf16[256,1024]{1,0:T(8,128)(2,1)} collective-permute-done((bf16[256,1024]{1,0:T(8,128)(2,1)S(1)}, bf16[256,1024]{1,0:T(8,128)(2,1)}, u32[]{:S(2)}, u32[]{:S(2)}) %collective-permute-start.12) | collective-permute-done | bytes 524320 | tf_op jit(solution)/shard_map/ppermute | solution.py:260
  125.3 1.5 collective-permute-start.3
  126.8 1.2 copy-done.1
  128.0 3.3 %shard.4 = (bf16[256,512]{1,0:T(8,128)(2,1)S(1)}, bf16[256,512]{1,0:T(8,128)(2,1)}, bf16[512,512]{1,0:T(8,128)(2,1)}) custom-call(bf16[256,1024]{1,0:T(8,128)(2,1)S(1)} %broadcast_select_fusion.mine, bf16[256,1024]{1,0:T(8,128)(2,1)} %collective-permute-done.12.theirs, bf16[2048,256]{1,0:T(8,128)(2,1)S(1)} %copy-done.1, ...), custom_call_target="tpu_custom_call" | custom-call | tf_op jit(solution)/shard_map/shard/pallas_call | solution.py:169
  132.1 4.5 %collective-permute-done.16.theirs = bf16[256,1024]{1,0:T(8,128)(2,1)} collective-permute-done((bf16[256,1024]{1,0:T(8,128)(2,1)}, bf16[256,1024]{1,0:T(8,128)(2,1)}, u32[]{:S(2)}, u32[]{:S(2)}) %collective-permute-start.16) | collective-permute-done | bytes 524320 | tf_op jit(solution)/shard_map/ppermute | solution.py:260
  136.6 1.5 collective-permute-start.14
  138.1 3.5 %shard.5 = (bf16[256,512]{1,0:T(8,128)(2,1)S(1)}, bf16[256,512]{1,0:T(8,128)(2,1)}, bf16[512,512]{1,0:T(8,128)(2,1)}) custom-call(bf16[256,1024]{1,0:T(8,128)(2,1)} %collective-permute-done.mine, bf16[256,1024]{1,0:T(8,128)(2,1)} %collective-permute-done.16.theirs, bf16[2048,256]{1,0:T(8,128)(2,1)S(1)} %copy-done.1, ...), custom_call_target="tpu_custom_call" | custom-call | tf_op jit(solution)/shard_map/shard/pallas_call | solution.py:169
  142.2 1.5 fusion
  143.8 1.0 copy-done.27
  145.4 1.7 slice.28
  147.1 1.0 copy-done.4
  148.1 2.8 %shard.3 = (bf16[256,512]{1,0:T(8,128)(2,1)S(1)}, bf16[256,512]{1,0:T(8,128)(2,1)S(1)}, bf16[512,512]{1,0:T(8,128)(2,1)S(1)}) custom-call(bf16[256,1024]{1,0:T(8,128)(2,1)} %broadcast_select_fusion.1.mine, bf16[256,1024]{1,0:T(8,128)(2,1)} %collective-permute-done.3.theirs, bf16[2048,256]{1,0:T(8,128)(2,1)S(1)} %copy-done.2, ...), custom_call_target="tpu_custom_call" | custom-call | tf_op jit(solution)/shard_map/shard/pallas_call | solution.py:169
  152.3 1.5 collective-permute-start.8
  153.8 3.5 %collective-permute-start.31 = (bf16[32,512]{1,0:T(8,128)(2,1)}, bf16[32,512]{1,0:T(8,128)(2,1)S(1)}, u32[]{:S(2)}, u32[]{:S(2)}) collective-permute-start(bf16[32,512]{1,0:T(8,128)(2,1)} %get-tuple-element.42), channel_id=1, source_target_pairs={{0,8},{1,9},{2,10},{3,11},{4,12},{5,13},{6,14},{7,15},{8,0},{9,1},... | collective-permute-start | bytes 98312 | tf_op jit(solution)/shard_map/ppermute | solution.py:255
  158.0 1.7 collective-permute-done.31
  159.7 3.1 %collective-permute-start.32 = (bf16[32,512]{1,0:T(8,128)(2,1)}, bf16[32,512]{1,0:T(8,128)(2,1)S(1)}, u32[]{:S(2)}, u32[]{:S(2)}) collective-permute-start(bf16[32,512]{1,0:T(8,128)(2,1)} %get-tuple-element.42), channel_id=1, source_target_pairs={{0,12},{1,13},{2,14},{3,15},{4,0},{5,1},{6,2},{7,3},{8,4},{9,5},{1... | collective-permute-start | bytes 98312 | tf_op jit(solution)/shard_map/ppermute | solution.py:255
  163.4 1.3 collective-permute-done.32
  164.7 4.4 %collective-permute-done.8.across = bf16[512,512]{1,0:T(8,128)(2,1)S(1)} collective-permute-done((bf16[512,512]{1,0:T(8,128)(2,1)S(1)}, bf16[512,512]{1,0:T(8,128)(2,1)S(1)}, u32[]{:S(2)}, u32[]{:S(2)}) %collective-permute-start.8) | collective-permute-done | bytes 524320 | tf_op jit(solution)/shard_map/ppermute | solution.py:252
  169.2 1.6 collective-permute-start.33
  170.8 1.7 slice.26
  172.5 1.0 slice.27
  176.6 1.1 collective-permute-done.19.both
  177.9 2.2 %place.4.refs_0_ = bf16[256,8192]{1,0:T(8,128)(2,1)} custom-call(bf16[256,512]{1,0:T(8,128)(2,1)S(1)} %copy-done.21, bf16[256,512]{1,0:T(8,128)(2,1)} %collective-permute-done.20.core, bf16[512,512]{1,0:T(8,128)(2,1)} %collective-permute-done.21.across, bf16[256,512]{1,0:T(8,128)(2,1)S(1)} %collective-permute-done.22.both), custom_call_target="tpu_custom_call" | custom-call | tf_op jit(solution)/shard_map/place/pallas_call | solution.py:196
  180.1 2.1 %place.5.refs_0_ = bf16[256,8192]{1,0:T(8,128)(2,1)} custom-call(bf16[256,512]{1,0:T(8,128)(2,1)S(1)} %copy-done.17, bf16[256,512]{1,0:T(8,128)(2,1)S(1)} %collective-permute-done.17.core, bf16[512,512]{1,0:T(8,128)(2,1)} %collective-permute-done.18.across, bf16[256,512]{1,0:T(8,128)(2,1)S(1)} %collective-permute-done.19.both, ...), custom_call_target="tpu_custom_call", output_to_operand_aliasing={{}: (4, {})} | custom-call | tf_op jit(solution)/shard_map/place/pallas_call | solution.py:196
  182.2 2.1 %place.6.refs_0_ = bf16[256,8192]{1,0:T(8,128)(2,1)} custom-call(bf16[256,512]{1,0:T(8,128)(2,1)S(1)} %copy-done.15, bf16[256,512]{1,0:T(8,128)(2,1)S(1)} %collective-permute-done.13.core, bf16[512,512]{1,0:T(8,128)(2,1)} %collective-permute-done.14.across, bf16[256,512]{1,0:T(8,128)(2,1)S(1)} %collective-permute-done.15.both, ...), custom_call_target="tpu_custom_call", output_to_operand_aliasing={{}: (4, {})} | custom-call | tf_op jit(solution)/shard_map/place/pallas_call | solution.py:196
  184.3 1.0 place.7
  185.9 1.0 fusion.6
  186.9 1.0 copy.34
  187.9 1.0 broadcast_select_fusion.3
  189.0 1.1 maximum_convert_fusion
  (123 shorter events, 12.9 us)
Async XLA Ops:
  7.2 119.6 %all-gather.2.cloned.1.call-start = ((), (), s32[]{:S(2)}) async-start(), calls=%async_computation | async-start | bytes 1310720 | tf_op jit(solution)/shard_map/all_gather | solution.py:262
  7.2 2.2 %copy-start = (bf16[256,8192]{1,0:T(8,128)(2,1)S(1)}, bf16[256,8192]{1,0:T(8,128)(2,1)}, u32[]{:S(2)}) copy-start(bf16[256,8192]{1,0:T(8,128)(2,1)} %tok_keep.1) | copy-start | bytes 12582916
  9.4 1.0 copy-start.9
  10.4 1.0 copy-start.11
  12.1 7.0 %copy-start.34 = (bf16[256,64]{0,1:T(8,128)(2,1)S(1)}, bf16[256,64]{0,1:T(8,128)(2,1)}, u32[]{:S(2)}) copy-start(bf16[256,64]{0,1:T(8,128)(2,1)} %param.9) | copy-start | bytes 98308
  12.1 7.1 %copy-start.10 = (bf16[256,1024]{1,0:T(8,128)(2,1)S(1)}, bf16[256,1024]{1,0:T(8,128)(2,1)}, u32[]{:S(2)}) copy-start(bf16[256,1024]{1,0:T(8,128)(2,1)} %g.1) | copy-start | bytes 1572868
  17.4 1.3 copy-start.5
  18.7 24.7 %collective-permute-start.23 = (bf16[8,256,512]{2,1,0:T(8,128)(2,1)}, bf16[8,256,512]{2,1,0:T(8,128)(2,1)}, u32[]{:S(2)}, u32[]{:S(2)}) collective-permute-start(bf16[8,256,512]{2,1,0:T(8,128)(2,1)} %get-tuple-element.33), channel_id=1, source_target_pairs={{0,1},{1,0},{2,3},{3,2},{4,5},{5,4},{6,7},{7,6},{8,9},{9,8},{10,11... | collective-permute-start | bytes 6291464 | tf_op jit(solution)/shard_map/ppermute | solution.py:252
  19.3 16.2 %copy-start.7 = (bf16[512,1024]{1,0:T(8,128)(2,1)S(1)}, bf16[512,1024]{1,0:T(8,128)(2,1)}, u32[]{:S(2)}) copy-start(bf16[512,1024]{1,0:T(8,128)(2,1)} %w.1) | copy-start | bytes 3145732
  19.6 15.9 %collective-permute-start.5 = (bf16[256,1088]{0,1:T(8,128)(2,1)S(1)}, bf16[256,1088]{0,1:T(8,128)(2,1)S(1)}, u32[]{:S(2)}, u32[]{:S(2)}) collective-permute-start(bf16[256,1088]{0,1:T(8,128)(2,1)S(1)} %copy.17), channel_id=1, source_target_pairs={{0,2},{1,3},{2,0},{3,1},{4,6},{5,7},{6,4},{7,5},{8,10},{9,11},{10,... | collective-permute-start | bytes 1671176 | tf_op jit(solution)/shard_map/ppermute | solution.py:252
  22.1 16.2 %collective-permute-start.4 = (bf16[256,1088]{0,1:T(8,128)(2,1)S(1)}, bf16[256,1088]{0,1:T(8,128)(2,1)}, u32[]{:S(2)}, u32[]{:S(2)}) collective-permute-start(bf16[256,1088]{0,1:T(8,128)(2,1)S(1)} %copy.17), channel_id=1, source_target_pairs={{0,1},{1,0},{2,3},{3,2},{4,5},{5,4},{6,7},{7,6},{8,9},{9,8},{10,11... | collective-permute-start | bytes 1671176 | tf_op jit(solution)/shard_map/ppermute | solution.py:252
  35.4 4.4 %collective-permute-start.6 = (bf16[256,1088]{0,1:T(8,128)(2,1)S(1)}, bf16[256,1088]{0,1:T(8,128)(2,1)}, u32[]{:S(2)}, u32[]{:S(2)}) collective-permute-start(bf16[256,1088]{0,1:T(8,128)(2,1)S(1)} %collective-permute-done.5), channel_id=1, source_target_pairs={{0,1},{1,0},{2,3},{3,2},{4,5},{5,4},{6,7},{7,6},{8,9},{9,8},{10,11... | collective-permute-start | bytes 1671176 | tf_op jit(solution)/shard_map/ppermute | solution.py:252
  36.3 15.1 %collective-permute-start = (bf16[256,1024]{1,0:T(8,128)(2,1)}, bf16[256,1024]{1,0:T(8,128)(2,1)}, u32[]{:S(2)}, u32[]{:S(2)}) collective-permute-start(bf16[256,1024]{1,0:T(8,128)(2,1)} %constant_dynamic-slice_fusion), channel_id=1, source_target_pairs={{0,4},{1,5},{2,6},{3,7},{4,0},{5,1},{6,2},{7,3},{8,12},{9,13},{10,... | collective-permute-start | bytes 1572872 | tf_op jit(solution)/shard_map/ppermute | solution.py:255
  38.4 2.8 %copy-start.12 = (bf16[256,1024]{1,0:T(8,128)(2,1)S(1)}, bf16[256,1024]{1,0:T(8,128)(2,1)}, u32[]{:S(2)}) copy-start(bf16[256,1024]{1,0:T(8,128)(2,1)} %b.3) | copy-start | bytes 1572868
  38.4 2.8 %copy-start.23 = (s32[32]{0:T(128)S(1)}, s32[32]{0:T(128)}, u32[]{:S(2)}) copy-start(s32[32]{0:T(128)} %members.3) | copy-start | bytes 388
  41.2 2.2 %copy-start.6 = (bf16[8,256,512]{2,1,0:T(8,128)(2,1)S(1)}, bf16[8,256,512]{2,1,0:T(8,128)(2,1)}, u32[]{:S(2)}) copy-start(bf16[8,256,512]{2,1,0:T(8,128)(2,1)} %copy-done.5) | copy-start | bytes 6291460
  42.6 95.4 %copy-start.3 = (bf16[4,256,256]{2,1,0:T(8,128)(2,1)}, bf16[4,256,256]{2,1,0:T(8,128)(2,1)S(1)}, u32[]{:S(2)}) copy-start(bf16[4,256,256]{2,1,0:T(8,128)(2,1)S(1)} %get-tuple-element.19.spread) | copy-start | bytes 1572868
  47.7 15.1 %collective-permute-start.24 = (bf16[544,512]{1,0:T(8,128)(2,1)S(1)}, bf16[544,512]{1,0:T(8,128)(2,1)S(1)}, u32[]{:S(2)}, u32[]{:S(2)}) collective-permute-start(bf16[544,512]{1,0:T(8,128)(2,1)S(1)} %pad_maximum_fusion.1), channel_id=1, source_target_pairs={{0,4},{1,5},{2,6},{3,7},{12,8},{13,9},{14,10},{15,11},{16,20},{17,... | collective-permute-start | bytes 1671176 | tf_op jit(solution)/shard_map/ppermute | solution.py:255
  49.9 15.5 %collective-permute-start.10 = (bf16[256,1024]{1,0:T(8,128)(2,1)}, bf16[256,1024]{1,0:T(8,128)(2,1)}, u32[]{:S(2)}, u32[]{:S(2)}) collective-permute-start(bf16[256,1024]{1,0:T(8,128)(2,1)} %constant_dynamic-slice_fusion), channel_id=1, source_target_pairs={{4,8},{5,9},{6,10},{7,11},{8,4},{9,5},{10,6},{11,7},{20,24},{21,25... | collective-permute-start | bytes 1572872 | tf_op jit(solution)/shard_map/ppermute | solution.py:255
  51.3 15.3 %collective-permute-start.1 = (bf16[256,1024]{1,0:T(8,128)(2,1)}, bf16[256,1024]{1,0:T(8,128)(2,1)}, u32[]{:S(2)}, u32[]{:S(2)}) collective-permute-start(bf16[256,1024]{1,0:T(8,128)(2,1)} %collective-permute-done.mine), channel_id=1, source_target_pairs={{4,8},{5,9},{6,10},{7,11},{8,4},{9,5},{10,6},{11,7},{20,24},{21,25... | collective-permute-start | bytes 1572872 | tf_op jit(solution)/shard_map/ppermute | solution.py:255
  53.7 20.5 %collective-permute-start.27 = (bf16[544,512]{1,0:T(8,128)(2,1)}, bf16[544,512]{1,0:T(8,128)(2,1)S(1)}, u32[]{:S(2)}, u32[]{:S(2)}) collective-permute-start(bf16[544,512]{1,0:T(8,128)(2,1)} %pad_maximum_fusion.2), channel_id=1, source_target_pairs={{0,4},{1,5},{2,6},{3,7},{12,8},{13,9},{14,10},{15,11},{16,20},{17,... | collective-permute-start | bytes 1671176 | tf_op jit(solution)/shard_map/ppermute | solution.py:255
  63.9 14.1 %collective-permute-start.25 = (bf16[544,512]{1,0:T(8,128)(2,1)}, bf16[544,512]{1,0:T(8,128)(2,1)}, u32[]{:S(2)}, u32[]{:S(2)}) collective-permute-start(bf16[544,512]{1,0:T(8,128)(2,1)} %fusion.2), channel_id=1, source_target_pairs={{8,4},{9,5},{10,6},{11,7},{4,8},{5,9},{6,10},{7,11},{24,20},{25,21... | collective-permute-start | bytes 1671176 | tf_op jit(solution)/shard_map/ppermute | solution.py:255
  65.4 43.8 %collective-permute-start.11 = (bf16[256,1024]{1,0:T(8,128)(2,1)}, bf16[256,1024]{1,0:T(8,128)(2,1)}, u32[]{:S(2)}, u32[]{:S(2)}) collective-permute-start(bf16[256,1024]{1,0:T(8,128)(2,1)} %collective-permute-done.10), channel_id=1, source_target_pairs={{4,0},{5,1},{6,2},{7,3},{8,12},{9,13},{10,14},{11,15},{20,16},{21,... | collective-permute-start | bytes 1572872 | tf_op jit(solution)/shard_map/ppermute | solution.py:255
  66.7 49.9 %collective-permute-start.2 = (bf16[256,1024]{1,0:T(8,128)(2,1)}, bf16[256,1024]{1,0:T(8,128)(2,1)}, u32[]{:S(2)}, u32[]{:S(2)}) collective-permute-start(bf16[256,1024]{1,0:T(8,128)(2,1)} %collective-permute-done.1), channel_id=1, source_target_pairs={{4,0},{5,1},{6,2},{7,3},{8,12},{9,13},{10,14},{11,15},{20,16},{21,... | collective-permute-start | bytes 1572872 | tf_op jit(solution)/shard_map/ppermute | solution.py:255
  74.2 3.8 %copy-start.30 = (f32[512,512]{1,0:T(8,128)S(1)}, f32[512,512]{1,0:T(8,128)}, u32[]{:S(2)}) copy-start(f32[512,512]{1,0:T(8,128)} %get-tuple-element.47) | copy-start | bytes 3145732
  74.2 3.8 %copy-start.33 = (f32[32,512]{1,0:T(8,128)S(1)}, f32[32,512]{1,0:T(8,128)}, u32[]{:S(2)}) copy-start(f32[32,512]{1,0:T(8,128)} %get-tuple-element.57) | copy-start | bytes 196612
  76.5 65.1 %collective-permute-start.28 = (bf16[544,512]{1,0:T(8,128)(2,1)}, bf16[544,512]{1,0:T(8,128)(2,1)}, u32[]{:S(2)}, u32[]{:S(2)}) collective-permute-start(bf16[544,512]{1,0:T(8,128)(2,1)} %fusion.3), channel_id=1, source_target_pairs={{8,4},{9,5},{10,6},{11,7},{4,8},{5,9},{6,10},{7,11},{24,20},{25,21... | collective-permute-start | bytes 1671176 | tf_op jit(solution)/shard_map/ppermute | solution.py:255
  80.1 62.1 %collective-permute-start.26 = (bf16[544,512]{1,0:T(8,128)(2,1)}, bf16[544,512]{1,0:T(8,128)(2,1)}, u32[]{:S(2)}, u32[]{:S(2)}) collective-permute-start(bf16[544,512]{1,0:T(8,128)(2,1)} %fusion.1), channel_id=1, source_target_pairs={{4,0},{5,1},{6,2},{7,3},{0,4},{1,5},{2,6},{3,7},{12,8},{13,9},{14,... | collective-permute-start | bytes 1671176 | tf_op jit(solution)/shard_map/ppermute | solution.py:255
  110.3 15.0 %collective-permute-start.12 = (bf16[256,1024]{1,0:T(8,128)(2,1)S(1)}, bf16[256,1024]{1,0:T(8,128)(2,1)}, u32[]{:S(2)}, u32[]{:S(2)}) collective-permute-start(bf16[256,1024]{1,0:T(8,128)(2,1)S(1)} %broadcast_select_fusion.mine), channel_id=1, source_target_pairs={{0,16},{16,0},{1,17},{17,1},{2,18},{18,2},{3,19},{19,3},{4,20},{20... | collective-permute-start | bytes 1572872 | tf_op jit(solution)/shard_map/ppermute | solution.py:260
  111.8 24.7 %collective-permute-start.16 = (bf16[256,1024]{1,0:T(8,128)(2,1)}, bf16[256,1024]{1,0:T(8,128)(2,1)}, u32[]{:S(2)}, u32[]{:S(2)}) collective-permute-start(bf16[256,1024]{1,0:T(8,128)(2,1)} %collective-permute-done.mine), channel_id=1, source_target_pairs={{0,16},{16,0},{1,17},{17,1},{2,18},{18,2},{3,19},{19,3},{4,20},{20... | collective-permute-start | bytes 1572872 | tf_op jit(solution)/shard_map/ppermute | solution.py:260
  112.4 1.2 copy-start.8
  116.6 8.8 %copy-start.20 = (bf16[256,512]{1,0:T(8,128)(2,1)}, bf16[256,512]{1,0:T(8,128)(2,1)S(1)}, u32[]{:S(2)}) copy-start(bf16[256,512]{1,0:T(8,128)(2,1)S(1)} %get-tuple-element.29.own) | copy-start | bytes 786436
  116.6 8.8 %copy-start.24 = (bf16[256,512]{1,0:T(8,128)(2,1)}, bf16[256,512]{1,0:T(8,128)(2,1)S(1)}, u32[]{:S(2)}) copy-start(bf16[256,512]{1,0:T(8,128)(2,1)S(1)} %get-tuple-element.30) | copy-start | bytes 786436
  116.6 28.8 %collective-permute-start.21 = (bf16[512,512]{1,0:T(8,128)(2,1)}, bf16[512,512]{1,0:T(8,128)(2,1)}, u32[]{:S(2)}, u32[]{:S(2)}) collective-permute-start(bf16[512,512]{1,0:T(8,128)(2,1)} %get-tuple-element.31), channel_id=1, source_target_pairs={{0,2},{1,3},{2,0},{3,1},{4,6},{5,7},{6,4},{7,5},{8,10},{9,11},{10,... | collective-permute-start | bytes 1572872 | tf_op jit(solution)/shard_map/ppermute | solution.py:252
  125.3 21.7 %collective-permute-start.3 = (bf16[256,1024]{1,0:T(8,128)(2,1)}, bf16[256,1024]{1,0:T(8,128)(2,1)}, u32[]{:S(2)}, u32[]{:S(2)}) collective-permute-start(bf16[256,1024]{1,0:T(8,128)(2,1)} %broadcast_select_fusion.1.mine), channel_id=1, source_target_pairs={{0,16},{16,0},{1,17},{17,1},{2,18},{18,2},{3,19},{19,3},{4,20},{20... | collective-permute-start | bytes 1572872 | tf_op jit(solution)/shard_map/ppermute | solution.py:260
  126.8 1.2 copy-start.1
  136.6 5.6 %copy-start.29 = (f32[512,512]{1,0:T(8,128)S(1)}, f32[512,512]{1,0:T(8,128)}, u32[]{:S(2)}) copy-start(f32[512,512]{1,0:T(8,128)} %get-tuple-element.48) | copy-start | bytes 3145732
  136.6 26.3 %collective-permute-start.14 = (bf16[512,512]{1,0:T(8,128)(2,1)}, bf16[512,512]{1,0:T(8,128)(2,1)}, u32[]{:S(2)}, u32[]{:S(2)}) collective-permute-start(bf16[512,512]{1,0:T(8,128)(2,1)} %get-tuple-element.25), channel_id=1, source_target_pairs={{0,2},{1,3},{2,0},{3,1},{4,6},{5,7},{6,4},{7,5},{8,10},{9,11},{10,... | collective-permute-start | bytes 1572872 | tf_op jit(solution)/shard_map/ppermute | solution.py:252
  141.6 2.1 %copy-start.16 = (bf16[256,512]{1,0:T(8,128)(2,1)}, bf16[256,512]{1,0:T(8,128)(2,1)S(1)}, u32[]{:S(2)}) copy-start(bf16[256,512]{1,0:T(8,128)(2,1)S(1)} %get-tuple-element.26.own) | copy-start | bytes 786436
  141.6 21.3 %collective-permute-start.18 = (bf16[512,512]{1,0:T(8,128)(2,1)}, bf16[512,512]{1,0:T(8,128)(2,1)}, u32[]{:S(2)}, u32[]{:S(2)}) collective-permute-start(bf16[512,512]{1,0:T(8,128)(2,1)} %get-tuple-element.28), channel_id=1, source_target_pairs={{0,2},{1,3},{2,0},{3,1},{4,6},{5,7},{6,4},{7,5},{8,10},{9,11},{10,... | collective-permute-start | bytes 1572872 | tf_op jit(solution)/shard_map/ppermute | solution.py:252
  142.2 4.9 %copy-start.2 = (bf16[2048,256]{1,0:T(8,128)(2,1)S(1)}, bf16[2048,256]{1,0:T(8,128)(2,1)}, u32[]{:S(2)}) copy-start(bf16[2048,256]{1,0:T(8,128)(2,1)} %all-gather.2.cloned.1.call-done.a) | copy-start | bytes 3145732
  145.4 8.4 %collective-permute-start.30 = (bf16[32,512]{1,0:T(8,128)(2,1)}, bf16[32,512]{1,0:T(8,128)(2,1)}, u32[]{:S(2)}, u32[]{:S(2)}) collective-permute-start(bf16[32,512]{1,0:T(8,128)(2,1)} %get-tuple-element.42), channel_id=1, source_target_pairs={{0,4},{1,5},{2,6},{3,7},{4,8},{5,9},{6,10},{7,11},{8,12},{9,13},{1... | collective-permute-start | bytes 98312 | tf_op jit(solution)/shard_map/ppermute | solution.py:255
  145.4 29.7 %collective-permute-start.20 = (bf16[256,512]{1,0:T(8,128)(2,1)}, bf16[256,512]{1,0:T(8,128)(2,1)}, u32[]{:S(2)}, u32[]{:S(2)}) collective-permute-start(bf16[256,512]{1,0:T(8,128)(2,1)} %copy-done.24), channel_id=1, source_target_pairs={{0,1},{1,0},{2,3},{3,2},{4,5},{5,4},{6,7},{7,6},{8,9},{9,8},{10,11... | collective-permute-start | bytes 786440 | tf_op jit(solution)/shard_map/ppermute | solution.py:252
  147.1 1.0 copy-start.4
  152.3 21.9 %copy-start.28 = (f32[544,512]{1,0:T(8,128)S(1)}, f32[544,512]{1,0:T(8,128)}, u32[]{:S(2)}) copy-start(f32[544,512]{1,0:T(8,128)} %copy-done.27) | copy-start | bytes 3342340
  152.3 16.9 %collective-permute-start.8 = (bf16[512,512]{1,0:T(8,128)(2,1)S(1)}, bf16[512,512]{1,0:T(8,128)(2,1)S(1)}, u32[]{:S(2)}, u32[]{:S(2)}) collective-permute-start(bf16[512,512]{1,0:T(8,128)(2,1)S(1)} %get-tuple-element.22), channel_id=1, source_target_pairs={{0,2},{1,3},{2,0},{3,1},{4,6},{5,7},{6,4},{7,5},{8,10},{9,11},{10,... | collective-permute-start | bytes 1572872 | tf_op jit(solution)/shard_map/ppermute | solution.py:252
  153.8 6.0 %collective-permute-start.31 = (bf16[32,512]{1,0:T(8,128)(2,1)}, bf16[32,512]{1,0:T(8,128)(2,1)S(1)}, u32[]{:S(2)}, u32[]{:S(2)}) collective-permute-start(bf16[32,512]{1,0:T(8,128)(2,1)} %get-tuple-element.42), channel_id=1, source_target_pairs={{0,8},{1,9},{2,10},{3,11},{4,12},{5,13},{6,14},{7,15},{8,0},{9,1},... | collective-permute-start | bytes 98312 | tf_op jit(solution)/shard_map/ppermute | solution.py:255
  159.7 5.0 %collective-permute-start.32 = (bf16[32,512]{1,0:T(8,128)(2,1)}, bf16[32,512]{1,0:T(8,128)(2,1)S(1)}, u32[]{:S(2)}, u32[]{:S(2)}) collective-permute-start(bf16[32,512]{1,0:T(8,128)(2,1)} %get-tuple-element.42), channel_id=1, source_target_pairs={{0,12},{1,13},{2,14},{3,15},{4,0},{5,1},{6,2},{7,3},{8,4},{9,5},{1... | collective-permute-start | bytes 98312 | tf_op jit(solution)/shard_map/ppermute | solution.py:255
  162.8 12.3 %collective-permute-start.13 = (bf16[256,512]{1,0:T(8,128)(2,1)}, bf16[256,512]{1,0:T(8,128)(2,1)S(1)}, u32[]{:S(2)}, u32[]{:S(2)}) collective-permute-start(bf16[256,512]{1,0:T(8,128)(2,1)} %get-tuple-element.24), channel_id=1, source_target_pairs={{0,1},{1,0},{2,3},{3,2},{4,5},{5,4},{6,7},{7,6},{8,9},{9,8},{10,11... | collective-permute-start | bytes 786440 | tf_op jit(solution)/shard_map/ppermute | solution.py:252
  162.9 12.7 %collective-permute-start.17 = (bf16[256,512]{1,0:T(8,128)(2,1)}, bf16[256,512]{1,0:T(8,128)(2,1)S(1)}, u32[]{:S(2)}, u32[]{:S(2)}) collective-permute-start(bf16[256,512]{1,0:T(8,128)(2,1)} %get-tuple-element.27), channel_id=1, source_target_pairs={{0,1},{1,0},{2,3},{3,2},{4,5},{5,4},{6,7},{7,6},{8,9},{9,8},{10,11... | collective-permute-start | bytes 786440 | tf_op jit(solution)/shard_map/ppermute | solution.py:252
  164.7 11.0 %collective-permute-start.22 = (bf16[256,512]{1,0:T(8,128)(2,1)}, bf16[256,512]{1,0:T(8,128)(2,1)S(1)}, u32[]{:S(2)}, u32[]{:S(2)}) collective-permute-start(bf16[256,512]{1,0:T(8,128)(2,1)} %slice.28), channel_id=1, source_target_pairs={{0,1},{1,0},{2,3},{3,2},{4,5},{5,4},{6,7},{7,6},{8,9},{9,8},{10,11... | collective-permute-start | bytes 786440 | tf_op jit(solution)/shard_map/ppermute | solution.py:252
  169.2 7.0 %collective-permute-start.33 = (bf16[128,512]{1,0:T(8,128)(2,1)S(1)}, bf16[128,512]{1,0:T(8,128)(2,1)S(1)}, u32[]{:S(2)}, u32[]{:S(2)}) collective-permute-start(bf16[128,512]{1,0:T(8,128)(2,1)S(1)} %bitcast.55), channel_id=1, source_target_pairs={{0,2},{1,3},{2,0},{3,1},{4,6},{5,7},{6,4},{7,5},{8,10},{9,11},{10,... | collective-permute-start | bytes 393224 | tf_op jit(solution)/shard_map/ppermute | solution.py:252
  174.3 3.5 %copy-start.31 = (f32[512,512]{1,0:T(8,128)}, f32[512,512]{1,0:T(8,128)S(1)}, u32[]{:S(2)}) copy-start(f32[512,512]{1,0:T(8,128)S(1)} %slice.29) | copy-start | bytes 3145732
  174.3 3.6 %copy-start.21 = (bf16[256,512]{1,0:T(8,128)(2,1)S(1)}, bf16[256,512]{1,0:T(8,128)(2,1)}, u32[]{:S(2)}) copy-start(bf16[256,512]{1,0:T(8,128)(2,1)} %copy-done.20) | copy-start | bytes 786436
  175.1 9.1 %collective-permute-start.7 = (bf16[256,512]{1,0:T(8,128)(2,1)S(1)}, bf16[256,512]{1,0:T(8,128)(2,1)S(1)}, u32[]{:S(2)}, u32[]{:S(2)}) collective-permute-start(bf16[256,512]{1,0:T(8,128)(2,1)S(1)} %copy-done.26), channel_id=1, source_target_pairs={{0,1},{1,0},{2,3},{3,2},{4,5},{5,4},{6,7},{7,6},{8,9},{9,8},{10,11... | collective-permute-start | bytes 786440 | tf_op jit(solution)/shard_map/ppermute | solution.py:252
  175.1 7.0 %collective-permute-start.15 = (bf16[256,512]{1,0:T(8,128)(2,1)}, bf16[256,512]{1,0:T(8,128)(2,1)S(1)}, u32[]{:S(2)}, u32[]{:S(2)}) collective-permute-start(bf16[256,512]{1,0:T(8,128)(2,1)} %slice.26), channel_id=1, source_target_pairs={{0,1},{1,0},{2,3},{3,2},{4,5},{5,4},{6,7},{7,6},{8,9},{9,8},{10,11... | collective-permute-start | bytes 786440 | tf_op jit(solution)/shard_map/ppermute | solution.py:252
  175.7 2.1 %collective-permute-start.19 = (bf16[256,512]{1,0:T(8,128)(2,1)S(1)}, bf16[256,512]{1,0:T(8,128)(2,1)S(1)}, u32[]{:S(2)}, u32[]{:S(2)}) collective-permute-start(bf16[256,512]{1,0:T(8,128)(2,1)S(1)} %slice.27), channel_id=1, source_target_pairs={{0,1},{1,0},{2,3},{3,2},{4,5},{5,4},{6,7},{7,6},{8,9},{9,8},{10,11... | collective-permute-start | bytes 786440 | tf_op jit(solution)/shard_map/ppermute | solution.py:252
  175.7 8.6 %collective-permute-start.9 = (bf16[256,512]{1,0:T(8,128)(2,1)}, bf16[256,512]{1,0:T(8,128)(2,1)S(1)}, u32[]{:S(2)}, u32[]{:S(2)}) collective-permute-start(bf16[256,512]{1,0:T(8,128)(2,1)} %slice.25), channel_id=1, source_target_pairs={{0,1},{1,0},{2,3},{3,2},{4,5},{5,4},{6,7},{7,6},{8,9},{9,8},{10,11... | collective-permute-start | bytes 786440 | tf_op jit(solution)/shard_map/ppermute | solution.py:252
  176.2 9.2 %collective-permute-start.29 = (bf16[256,512]{1,0:T(8,128)(2,1)}, bf16[256,512]{1,0:T(8,128)(2,1)}, u32[]{:S(2)}, u32[]{:S(2)}) collective-permute-start(bf16[256,512]{1,0:T(8,128)(2,1)} %fusion.7), channel_id=1, source_target_pairs={{0,2},{1,3},{2,0},{3,1},{4,6},{5,7},{6,4},{7,5},{8,10},{9,11},{10,... | collective-permute-start | bytes 786440 | tf_op jit(solution)/shard_map/ppermute | solution.py:252
  177.7 10.2 %collective-permute-start.34 = (bf16[256,512]{1,0:T(8,128)(2,1)S(1)}, bf16[256,512]{1,0:T(8,128)(2,1)}, u32[]{:S(2)}, u32[]{:S(2)}) collective-permute-start(bf16[256,512]{1,0:T(8,128)(2,1)S(1)} %pad_maximum_fusion.3), channel_id=1, source_target_pairs={{0,1},{1,0},{2,3},{3,2},{4,5},{5,4},{6,7},{7,6},{8,9},{9,8},{10,11... | collective-permute-start | bytes 786440 | tf_op jit(solution)/shard_map/ppermute | solution.py:252
  177.9 2.2 %copy-start.17 = (bf16[256,512]{1,0:T(8,128)(2,1)S(1)}, bf16[256,512]{1,0:T(8,128)(2,1)}, u32[]{:S(2)}) copy-start(bf16[256,512]{1,0:T(8,128)(2,1)} %copy-done.16) | copy-start | bytes 786436
  180.0 2.1 %copy-start.15 = (bf16[256,512]{1,0:T(8,128)(2,1)S(1)}, bf16[256,512]{1,0:T(8,128)(2,1)}, u32[]{:S(2)}) copy-start(bf16[256,512]{1,0:T(8,128)(2,1)} %copy-done.14) | copy-start | bytes 786436
  182.2 2.1 %copy-start.19 = (bf16[256,512]{1,0:T(8,128)(2,1)S(1)}, bf16[256,512]{1,0:T(8,128)(2,1)}, u32[]{:S(2)}) copy-start(bf16[256,512]{1,0:T(8,128)(2,1)} %copy-done.18) | copy-start | bytes 786436
  184.3 1.6 copy-start.32
  (7 other events, 5.7 us)
Sparse Core Ops, SparseCore 0:
  65.5 40.5 all-gather.1

commit v2 on v0

v2 whole, which is shorter than its diff:
```python
import functools

import jax
import jax.numpy as jnp
import numpy as np
from jax import lax
from jax.experimental import pallas as pl
from jax.experimental.pallas import tpu as pltpu
from jax.sharding import PartitionSpec as P

ADAPTER_RANK = 64
MEMBER_COUNT = 4
BLOCK = 128
HIDDEN_COPIES = 2
INNER = 4

adapter_scale = 2.0
VMEM_BYTES = 24 << 20

COST_DOWN = 6
COST_SPREAD = 40
COST_MM = 3
COST_PLACE = 1
COST_LAST = 15
COST_OWN = 40
COST_TERM = 4

F32 = jnp.float32
BF16 = jnp.bfloat16
VMEM = pl.BlockSpec(memory_space=pltpu.VMEM)
SMEM = pl.BlockSpec(memory_space=pltpu.SMEM)
ANY = pl.BlockSpec(memory_space=pl.ANY)
HBM = pl.BlockSpec(memory_space=pltpu.HBM)


def nt(a, b):
    return lax.dot_general(a, b, (((1,), (1,)), ((), ())), preferred_element_type=F32)


def tn(a, b):
    return lax.dot_general(a, b, (((0,), (0,)), ((), ())), preferred_element_type=F32)


def params(nbytes, **kw):
    return pltpu.CompilerParams(vmem_limit_bytes=nbytes, **kw)


def cost(microseconds):
    return pl.CostEstimate(
        flops=int(microseconds * 1.1e9), bytes_accessed=int(microseconds * 3.3e6), transcendentals=0
    )


def where_am_i():
    me = lax.axis_index("dp")
    return me // INNER, me % INNER


def member_of_rows(members_ref, first_block, shape, dim):
    position = lax.broadcasted_iota(jnp.int32, shape, dim) // BLOCK
    result = jnp.zeros(shape, jnp.int32)
    for b in range(shape[dim] // BLOCK):
        result = jnp.where(position == b, members_ref[first_block + b], result)
    return result


def first_kernel(split, frozen, maps, g, h, part, packed, h_in, h_out, sems):
    half, depth = frozen.shape[0] // split, frozen.shape[1]
    width = maps.shape[1]
    at = pl.multiple_of(lax.axis_index("groups") % split * half, half)
    load = pltpu.make_async_copy(h, h_in, sems.at[0])
    copies = [
        pltpu.make_async_copy(g, packed.at[:, :depth], sems.at[1]),
        pltpu.make_async_copy(frozen.at[pl.ds(at, half)], part.at[:, :depth], sems.at[2]),
    ]
    for i in range(split):
        cols = slice(depth + i * width, depth + (i + 1) * width)
        rows = slice(i * half, (i + 1) * half)
        copies.append(pltpu.make_async_copy(maps.at[rows], part.at[:, cols], sems.at[3 + i]))
    load.start()
    for copy in copies:
        copy.start()
    load.wait()
    h_out[...] = jnp.concatenate([h_in[...].T] * HIDDEN_COPIES, axis=1)
    copies.append(pltpu.make_async_copy(h_out, packed.at[:, depth:], sems.at[5]))
    copies[-1].start()
    for copy in copies:
        copy.wait()


def first_sent(split, frozen, maps, g, h):
    half, depth = frozen.shape[0] // split, frozen.shape[1]
    rows = g.shape[0]
    part = (half, depth + split * maps.shape[1])
    packed = (rows, depth + HIDDEN_COPIES * ADAPTER_RANK)
    return pl.pallas_call(
        functools.partial(first_kernel, split),
        out_shape=(jax.ShapeDtypeStruct(part, BF16), jax.ShapeDtypeStruct(packed, BF16)),
        in_specs=[HBM] * 4,
        out_specs=[ANY, ANY],
        scratch_shapes=[
            pltpu.VMEM(h.shape, BF16),
            pltpu.VMEM((rows, HIDDEN_COPIES * ADAPTER_RANK), BF16),
            pltpu.SemaphoreType.DMA((6,)),
        ],
        compiler_params=params(8 << 20),
        cost_estimate=cost(1),
        name="first_sent",
    )(frozen, maps, g, h)


def hold_kernel(*refs):
    del refs


def hold(x, *after):
    return pl.pallas_call(
        hold_kernel,
        out_shape=jax.ShapeDtypeStruct(x.shape, x.dtype),
        in_specs=[ANY] * (1 + len(after)),
        out_specs=ANY,
        input_output_aliases={0: 0},
        compiler_params=params(1 << 20),
        cost_estimate=cost(0),
        name="hold",
    )(x, *after)


def down_kernel(members, g, b, tokens, after, send, keep, g_in, b_in, block, result, sems, out_sems):
    del after
    rows, width = g.shape[0], b.shape[0]
    blocks, _, per = send.shape
    me = lax.axis_index("dp")
    first = [
        pltpu.make_async_copy(g, g_in, out_sems.at[0]),
        pltpu.make_async_copy(b, b_in, out_sems.at[1]),
    ]
    loads = []
    for i in range(2 * blocks):
        mine = me % 2 if i % 2 else 1 - me % 2
        at = pl.ds(pl.multiple_of((i // 2 * 2 + mine) * per, per), per)
        loads.append(pltpu.make_async_copy(tokens.at[:, at], block.at[i], sems.at[i]))
    for copy in first + loads:
        copy.start()
    for copy in first:
        copy.wait()
    wide = nt(b_in[...], g_in[...])
    owner = member_of_rows(members, me * (rows // BLOCK), (width, rows), 1)
    column = lax.broadcasted_iota(jnp.int32, (width, rows), 0) // ADAPTER_RANK
    left = jnp.where(owner == column, adapter_scale * wide, 0.0).astype(BF16)
    stores = []
    for i in [*range(0, 2 * blocks, 2), *range(1, 2 * blocks, 2)]:
        loads[i].wait()
        result[i] = jnp.dot(left, block[i], preferred_element_type=F32).astype(BF16)
        target = (keep if i % 2 else send).at[i // 2]
        stores.append(pltpu.make_async_copy(result.at[i], target, out_sems.at[2 + i]))
        stores[-1].start()
    for copy in stores:
        copy.wait()


def down_partials(members, g, b, tokens, per, n, after):
    rows, width = g.shape[0], b.shape[0]
    shape = jax.ShapeDtypeStruct((n // 2, width, per), BF16)
    return pl.pallas_call(
        down_kernel,
        out_shape=(shape, shape),
        in_specs=[SMEM] + [HBM] * 3 + [ANY],
        out_specs=[ANY, ANY],
        scratch_shapes=[
            pltpu.VMEM(g.shape, BF16),
            pltpu.VMEM(b.shape, BF16),
            pltpu.VMEM((n, rows, per), BF16),
            pltpu.VMEM((n, width, per), BF16),
            pltpu.SemaphoreType.DMA((n,)),
            pltpu.SemaphoreType.DMA((n + 2,)),
        ],
        compiler_params=params(12 << 20),
        cost_estimate=cost(COST_DOWN),
        name="down_partials",
    )(members, g, b, tokens, after)


def spread_kernel(members, b, *refs):
    gs, spread, up = refs[:INNER], refs[INNER], refs[INNER + 1]
    width, depth = b.shape
    rows = gs[0].shape[0]
    planes, piece, per = up.shape
    half, cols = width // 2, depth // 2
    across = cols // per
    z, q = where_am_i()
    total = jnp.zeros((half, cols), F32)
    for j in range(INNER):
        first = (z * INNER + (q ^ j)) * (rows // BLOCK)
        wide = nt(gs[j][:, :depth], b[...])
        owner = member_of_rows(members, first, (rows, width), 0)
        column = lax.broadcasted_iota(jnp.int32, (rows, width), 1) // ADAPTER_RANK
        spread[j] = jnp.where(owner == column, adapter_scale * wide, 0.0).astype(BF16)
        hidden = gs[j][:, depth:]
        column = column[:, :half] + (q // 2) * (half // ADAPTER_RANK)
        hidden = jnp.where(owner[:, :half] == column, hidden, jnp.zeros_like(hidden))
        total = total + tn(hidden, gs[j][:, pl.ds(pl.multiple_of((q % 2) * cols, cols), cols)])
    total = (adapter_scale * total).astype(BF16)
    for t in range(planes):
        row, col = t // across * piece, t % across * per
        up[t] = total[row : row + piece, col : col + per]


def spread_rows(members, b, gs, per, planes):
    rows, (width, depth) = gs[0].shape[0], b.shape
    return pl.pallas_call(
        spread_kernel,
        out_shape=(
            jax.ShapeDtypeStruct((INNER, rows, width), BF16),
            jax.ShapeDtypeStruct((planes, width * depth // (INNER * planes * per), per), BF16),
        ),
        in_specs=[SMEM] + [VMEM] * (1 + INNER),
        out_specs=[VMEM, VMEM],
        compiler_params=params(8 << 20),
        cost_estimate=cost(COST_SPREAD),
        name="spread_rows",
    )(members, b, *gs)


def on_choice(turn, options, act):
    planes = lax.axis_size("dp") // INNER
    z, _ = where_am_i()
    for i, option in enumerate(options):
        hit = functools.reduce(
            jnp.logical_or,
            [z == p for p in range(planes) if source(turn, p, planes) == option],
        )
        pl.when(hit)(functools.partial(act, i))


def part_index(side):
    if side in (0, 1):
        return side
    parity = lax.axis_index("groups") % 2
    return parity if side == "mine" else 1 - parity


def product_kernel(plan, n_sources, *refs):
    spread, gs, refs = refs[0], refs[1 : 1 + INNER], refs[1 + INNER :]
    sources, outs, (a, sems) = refs[:n_sources], refs[-5:-2], refs[-2:]
    _, unit, width = a.shape
    rows = gs[0].shape[0]
    weights, copies = [], []
    for h, (turn, side, split, w_at, maps_at) in enumerate(plan):
        index = part_index(side) if split > 1 else 0
        if turn:
            weights.append(sources[w_at])
            depth = sources[w_at].shape[1]
            cols = pl.ds(pl.multiple_of(depth + index * width, width), width)

            def maps(i, h=h, cols=cols, maps_at=maps_at):
                return pltpu.make_async_copy(
                    sources[maps_at[i][1]].at[:, cols], a.at[h], sems.at[h]
                )

            on_choice(turn, [o for o, _ in maps_at], lambda i, maps=maps: maps(i).start())
            copies.append(maps(0))
        else:
            at = slice(index * unit, (index + 1) * unit)
            weights.append(sources[w_at].at[at])
            copies.append(pltpu.make_async_copy(sources[maps_at].at[at], a.at[h], sems.at[h]))
            copies[-1].start()
    for copy in copies:
        copy.wait()
    for j in (2, 3, 1, 0):
        for h, w in enumerate(weights):
            value = (nt(gs[j][:, : w.shape[1]], w[...]) + nt(spread[j], a[h])).astype(BF16)
            at = slice(h * unit, (h + 1) * unit)
            if j < 2:
                outs[j][:, at] = value
            else:
                outs[2][(j - 2) * rows : (j - 1) * rows, at] = value


def product(plan, sources, spread, gs, unit, after):
    rows, width = gs[0].shape[0], spread.shape[2]
    n, cols = len(plan), len(plan) * unit
    shape = jax.ShapeDtypeStruct((rows, cols), BF16)
    pair = jax.ShapeDtypeStruct((2 * rows, cols), BF16)
    weights = {w_at for _, _, _, w_at, _ in plan}
    return pl.pallas_call(
        functools.partial(product_kernel, plan, len(sources)),
        out_shape=(shape, shape, pair),
        in_specs=[VMEM] * (1 + INNER)
        + [VMEM if i in weights else ANY for i in range(len(sources))]
        + [ANY] * len(after),
        out_specs=[VMEM] * 3,
        scratch_shapes=[pltpu.VMEM((n, unit, width), BF16), pltpu.SemaphoreType.DMA((n,))],
        compiler_params=params(12 << 20),
        cost_estimate=cost(COST_MM),
        name="product",
    )(spread, *gs, *sources, *after)


def choose_kernel(turn, options, *refs):
    out, sem = refs[-2], refs[-1]
    depth = out.shape[1]

    def fetch(i):
        copy = pltpu.make_async_copy(refs[i].at[:, :depth], out, sem)
        copy.start()
        copy.wait()

    on_choice(turn, options, fetch)


def choose(turn, options, parts, depth, after):
    half = parts[0].shape[0]
    return pl.pallas_call(
        functools.partial(choose_kernel, turn, options),
        out_shape=jax.ShapeDtypeStruct((half, depth), BF16),
        in_specs=[ANY] * (len(parts) + len(after)),
        out_specs=VMEM,
        scratch_shapes=[pltpu.SemaphoreType.DMA],
        compiler_params=params(4 << 20),
        cost_estimate=cost(1),
        name="choose",
    )(*parts, *after)


def place_kernel(plan, own, core, across, both, *refs):
    out, token, sem = refs[-3:]
    rows, cols = own.shape
    unit = cols // len(plan)
    z, q = where_am_i()
    copies = []
    for h, (turn, side, split, *_) in enumerate(plan):
        index = part_index(side) if split > 1 else 0
        shard = shard_of(turn, z) * INNER
        for j, piece in enumerate((own, core, across, both)):
            at = pl.ds(pl.multiple_of(((shard + (q ^ j)) * split + index) * unit, unit), unit)
            source = piece.at[:rows, h * unit : (h + 1) * unit]
            copies.append(pltpu.make_async_copy(source, out.at[:, at], sem.at[h, j]))
            copies[-1].start()
    token[...] = jnp.zeros(token.shape, F32)
    for copy in copies:
        copy.wait()


def place(plan, pieces, out, shape, after, microseconds=COST_PLACE):
    given = [] if out is None else [out]
    return pl.pallas_call(
        functools.partial(place_kernel, plan),
        out_shape=(shape, jax.ShapeDtypeStruct((8, 128), F32)),
        in_specs=[VMEM] * INNER + [ANY] * (len(given) + len(after)),
        out_specs=[ANY, VMEM],
        scratch_shapes=[pltpu.SemaphoreType.DMA((len(plan), INNER))],
        input_output_aliases={INNER: 0} if given else {},
        compiler_params=params(6 << 20),
        cost_estimate=cost(microseconds),
        name="place",
    )(*pieces, *given, *after)


def start_loads(keep, got, up, came, t, block, sems):
    width = keep.shape[1]
    copies = [
        pltpu.make_async_copy(keep.at[2 * t + i], block.at[0, i * width : (i + 1) * width], sems.at[i])
        for i in range(2)
    ] + [
        pltpu.make_async_copy(got.at[2 * t + i], block.at[1, i * width : (i + 1) * width], sems.at[2 + i])
        for i in range(2)
    ]
    copies.append(pltpu.make_async_copy(up.at[t], block.at[0, 2 * width :], sems.at[4]))
    for i, c in enumerate(came):
        copies.append(pltpu.make_async_copy(c, block.at[2 + i], sems.at[5 + i]))
    for copy in copies:
        copy.start()
    return copies


def add_up(block, width, n_came):
    values = []
    for at in (slice(0, width), slice(width, 2 * width), slice(2 * width, None)):
        value = block[0, at].astype(F32)
        if at.stop:
            value = value + block[1, at].astype(F32)
        for i in range(n_came):
            value = value + block[2 + i, at].astype(F32)
        values.append(value)
    return values


def term_kernel(step, links, n_came, *refs):
    came, (keep, got, up), refs = refs[:n_came], refs[n_came : n_came + 3], refs[n_came + 3 :]
    n = len(links)
    width = keep.shape[1]
    outs, block, sems = refs[-2 - n : -2], refs[-2], refs[-1]
    planes = lax.axis_size("dp") // INNER
    z, _ = where_am_i()
    given, loads = list(came), []
    for i, (link, has) in enumerate(links):
        t = jnp.clip(jnp.where(z % 2 == link, z + step, z - step), 0, planes - 1)
        before = [given.pop(0)] if has else []
        loads.append(start_loads(keep, got, up, before, t, block.at[i], sems.at[i]))
    for i, (link, has) in enumerate(links):
        for copy in loads[i]:
            copy.wait()
        first, second, value = add_up(block.at[i], width, 1 if has else 0)
        outs[i][:width] = first.astype(BF16)
        outs[i][width : 2 * width] = second.astype(BF16)
        outs[i][2 * width :] = value.astype(BF16)


def terms(step, links, came, keep, got, up, after):
    rows = 2 * keep.shape[1] + up.shape[1]
    shape = jax.ShapeDtypeStruct((rows, keep.shape[2]), BF16)
    return pl.pallas_call(
        functools.partial(term_kernel, step, links, len(came)),
        out_shape=(shape,) * len(links),
        in_specs=[ANY] * (len(came) + 3 + len(after)),
        out_specs=[VMEM] * len(links),
        scratch_shapes=[
            pltpu.VMEM((len(links), 3, *shape.shape), BF16),
            pltpu.SemaphoreType.DMA((len(links), 6)),
        ],
        compiler_params=params(10 << 20),
        cost_estimate=cost(COST_TERM),
        name="running_sums",
    )(*came, keep, got, up, *after)


def total_kernel(n_came, *refs):
    came, (keep, got, up), refs = refs[:n_came], refs[n_came : n_came + 3], refs[n_came + 3 :]
    send, kept, piece, block, sems = refs[-5:]
    z, q = where_am_i()
    for copy in start_loads(keep, got, up, came, z, block, sems):
        copy.wait()
    first, second, value = add_up(block, keep.shape[1], n_came)
    low = q // 2 == 0
    kept[...] = jnp.where(low, first, second)
    send[...] = jnp.where(low, second, first).astype(BF16)
    piece[...] = value.astype(BF16)


def totals(came, keep, got, up, after):
    rows = 2 * keep.shape[1] + up.shape[1]
    return pl.pallas_call(
        functools.partial(total_kernel, len(came)),
        out_shape=(
            jax.ShapeDtypeStruct(keep.shape[1:], BF16),
            jax.ShapeDtypeStruct(keep.shape[1:], F32),
            jax.ShapeDtypeStruct(up.shape[1:], BF16),
        ),
        in_specs=[ANY] * (len(came) + 3 + len(after)),
        out_specs=[VMEM] * 3,
        scratch_shapes=[
            pltpu.VMEM((2 + len(came), rows, keep.shape[2]), BF16),
            pltpu.SemaphoreType.DMA((5 + len(came),)),
        ],
        compiler_params=params(10 << 20),
        cost_estimate=cost(COST_TERM),
        name="totals",
    )(*came, keep, got, up, *after)


def quarter_kernel(*refs):
    pieces, out = refs[:-1], refs[-1]
    planes = len(pieces)
    rows, per = pieces[0].shape
    across = out.shape[1] // per
    z, _ = where_am_i()
    for k, piece in enumerate(pieces):
        t = (z - k + planes) % planes
        row = pl.ds(pl.multiple_of(t // across * rows, rows), rows)
        col = pl.ds(pl.multiple_of(t % across * per, per), per)
        out[row, col] = piece[...]


def quarter(pieces, shape):
    return pl.pallas_call(
        quarter_kernel,
        out_shape=jax.ShapeDtypeStruct(shape, BF16),
        in_specs=[VMEM] * len(pieces),
        out_specs=VMEM,
        compiler_params=params(2 << 20),
        cost_estimate=cost(1),
        name="quarter",
    )(*pieces)


def finish_kernel(kept, other, q0, q1, q2, q3, down, up):
    down[...] = (kept[...] + other[...].astype(F32)).T
    rows, cols = q0.shape
    _, q = where_am_i()
    for j, part in enumerate((q0, q1, q2, q3)):
        row = pl.ds(pl.multiple_of((q ^ j) // 2 * rows, rows), rows)
        col = pl.ds(pl.multiple_of((q ^ j) % 2 * cols, cols), cols)
        up[row, col] = part[...].astype(F32)


def finish(kept, other, quarters):
    rows, cols = quarters[0].shape
    return pl.pallas_call(
        finish_kernel,
        out_shape=(
            jax.ShapeDtypeStruct(kept.shape[::-1], F32),
            jax.ShapeDtypeStruct((2 * rows, 2 * cols), F32),
        ),
        in_specs=[VMEM] * 6,
        out_specs=[VMEM] * 2,
        compiler_params=params(6 << 20),
        cost_estimate=cost(1),
        name="finish",
    )(kept, other, *quarters)


def source(turn, z, planes):
    both = min(z, planes - 1 - z)
    if turn <= 2 * both:
        return (turn + 1) // 2, 1 - turn % 2
    even_is_far = (z % 2 == 0) == (z < planes // 2)
    return turn - both, 0 if even_is_far else 1


def far_plane(z, step, link):
    return z + step if z % 2 == link else z - step


def shard_of(turn, z):
    planes = lax.axis_size("dp") // INNER
    result = z
    if turn:
        for plane in range(planes):
            step, link = source(turn, plane, planes)
            result = jnp.where(z == plane, far_plane(plane, step, link), result)
    return result


def edges(step, link, planes):
    pairs = []
    for z in range(planes):
        right = z % 2 == link
        origin, to = (z - step + 1, z + 1) if right else (z + step - 1, z - 1)
        if 0 <= origin < planes and 0 <= to < planes:
            pairs.append((z, to))
    return pairs


def local(tokens, output_gradient, hidden, frozen, down_maps, up_maps, members):
    n = lax.axis_size("dp")
    groups = lax.axis_size("groups")
    planes = n // INNER
    per = frozen.shape[0]
    rows = tokens.shape[0]
    width, depth = up_maps.shape
    split = 2 if per % 256 == 0 and groups % 2 == 0 else 1
    unit = per // split

    def inner(x, bit):
        return lax.ppermute(x, "dp", [(i, i ^ bit) for i in range(n)])

    def along(x, pairs):
        return lax.ppermute(
            x, "dp", [(s * INNER + i, t * INNER + i) for s, t in pairs for i in range(INNER)]
        )

    def twin(x):
        return lax.ppermute(x, "groups", [(i, i ^ 1) for i in range(groups)])

    held = {}

    def pass_on(k):
        for link in (0, 1):
            if k > 1 and (k - 1, link) in held:
                held[k - 1, link] = hold(held[k - 1, link], mine[k - 1])
        for link in (0, 1):
            pairs = edges(k, link, planes) if k < planes else []
            if pairs:
                held[k, link] = along(held[k - 1, 1 - link], pairs)

    came = {}

    def add_on(k, after):
        links = [l for l in (0, 1) if edges(k, l, planes)]
        got_before = [came[k + 1, 1 - l] for l in links if (k + 1, 1 - l) in came]
        flags = [(l, (k + 1, 1 - l) in came) for l in links]
        values = terms(k, flags, got_before, keep, got, up, after)
        for link, value in zip(links, values):
            came[k, link] = along(value, [(t, s) for s, t in edges(k, link, planes)])
        return values[0]

    at = lax.axis_index("groups") % split * unit
    maps = [down_maps[i * unit : (i + 1) * unit] for i in range(split)]
    part = jnp.concatenate([lax.dynamic_slice_in_dim(frozen, at, unit), *maps], axis=1)
    packed = jnp.concatenate([output_gradient] + [hidden] * HIDDEN_COPIES, axis=1)
    held[0, 0] = held[0, 1] = part
    g2 = inner(packed, 2)
    pass_on(1)
    g1 = inner(packed, 1)
    send, keep = down_partials(members, output_gradient, up_maps, tokens, per, n, g1)
    got = inner(send, 1)
    g2 = hold(g2, send)
    g3 = inner(g2, 1)
    gs = [packed, g1, g2, g3]
    spread, up = spread_rows(members, up_maps, gs, per, planes)

    out_shape = jax.ShapeDtypeStruct(tokens.shape, BF16)

    def hand_on(turn, after):
        own, core, across = pieces[turn]
        if after is not None:
            across = hold(across, after)
        pieces[turn] = own, core, across, inner(across[rows:], 1)

    mine, theirs, plans, pieces = {}, {}, {}, {}
    result, token = None, send

    def shard_options(turn):
        options = sorted({source(turn, p, planes) for p in range(planes)})
        return options, [held[o] for o in options]

    def multiply(k, after):
        sources, plan = [], []

        def add(x):
            sources.append(x)
            return len(sources) - 1

        def add_part(turn, side, w):
            options, parts = shard_options(turn)
            maps = [(option, add(x)) for option, x in zip(options, parts)]
            plan.append((turn, side, split, add(w), maps))

        if k == 1:
            at = add(frozen), add(down_maps)
            plan += [(0, i, split, *at) for i in range(split)]
        elif split > 1:
            add_part(k - 1, "theirs", theirs[k - 1])
        if k < planes:
            add_part(k, "mine", mine[k])
        if not plan:
            return after[0]
        plans[k] = plan
        blocks = product(plan, sources, spread, gs, unit, after)
        pieces[k] = blocks[0], inner(blocks[1], 1), inner(blocks[2], 2)
        return blocks[0]

    def hand_on(k, after):
        own, core, across = pieces[k]
        if after is not None:
            across = hold(across, after)
        pieces[k] = own, core, across, inner(across[rows:], 1)
        return across

    last = send
    for k in range(1, planes):
        options, parts = shard_options(k)
        waits = [held[k, l] for l in (0, 1) if (k, l) in held]
        waits += [theirs[k - 1]] if k - 1 in theirs else []
        waits += [came[planes - k + 1, l] for l in (0, 1) if (planes - k + 1, l) in came]
        mine[k] = choose(k, options, parts, depth, waits + [last, token])
        pass_on(k + 1)
        if split > 1:
            theirs[k] = twin(mine[k])
        summed = add_on(planes - k, [mine[k]])
        across = hand_on(k - 1, summed) if k > 1 else summed
        last = multiply(k, [across])
        if k > 1:
            result, token = place(plans[k - 1], pieces[k - 1], result, out_shape, [last])
    if planes > 1:
        last = hand_on(planes - 1, last)
    last = multiply(planes, [last])
    if planes > 1:
        result, token = place(plans[planes - 1], pieces[planes - 1], result, out_shape, [last])
    came_last = [came[1, l] for l in (0, 1) if (1, l) in came]
    down_send, down_kept, piece = totals(came_last, keep, got, up, [])
    other = inner(down_send, 2)
    moved = [
        along(piece, [(s, (s + k) % planes) for s in range(planes)]) for k in range(1, planes)
    ]
    mine_up = quarter([piece, *moved], (width // 2, depth // 2))
    over_y = inner(mine_up, 2)
    quarters = [mine_up, inner(mine_up, 1), over_y, inner(over_y, 1)]
    if planes in plans:
        hand_on(planes, None)
        result, token = place(plans[planes], pieces[planes], result, out_shape, [], COST_LAST)
    down_grad, up_grad = finish(down_kept, other, quarters)
    return result, down_grad, up_grad


def solution(mesh):
    in_specs = (
        P(("groups", "dp"), None),
        P(("groups", "dp"), None),
        P(("groups", "dp"), None),
        P("dp", None),
        P(("groups", "dp"), None),
        P("groups", None),
        P("groups"),
    )
    out_specs = (P(("groups", "dp"), None), P(("groups", "dp"), None), P("groups", None))
    return jax.shard_map(local, mesh=mesh, in_specs=in_specs, out_specs=out_specs, check_vma=False)
```

time: 404 us -> 120 us (0.30)
  waiting for transfers between devices: 358 us -> 43.8 us
  starting transfers between devices: 0.16 us -> 44.3 us
  matrix products: 25.5 us -> 0 us
  Pallas kernels: 0 us -> 24.5 us
  between operations: 13.8 us -> 1.29 us
    all_gather x2 -> x0, waiting for transfers between devices: 170 us -> none  [the longest x1 127 us: local(): lax.all_gather(frozen_value_weight, 'dp', axis=0, tiled=True)]
    reduce_scatter x1 -> x0, waiting for transfers between devices: 102 us -> none  [local(): lax.psum_scatter(jnp.dot(tokens.T, expanded_rows, preferred_element_type=...]
    psum x1 -> x0, waiting for transfers between devices: 84.8 us -> none  [local(): up_map_gradient = lax.psum(partial_up_gradient, 'dp')]
    ppermute x0 -> x36, starting transfers between devices: none -> 44.3 us  [the longest x13 28 us: along(): lax.ppermute(x, 'dp', [(s * INNER + i, t * INNER + i) for s, t in pairs f...]
    ppermute x0 -> x36, waiting for transfers between devices: none -> 43.8 us  [the longest x20 27.7 us: inner(): return lax.ppermute(x, 'dp', [(i, i ^ bit) for i in range(n)])]
    dot_general x5 -> x0, matrix products: 25.5 us -> none  [the longest x1 10.7 us: local(): jnp.dot(output_gradient, lax.all_gather(frozen_value_weight, 'dp', axis=0...]
    pallas_call x0 -> x28, Pallas kernels: none -> 24.5 us  [the longest x4 6.96 us: product(): pl.pallas_call(functools.partial(product_kernel, plan, len(sources)), out...]
  transfers between devices with their start and end apart: 4 -> 36, of which waited for: 4 -> 11; matrix products, arithmetic and copies ran while one was open for 7% -> 1% of each run, Pallas kernels for 0% -> 19%
where the time goes in v2:
time: 120 us; the launch traced here: 119 us
  starting transfers between devices  44.3 us (37%)
  waiting for transfers between devices  43.8 us (36%)
  Pallas kernels  24.5 us (20%)
  local copies, waits for them, and re-layouts  5.55 us (5%)
  between operations  1.29 us (1%)
    ppermute x13, starting transfers between devices, along(): lax.ppermute(x, 'dp', [(s * INNER + i, t * INNER + i) for s, t in pairs f...  28 us
    ppermute x20, waiting for transfers between devices, inner(): return lax.ppermute(x, 'dp', [(i, i ^ bit) for i in range(n)])  27.7 us
    ppermute x3, waiting for transfers between devices, twin(): return lax.ppermute(x, 'groups', [(i, i ^ 1) for i in range(groups)])  13.6 us
    ppermute x20, starting transfers between devices, inner(): return lax.ppermute(x, 'dp', [(i, i ^ bit) for i in range(n)])  12.7 us
    pallas_call x4, Pallas kernels, product(): pl.pallas_call(functools.partial(product_kernel, plan, len(sources)), out...  6.96 us
    pallas_call x1, Pallas kernels, down_partials(): pl.pallas_call(down_kernel, out_shape=(shape, shape), in_specs=[SMEM] + [...  5.91 us
    pallas_call x4, Pallas kernels, place(): pl.pallas_call(functools.partial(place_kernel, plan), out_shape=(shape, j...  5.88 us
    ppermute x3, starting transfers between devices, twin(): return lax.ppermute(x, 'groups', [(i, i ^ 1) for i in range(groups)])  3.58 us
  transfers between devices with their start and end apart: 36, of which 11 were waited for; matrix products, arithmetic and copies ran while one was open for 1% of the time, Pallas kernels for 19%

profile of v2, /device:TPU:0, one launch (start us, length us, event | category | flops | bytes accessed | tf_op | source)
XLA Modules:
  0.0 119.4 jit_solution(6604456216302523713)
XLA Ops:
  0.6 0.9 copy.22
  1.6 1.3 %concatenate.6.refs_0_.refs_1_ = bf16[256,1152]{1,0:T(8,128)(2,1)S(1)} concatenate(bf16[256,1024]{1,0:T(8,128)(2,1)} %g.1, bf16[256,64]{1,0:T(8,128)(2,1)S(1)} %copy.22, bf16[256,64]{1,0:T(8,128)(2,1)S(1)} %copy.22), dimensions={1} | concatenate | bytes 1179648 | tf_op jit(solution)/shard_map/concatenate | solution.py:591
  2.9 0.5 collective-permute-start
  3.4 1.1 constant_dynamic-slice_fusion
  4.5 0.1 pad_maximum_fusion
  4.6 2.7 %collective-permute-start.3 = (bf16[256,1536]{1,0:T(8,128)(2,1)S(1)}, bf16[256,1536]{1,0:T(8,128)(2,1)S(1)}, u32[]{:S(2)}, u32[]{:S(2)}) collective-permute-start(bf16[256,1536]{1,0:T(8,128)(2,1)S(1)} %pad_maximum_fusion), channel_id=1, source_target_pairs={{0,4},{1,5},{2,6},{3,7},{4,0},{5,1},{6,2},{7,3},{8,12},{9,13},{10,... | collective-permute-start | bytes 2359304 | tf_op jit(solution)/shard_map/ppermute | solution.py:559
  7.2 0.7 collective-permute-start.4
  7.9 1.6 %collective-permute-start.1 = (bf16[256,1152]{1,0:T(8,128)(2,1)S(1)}, bf16[256,1152]{1,0:T(8,128)(2,1)S(1)}, u32[]{:S(2)}, u32[]{:S(2)}) collective-permute-start(bf16[256,1152]{1,0:T(8,128)(2,1)S(1)} %concatenate.6.refs_0_.refs_1_), channel_id=1, source_target_pairs={{0,2},{1,3},{2,0},{3,1},{4,6},{5,7},{6,4},{7,5},{8,10},{9,11},{10,... | collective-permute-start | bytes 1769480 | tf_op jit(solution)/shard_map/ppermute | solution.py:556
  9.6 2.2 %copy-done.3 = bf16[256,8192]{1,0:T(8,128)(2,1)S(1)} copy-done((bf16[256,8192]{1,0:T(8,128)(2,1)S(1)}, bf16[256,8192]{1,0:T(8,128)(2,1)}, u32[]{:S(2)}) %copy-start.3) | copy-done | bytes 4194328
  11.7 5.9 %down_partials.1 = (bf16[8,256,512]{2,1,0:T(8,128)(2,1)S(1)}, bf16[8,256,512]{2,1,0:T(8,128)(2,1)S(1)}) custom-call(s32[32]{0:T(128)S(1)} %copy-done.5, bf16[256,1024]{1,0:T(8,128)(2,1)S(1)} %copy-done, bf16[256,1024]{1,0:T(8,128)(2,1)S(1)} %copy-done.4, bf16[256,8192]{1,0:T(8,128)(2,1)S(1)} %copy-done.3, ...), custom_call_target="tpu_custom_call" | custom-call | flops 6600000000 | bytes 19800000 | tf_op jit(solution)/shard_map/down_partials/pallas_call | solution.py:165
  17.6 5.8 %collective-permute-done.1.refs_0_ = bf16[256,1152]{1,0:T(8,128)(2,1)S(1)} collective-permute-done((bf16[256,1152]{1,0:T(8,128)(2,1)S(1)}, bf16[256,1152]{1,0:T(8,128)(2,1)S(1)}, u32[]{:S(2)}, u32[]{:S(2)}) %collective-permute-start.1) | collective-permute-done | bytes 589856 | tf_op jit(solution)/shard_map/ppermute | solution.py:556
  23.4 0.5 collective-permute-start.8
  23.9 1.5 %collective-permute-done.3.refs_0_.refs_1_ = bf16[256,1536]{1,0:T(8,128)(2,1)S(1)} collective-permute-done((bf16[256,1536]{1,0:T(8,128)(2,1)S(1)}, bf16[256,1536]{1,0:T(8,128)(2,1)S(1)}, u32[]{:S(2)}, u32[]{:S(2)}) %collective-permute-start.3) | collective-permute-done | bytes 786464 | tf_op jit(solution)/shard_map/ppermute | solution.py:559
  25.4 0.1 choose.3.refs_1_.refs_3_.refs_8_
  25.5 1.3 %collective-permute-start.6 = (bf16[256,1536]{1,0:T(8,128)(2,1)S(1)}, bf16[256,1536]{1,0:T(8,128)(2,1)S(1)}, u32[]{:S(2)}, u32[]{:S(2)}) collective-permute-start(bf16[256,1536]{1,0:T(8,128)(2,1)S(1)} %hold.11.refs_0_.refs_7_.refs_5_), channel_id=1, source_target_pairs={{4,0},{5,1},{6,2},{7,3},{8,12},{9,13},{10,14},{11,15},{20,16},{21,... | collective-permute-start | bytes 2359304 | tf_op jit(solution)/shard_map/ppermute | solution.py:559
  26.8 0.7 collective-permute-start.5
  27.5 1.5 %spread_rows.1 = (bf16[4,256,256]{2,1,0:T(8,128)(2,1)S(1)}, bf16[4,32,512]{2,1,0:T(8,128)(2,1)S(1)}) custom-call(s32[32]{0:T(128)S(1)} %copy-done.5, bf16[256,1024]{1,0:T(8,128)(2,1)S(1)} %copy-done.4, bf16[256,1152]{1,0:T(8,128)(2,1)S(1)} %concatenate.6.refs_0_.refs_1_, bf16[256,1152]{1,0:T(8,128)(2,1)S(1)} %collective-permute-done.after.refs_1_.refs_2_, ...), custom_call_target="tpu_custom_call" | custom-call | flops 44000002048 | bytes 132000000 | tf_op jit(solution)/shard_map/spread_rows/pallas_call | solution.py:211
  29.0 0.3 running_sums.3.refs_9_
  29.3 9.7 %collective-permute-start.9 = (bf16[544,512]{1,0:T(8,128)(2,1)S(1)}, bf16[544,512]{1,0:T(8,128)(2,1)S(1)}, u32[]{:S(2)}, u32[]{:S(2)}) collective-permute-start(bf16[544,512]{1,0:T(8,128)(2,1)S(1)} %running_sums.3.refs_9_), channel_id=1, source_target_pairs={{0,4},{1,5},{2,6},{3,7},{12,8},{13,9},{14,10},{15,11},{16,20},{17,... | collective-permute-start | bytes 1671176 | tf_op jit(solution)/shard_map/ppermute | solution.py:559
  39.0 1.6 %collective-permute-start.7 = (bf16[256,1024]{1,0:T(8,128)(2,1)S(1)}, bf16[256,1024]{1,0:T(8,128)(2,1)S(1)}, u32[]{:S(2)}, u32[]{:S(2)}) collective-permute-start(bf16[256,1024]{1,0:T(8,128)(2,1)S(1)} %choose.3.refs_1_.refs_3_.refs_8_), channel_id=1, source_target_pairs={{0,16},{16,0},{1,17},{17,1},{2,18},{18,2},{3,19},{19,3},{4,20},{20... | collective-permute-start | bytes 1572872 | tf_op jit(solution)/shard_map/ppermute | solution.py:564
  40.6 2.6 %product.4 = (bf16[256,768]{1,0:T(8,128)(2,1)S(1)}, bf16[256,768]{1,0:T(8,128)(2,1)S(1)}, bf16[512,768]{1,0:T(8,128)(2,1)S(1)}) custom-call(bf16[4,256,256]{2,1,0:T(8,128)(2,1)S(1)} %get-tuple-element.34.refs_0_, bf16[256,1152]{1,0:T(8,128)(2,1)S(1)} %concatenate.6.refs_0_.refs_1_, bf16[256,1152]{1,0:T(8,128)(2,1)S(1)} %collective-permute-done.after.refs_1_.refs_2_, ...), custom_call_target="tpu_custom_call" | custom-call | flops 3300000000 | bytes 9900000 | tf_op jit(solution)/shard_map/product/pallas_call | solution.py:286
  43.2 1.6 %collective-permute-start.14 = (bf16[512,768]{1,0:T(8,128)(2,1)S(1)}, bf16[512,768]{1,0:T(8,128)(2,1)S(1)}, u32[]{:S(2)}, u32[]{:S(2)}) collective-permute-start(bf16[512,768]{1,0:T(8,128)(2,1)S(1)} %get-tuple-element.40), channel_id=1, source_target_pairs={{0,2},{1,3},{2,0},{3,1},{4,6},{5,7},{6,4},{7,5},{8,10},{9,11},{10,... | collective-permute-start | bytes 2359304 | tf_op jit(solution)/shard_map/ppermute | solution.py:556
  44.8 6.9 %collective-permute-done.7.refs_4_.refs_6_ = bf16[256,1024]{1,0:T(8,128)(2,1)S(1)} collective-permute-done((bf16[256,1024]{1,0:T(8,128)(2,1)S(1)}, bf16[256,1024]{1,0:T(8,128)(2,1)S(1)}, u32[]{:S(2)}, u32[]{:S(2)}) %collective-permute-start.7) | collective-permute-done | bytes 524320 | tf_op jit(solution)/shard_map/ppermute | solution.py:564
  51.8 0.1 choose.4.refs_1_.refs_4_.refs_9_
  51.9 1.3 %collective-permute-start.10 = (bf16[256,1536]{1,0:T(8,128)(2,1)S(1)}, bf16[256,1536]{1,0:T(8,128)(2,1)S(1)}, u32[]{:S(2)}, u32[]{:S(2)}) collective-permute-start(bf16[256,1536]{1,0:T(8,128)(2,1)S(1)} %hold.12.refs_0_.refs_8_.refs_5_), channel_id=1, source_target_pairs={{4,0},{5,1},{6,2},{7,3},{8,12},{9,13},{10,14},{11,15},{20,16},{21,... | collective-permute-start | bytes 2359304 | tf_op jit(solution)/shard_map/ppermute | solution.py:559
  53.2 0.8 running_sums.4
  53.9 4.6 %collective-permute-start.12 = (bf16[544,512]{1,0:T(8,128)(2,1)S(1)}, bf16[544,512]{1,0:T(8,128)(2,1)S(1)}, u32[]{:S(2)}, u32[]{:S(2)}) collective-permute-start(bf16[544,512]{1,0:T(8,128)(2,1)S(1)} %get-tuple-element.38.refs_1_), channel_id=1, source_target_pairs={{0,4},{1,5},{2,6},{3,7},{12,8},{13,9},{14,10},{15,11},{16,20},{17,... | collective-permute-start | bytes 1671176 | tf_op jit(solution)/shard_map/ppermute | solution.py:559
  58.6 0.7 collective-permute-start.13
  59.3 2.0 %collective-permute-done.14.refs_0_ = bf16[512,768]{1,0:T(8,128)(2,1)S(1)} collective-permute-done((bf16[512,768]{1,0:T(8,128)(2,1)S(1)}, bf16[512,768]{1,0:T(8,128)(2,1)S(1)}, u32[]{:S(2)}, u32[]{:S(2)}) %collective-permute-start.14) | collective-permute-done | bytes 786464 | tf_op jit(solution)/shard_map/ppermute | solution.py:556
  61.3 0.5 collective-permute-start.11
  61.8 0.1 collective-permute-start.16
  61.9 1.6 %product.5 = (bf16[256,512]{1,0:T(8,128)(2,1)S(1)}, bf16[256,512]{1,0:T(8,128)(2,1)S(1)}, bf16[512,512]{1,0:T(8,128)(2,1)S(1)}) custom-call(bf16[4,256,256]{2,1,0:T(8,128)(2,1)S(1)} %get-tuple-element.34.refs_0_, bf16[256,1152]{1,0:T(8,128)(2,1)S(1)} %concatenate.6.refs_0_.refs_1_, bf16[256,1152]{1,0:T(8,128)(2,1)S(1)} %collective-permute-done.after.refs_1_.refs_2_, ...), custom_call_target="tpu_custom_call" | custom-call | flops 3300000000 | bytes 9900000 | tf_op jit(solution)/shard_map/product/pallas_call | solution.py:286
  63.6 0.1 collective-permute-done.16.both
  63.6 1.5 %collective-permute-start.18 = (bf16[512,512]{1,0:T(8,128)(2,1)S(1)}, bf16[512,512]{1,0:T(8,128)(2,1)S(1)}, u32[]{:S(2)}, u32[]{:S(2)}) collective-permute-start(bf16[512,512]{1,0:T(8,128)(2,1)S(1)} %get-tuple-element.44), channel_id=1, source_target_pairs={{0,2},{1,3},{2,0},{3,1},{4,6},{5,7},{6,4},{7,5},{8,10},{9,11},{10,... | collective-permute-start | bytes 1572872 | tf_op jit(solution)/shard_map/ppermute | solution.py:556
  65.2 1.2 %place.4 = (bf16[256,8192]{1,0:T(8,128)(2,1)}, f32[8,128]{1,0:T(8,128)S(1)}) custom-call(bf16[256,768]{1,0:T(8,128)(2,1)S(1)} %get-tuple-element.37.refs_6_.own, bf16[256,768]{1,0:T(8,128)(2,1)S(1)} %collective-permute-done.15.core, bf16[512,768]{1,0:T(8,128)(2,1)S(1)} %hold.14.refs_10_.across, bf16[256,768]{1,0:T(8,128)(2,1)S(1)} %collective-permute-done.16.both, ...), custom_call_target="tpu_custom_call" | custom-call | flops 1100000000 | bytes 3300000 | tf_op jit(solution)/shard_map/place/pallas_call | solution.py:347
  66.4 6.7 %collective-permute-done.11.refs_3_.refs_7_ = bf16[256,1024]{1,0:T(8,128)(2,1)S(1)} collective-permute-done((bf16[256,1024]{1,0:T(8,128)(2,1)S(1)}, bf16[256,1024]{1,0:T(8,128)(2,1)S(1)}, u32[]{:S(2)}, u32[]{:S(2)}) %collective-permute-start.11) | collective-permute-done | bytes 524320 | tf_op jit(solution)/shard_map/ppermute | solution.py:564
  73.1 0.6 collective-permute-done.10.refs_1_.refs_2_.refs_0_
  73.8 0.9 running_sums.5
  74.7 0.9 collective-permute-start.27
  75.6 0.7 collective-permute-start.28
  76.3 1.6 %collective-permute-done.18.refs_0_ = bf16[512,512]{1,0:T(8,128)(2,1)S(1)} collective-permute-done((bf16[512,512]{1,0:T(8,128)(2,1)S(1)}, bf16[512,512]{1,0:T(8,128)(2,1)S(1)}, u32[]{:S(2)}, u32[]{:S(2)}) %collective-permute-start.18) | collective-permute-done | bytes 524320 | tf_op jit(solution)/shard_map/ppermute | solution.py:556
  77.9 1.8 %product.6 = (bf16[256,512]{1,0:T(8,128)(2,1)S(1)}, bf16[256,512]{1,0:T(8,128)(2,1)S(1)}, bf16[512,512]{1,0:T(8,128)(2,1)S(1)}) custom-call(bf16[4,256,256]{2,1,0:T(8,128)(2,1)S(1)} %get-tuple-element.34.refs_0_, bf16[256,1152]{1,0:T(8,128)(2,1)S(1)} %concatenate.6.refs_0_.refs_1_, bf16[256,1152]{1,0:T(8,128)(2,1)S(1)} %collective-permute-done.after.refs_1_.refs_2_, ...), custom_call_target="tpu_custom_call" | custom-call | flops 3300000000 | bytes 9900000 | tf_op jit(solution)/shard_map/product/pallas_call | solution.py:286
  79.7 1.6 %collective-permute-start.19 = (bf16[512,512]{1,0:T(8,128)(2,1)S(1)}, bf16[512,512]{1,0:T(8,128)(2,1)S(1)}, u32[]{:S(2)}, u32[]{:S(2)}) collective-permute-start(bf16[512,512]{1,0:T(8,128)(2,1)S(1)} %get-tuple-element.46), channel_id=1, source_target_pairs={{0,2},{1,3},{2,0},{3,1},{4,6},{5,7},{6,4},{7,5},{8,10},{9,11},{10,... | collective-permute-start | bytes 1572872 | tf_op jit(solution)/shard_map/ppermute | solution.py:556
  81.3 1.5 %collective-permute-start.17 = (bf16[256,1024]{1,0:T(8,128)(2,1)S(1)}, bf16[256,1024]{1,0:T(8,128)(2,1)S(1)}, u32[]{:S(2)}, u32[]{:S(2)}) collective-permute-start(bf16[256,1024]{1,0:T(8,128)(2,1)S(1)} %choose.5.refs_1_.refs_5_.refs_10_), channel_id=1, source_target_pairs={{0,16},{16,0},{1,17},{17,1},{2,18},{18,2},{3,19},{19,3},{4,20},{20... | collective-permute-start | bytes 1572872 | tf_op jit(solution)/shard_map/ppermute | solution.py:564
  82.8 10.5 %collective-permute-done.19.refs_0_ = bf16[512,512]{1,0:T(8,128)(2,1)S(1)} collective-permute-done((bf16[512,512]{1,0:T(8,128)(2,1)S(1)}, bf16[512,512]{1,0:T(8,128)(2,1)S(1)}, u32[]{:S(2)}, u32[]{:S(2)}) %collective-permute-start.19) | collective-permute-done | bytes 524320 | tf_op jit(solution)/shard_map/ppermute | solution.py:556
  93.3 0.7 totals.1
  94.0 1.0 collective-permute-start.30
  95.0 1.2 collective-permute-start.31
  96.1 2.6 %collective-permute-start.32 = (bf16[32,512]{1,0:T(8,128)(2,1)S(1)}, bf16[32,512]{1,0:T(8,128)(2,1)S(1)}, u32[]{:S(2)}, u32[]{:S(2)}) collective-permute-start(bf16[32,512]{1,0:T(8,128)(2,1)S(1)} %get-tuple-element.60.refs_0_), channel_id=1, source_target_pairs={{0,12},{1,13},{2,14},{3,15},{4,0},{5,1},{6,2},{7,3},{8,4},{9,5},{1... | collective-permute-start | bytes 98312 | tf_op jit(solution)/shard_map/ppermute | solution.py:559
  98.7 0.9 product.7
  99.7 0.4 collective-permute-done.30.refs_1_
  100.0 1.5 %collective-permute-start.21 = (bf16[512,256]{1,0:T(8,128)(2,1)S(1)}, bf16[512,256]{1,0:T(8,128)(2,1)S(1)}, u32[]{:S(2)}, u32[]{:S(2)}) collective-permute-start(bf16[512,256]{1,0:T(8,128)(2,1)S(1)} %get-tuple-element.50), channel_id=1, source_target_pairs={{0,2},{1,3},{2,0},{3,1},{4,6},{5,7},{6,4},{7,5},{8,10},{9,11},{10,... | collective-permute-start | bytes 786440 | tf_op jit(solution)/shard_map/ppermute | solution.py:556
  101.6 0.1 collective-permute-start.23
  101.7 0.5 collective-permute-start.24
  102.2 0.9 collective-permute-start.34
  103.1 1.2 collective-permute-start.29
  104.3 7.8 %collective-permute-done.34.q2 = bf16[128,512]{1,0:T(8,128)(2,1)S(1)} collective-permute-done((bf16[128,512]{1,0:T(8,128)(2,1)S(1)}, bf16[128,512]{1,0:T(8,128)(2,1)S(1)}, u32[]{:S(2)}, u32[]{:S(2)}) %collective-permute-start.34) | collective-permute-done | bytes 131104 | tf_op jit(solution)/shard_map/ppermute | solution.py:556
  112.1 0.5 collective-permute-start.35
  112.6 1.6 %place.5 = (bf16[256,8192]{1,0:T(8,128)(2,1)}, f32[8,128]{1,0:T(8,128)}) custom-call(bf16[256,512]{1,0:T(8,128)(2,1)S(1)} %get-tuple-element.41.refs_0_.refs_6_.own, bf16[256,512]{1,0:T(8,128)(2,1)S(1)} %collective-permute-done.25.core, bf16[512,512]{1,0:T(8,128)(2,1)S(1)} %hold.16.refs_11_.across, ...), custom_call_target="tpu_custom_call", output_to_operand_aliasing={{0}: (4, {})} | custom-call | flops 1100000000 | bytes 3300000 | tf_op jit(solution)/shard_map/place/pallas_call | solution.py:347
  114.2 0.1 collective-permute-start.20
  114.3 0.5 collective-permute-start.22
  114.8 1.6 %place.6 = (bf16[256,8192]{1,0:T(8,128)(2,1)}, f32[8,128]{1,0:T(8,128)}) custom-call(bf16[256,512]{1,0:T(8,128)(2,1)S(1)} %get-tuple-element.47.refs_1_.own, bf16[256,512]{1,0:T(8,128)(2,1)S(1)} %collective-permute-done.23.core, bf16[512,512]{1,0:T(8,128)(2,1)S(1)} %hold.17.refs_8_.across, ...), custom_call_target="tpu_custom_call", output_to_operand_aliasing={{0}: (4, {})} | custom-call | flops 1100000000 | bytes 3300000 | tf_op jit(solution)/shard_map/place/pallas_call | solution.py:347
  116.5 1.3 %finish.1 = (f32[512,256]{1,0:T(8,128)}, f32[256,1024]{1,0:T(8,128)}) custom-call(f32[256,512]{1,0:T(8,128)S(1)} %get-tuple-element.58.kept, bf16[256,512]{1,0:T(8,128)(2,1)S(1)} %collective-permute-done.29.other, bf16[128,512]{1,0:T(8,128)(2,1)S(1)} %quarter.1.q0, bf16[128,512]{1,0:T(8,128)(2,1)S(1)} %collective-permute-done.33.q1, ...), custom_call_target="tpu_custom_call" | custom-call | flops 1100000000 | bytes 3300000 | tf_op jit(solution)/shard_map/finish/pallas_call | solution.py:499
  117.8 1.4 %place.7 = (bf16[256,8192]{1,0:T(8,128)(2,1)}, f32[8,128]{1,0:T(8,128)}) custom-call(bf16[256,256]{1,0:T(8,128)(2,1)S(1)} %get-tuple-element.48.refs_1_.own, bf16[256,256]{1,0:T(8,128)(2,1)S(1)} %collective-permute-done.20.core, bf16[512,256]{1,0:T(8,128)(2,1)S(1)} %collective-permute-done.21.across, ...), custom_call_target="tpu_custom_call", output_to_operand_aliasing={{0}: (4, {})} | custom-call | flops 16499999744 | bytes 49500000 | tf_op jit(solution)/shard_map/place/pallas_call | solution.py:347
  (57 shorter events, 0.3 us)
Async XLA Ops:
  0.6 3.8 %copy-start.1 = (bf16[512,256]{1,0:T(8,128)(2,1)S(1)}, bf16[512,256]{1,0:T(8,128)(2,1)}, u32[]{:S(2)}) copy-start(bf16[512,256]{1,0:T(8,128)(2,1)} %refs_6_.1) | copy-start | bytes 786436
  1.6 8.0 %copy-start = (bf16[256,1024]{1,0:T(8,128)(2,1)S(1)}, bf16[256,1024]{1,0:T(8,128)(2,1)}, u32[]{:S(2)}) copy-start(bf16[256,1024]{1,0:T(8,128)(2,1)} %g.1) | copy-start | bytes 1572868
  1.6 8.0 %copy-start.4 = (bf16[256,1024]{1,0:T(8,128)(2,1)S(1)}, bf16[256,1024]{1,0:T(8,128)(2,1)}, u32[]{:S(2)}) copy-start(bf16[256,1024]{1,0:T(8,128)(2,1)} %b.3) | copy-start | bytes 1572868
  1.6 8.0 %copy-start.5 = (s32[32]{0:T(128)S(1)}, s32[32]{0:T(128)}, u32[]{:S(2)}) copy-start(s32[32]{0:T(128)} %members.3) | copy-start | bytes 388
  2.9 6.7 %collective-permute-start = (bf16[256,1152]{1,0:T(8,128)(2,1)S(1)}, bf16[256,1152]{1,0:T(8,128)(2,1)S(1)}, u32[]{:S(2)}, u32[]{:S(2)}) collective-permute-start(bf16[256,1152]{1,0:T(8,128)(2,1)S(1)} %concatenate.6.refs_0_.refs_1_), channel_id=1, source_target_pairs={{0,1},{1,0},{2,3},{3,2},{4,5},{5,4},{6,7},{7,6},{8,9},{9,8},{10,11... | collective-permute-start | bytes 1769480 | tf_op jit(solution)/shard_map/ppermute | solution.py:556
  4.6 20.9 %collective-permute-start.3 = (bf16[256,1536]{1,0:T(8,128)(2,1)S(1)}, bf16[256,1536]{1,0:T(8,128)(2,1)S(1)}, u32[]{:S(2)}, u32[]{:S(2)}) collective-permute-start(bf16[256,1536]{1,0:T(8,128)(2,1)S(1)} %pad_maximum_fusion), channel_id=1, source_target_pairs={{0,4},{1,5},{2,6},{3,7},{4,0},{5,1},{6,2},{7,3},{8,12},{9,13},{10,... | collective-permute-start | bytes 2359304 | tf_op jit(solution)/shard_map/ppermute | solution.py:559
  7.2 18.2 %collective-permute-start.4 = (bf16[256,1536]{1,0:T(8,128)(2,1)S(1)}, bf16[256,1536]{1,0:T(8,128)(2,1)S(1)}, u32[]{:S(2)}, u32[]{:S(2)}) collective-permute-start(bf16[256,1536]{1,0:T(8,128)(2,1)S(1)} %pad_maximum_fusion), channel_id=1, source_target_pairs={{4,8},{5,9},{6,10},{7,11},{8,4},{9,5},{10,6},{11,7},{20,24},{21,25... | collective-permute-start | bytes 2359304 | tf_op jit(solution)/shard_map/ppermute | solution.py:559
  7.9 15.5 %collective-permute-start.1 = (bf16[256,1152]{1,0:T(8,128)(2,1)S(1)}, bf16[256,1152]{1,0:T(8,128)(2,1)S(1)}, u32[]{:S(2)}, u32[]{:S(2)}) collective-permute-start(bf16[256,1152]{1,0:T(8,128)(2,1)S(1)} %concatenate.6.refs_0_.refs_1_), channel_id=1, source_target_pairs={{0,2},{1,3},{2,0},{3,1},{4,6},{5,7},{6,4},{7,5},{8,10},{9,11},{10,... | collective-permute-start | bytes 1769480 | tf_op jit(solution)/shard_map/ppermute | solution.py:556
  9.5 2.2 %copy-start.3 = (bf16[256,8192]{1,0:T(8,128)(2,1)S(1)}, bf16[256,8192]{1,0:T(8,128)(2,1)}, u32[]{:S(2)}) copy-start(bf16[256,8192]{1,0:T(8,128)(2,1)} %tokens.1) | copy-start | bytes 12582916
  23.4 4.1 %collective-permute-start.2 = (bf16[256,1152]{1,0:T(8,128)(2,1)S(1)}, bf16[256,1152]{1,0:T(8,128)(2,1)S(1)}, u32[]{:S(2)}, u32[]{:S(2)}) collective-permute-start(bf16[256,1152]{1,0:T(8,128)(2,1)S(1)} %hold.9.refs_2_.refs_3_), channel_id=1, source_target_pairs={{0,1},{1,0},{2,3},{3,2},{4,5},{5,4},{6,7},{7,6},{8,9},{9,8},{10,11... | collective-permute-start | bytes 1769480 | tf_op jit(solution)/shard_map/ppermute | solution.py:556
  23.4 5.6 %collective-permute-start.8 = (bf16[8,256,512]{2,1,0:T(8,128)(2,1)S(1)}, bf16[8,256,512]{2,1,0:T(8,128)(2,1)S(1)}, u32[]{:S(2)}, u32[]{:S(2)}) collective-permute-start(bf16[8,256,512]{2,1,0:T(8,128)(2,1)S(1)} %get-tuple-element.33.refs_1_.refs_3_.refs_4_.refs_7_), channel_id=1, source_target_pairs={{0,1},{1,0},{2,3},{3,2},{4,5},{5,4},{6,7},{7,6},{8,9},{9,8},{10,11... | collective-permute-start | bytes 6291464 | tf_op jit(solution)/shard_map/ppermute | solution.py:556
  25.5 26.3 %collective-permute-start.6 = (bf16[256,1536]{1,0:T(8,128)(2,1)S(1)}, bf16[256,1536]{1,0:T(8,128)(2,1)S(1)}, u32[]{:S(2)}, u32[]{:S(2)}) collective-permute-start(bf16[256,1536]{1,0:T(8,128)(2,1)S(1)} %hold.11.refs_0_.refs_7_.refs_5_), channel_id=1, source_target_pairs={{4,0},{5,1},{6,2},{7,3},{8,12},{9,13},{10,14},{11,15},{20,16},{21,... | collective-permute-start | bytes 2359304 | tf_op jit(solution)/shard_map/ppermute | solution.py:559
  26.8 25.0 %collective-permute-start.5 = (bf16[256,1536]{1,0:T(8,128)(2,1)S(1)}, bf16[256,1536]{1,0:T(8,128)(2,1)S(1)}, u32[]{:S(2)}, u32[]{:S(2)}) collective-permute-start(bf16[256,1536]{1,0:T(8,128)(2,1)S(1)} %hold.10.refs_7_.refs_5_), channel_id=1, source_target_pairs={{4,8},{5,9},{6,10},{7,11},{8,4},{9,5},{10,6},{11,7},{20,24},{21,25... | collective-permute-start | bytes 2359304 | tf_op jit(solution)/shard_map/ppermute | solution.py:559
  29.0 11.6 %copy-start.2 = (bf16[512,1024]{1,0:T(8,128)(2,1)S(1)}, bf16[512,1024]{1,0:T(8,128)(2,1)}, u32[]{:S(2)}) copy-start(bf16[512,1024]{1,0:T(8,128)(2,1)} %refs_5_.1) | copy-start | bytes 3145732
  29.3 22.4 %collective-permute-start.9 = (bf16[544,512]{1,0:T(8,128)(2,1)S(1)}, bf16[544,512]{1,0:T(8,128)(2,1)S(1)}, u32[]{:S(2)}, u32[]{:S(2)}) collective-permute-start(bf16[544,512]{1,0:T(8,128)(2,1)S(1)} %running_sums.3.refs_9_), channel_id=1, source_target_pairs={{0,4},{1,5},{2,6},{3,7},{12,8},{13,9},{14,10},{15,11},{16,20},{17,... | collective-permute-start | bytes 1671176 | tf_op jit(solution)/shard_map/ppermute | solution.py:559
  39.0 12.7 %collective-permute-start.7 = (bf16[256,1024]{1,0:T(8,128)(2,1)S(1)}, bf16[256,1024]{1,0:T(8,128)(2,1)S(1)}, u32[]{:S(2)}, u32[]{:S(2)}) collective-permute-start(bf16[256,1024]{1,0:T(8,128)(2,1)S(1)} %choose.3.refs_1_.refs_3_.refs_8_), channel_id=1, source_target_pairs={{0,16},{16,0},{1,17},{17,1},{2,18},{18,2},{3,19},{19,3},{4,20},{20... | collective-permute-start | bytes 1572872 | tf_op jit(solution)/shard_map/ppermute | solution.py:564
  43.2 18.1 %collective-permute-start.14 = (bf16[512,768]{1,0:T(8,128)(2,1)S(1)}, bf16[512,768]{1,0:T(8,128)(2,1)S(1)}, u32[]{:S(2)}, u32[]{:S(2)}) collective-permute-start(bf16[512,768]{1,0:T(8,128)(2,1)S(1)} %get-tuple-element.40), channel_id=1, source_target_pairs={{0,2},{1,3},{2,0},{3,1},{4,6},{5,7},{6,4},{7,5},{8,10},{9,11},{10,... | collective-permute-start | bytes 2359304 | tf_op jit(solution)/shard_map/ppermute | solution.py:556
  51.7 10.1 %collective-permute-start.15 = (bf16[256,768]{1,0:T(8,128)(2,1)S(1)}, bf16[256,768]{1,0:T(8,128)(2,1)S(1)}, u32[]{:S(2)}, u32[]{:S(2)}) collective-permute-start(bf16[256,768]{1,0:T(8,128)(2,1)S(1)} %get-tuple-element.42), channel_id=1, source_target_pairs={{0,1},{1,0},{2,3},{3,2},{4,5},{5,4},{6,7},{7,6},{8,9},{9,8},{10,11... | collective-permute-start | bytes 1179656 | tf_op jit(solution)/shard_map/ppermute | solution.py:556
  51.9 21.8 %collective-permute-start.10 = (bf16[256,1536]{1,0:T(8,128)(2,1)S(1)}, bf16[256,1536]{1,0:T(8,128)(2,1)S(1)}, u32[]{:S(2)}, u32[]{:S(2)}) collective-permute-start(bf16[256,1536]{1,0:T(8,128)(2,1)S(1)} %hold.12.refs_0_.refs_8_.refs_5_), channel_id=1, source_target_pairs={{4,0},{5,1},{6,2},{7,3},{8,12},{9,13},{10,14},{11,15},{20,16},{21,... | collective-permute-start | bytes 2359304 | tf_op jit(solution)/shard_map/ppermute | solution.py:559
  53.9 19.2 %collective-permute-start.12 = (bf16[544,512]{1,0:T(8,128)(2,1)S(1)}, bf16[544,512]{1,0:T(8,128)(2,1)S(1)}, u32[]{:S(2)}, u32[]{:S(2)}) collective-permute-start(bf16[544,512]{1,0:T(8,128)(2,1)S(1)} %get-tuple-element.38.refs_1_), channel_id=1, source_target_pairs={{0,4},{1,5},{2,6},{3,7},{12,8},{13,9},{14,10},{15,11},{16,20},{17,... | collective-permute-start | bytes 1671176 | tf_op jit(solution)/shard_map/ppermute | solution.py:559
  58.6 14.6 %collective-permute-start.13 = (bf16[544,512]{1,0:T(8,128)(2,1)S(1)}, bf16[544,512]{1,0:T(8,128)(2,1)S(1)}, u32[]{:S(2)}, u32[]{:S(2)}) collective-permute-start(bf16[544,512]{1,0:T(8,128)(2,1)S(1)} %get-tuple-element.39), channel_id=1, source_target_pairs={{8,4},{9,5},{10,6},{11,7},{4,8},{5,9},{6,10},{7,11},{24,20},{25,21... | collective-permute-start | bytes 1671176 | tf_op jit(solution)/shard_map/ppermute | solution.py:559
  61.3 11.8 %collective-permute-start.11 = (bf16[256,1024]{1,0:T(8,128)(2,1)S(1)}, bf16[256,1024]{1,0:T(8,128)(2,1)S(1)}, u32[]{:S(2)}, u32[]{:S(2)}) collective-permute-start(bf16[256,1024]{1,0:T(8,128)(2,1)S(1)} %choose.4.refs_1_.refs_4_.refs_9_), channel_id=1, source_target_pairs={{0,16},{16,0},{1,17},{17,1},{2,18},{18,2},{3,19},{19,3},{4,20},{20... | collective-permute-start | bytes 1572872 | tf_op jit(solution)/shard_map/ppermute | solution.py:564
  61.8 1.8 %collective-permute-start.16 = (bf16[256,768]{1,0:T(8,128)(2,1)S(1)}, bf16[256,768]{1,0:T(8,128)(2,1)S(1)}, u32[]{:S(2)}, u32[]{:S(2)}) collective-permute-start(bf16[256,768]{1,0:T(8,128)(2,1)S(1)} %slice.24), channel_id=1, source_target_pairs={{0,1},{1,0},{2,3},{3,2},{4,5},{5,4},{6,7},{7,6},{8,9},{9,8},{10,11... | collective-permute-start | bytes 1179656 | tf_op jit(solution)/shard_map/ppermute | solution.py:556
  63.6 14.3 %collective-permute-start.18 = (bf16[512,512]{1,0:T(8,128)(2,1)S(1)}, bf16[512,512]{1,0:T(8,128)(2,1)S(1)}, u32[]{:S(2)}, u32[]{:S(2)}) collective-permute-start(bf16[512,512]{1,0:T(8,128)(2,1)S(1)} %get-tuple-element.44), channel_id=1, source_target_pairs={{0,2},{1,3},{2,0},{3,1},{4,6},{5,7},{6,4},{7,5},{8,10},{9,11},{10,... | collective-permute-start | bytes 1572872 | tf_op jit(solution)/shard_map/ppermute | solution.py:556
  74.7 18.6 %collective-permute-start.27 = (bf16[544,512]{1,0:T(8,128)(2,1)S(1)}, bf16[544,512]{1,0:T(8,128)(2,1)S(1)}, u32[]{:S(2)}, u32[]{:S(2)}) collective-permute-start(bf16[544,512]{1,0:T(8,128)(2,1)S(1)} %get-tuple-element.45.refs_1_), channel_id=1, source_target_pairs={{4,0},{5,1},{6,2},{7,3},{0,4},{1,5},{2,6},{3,7},{12,8},{13,9},{14,... | collective-permute-start | bytes 1671176 | tf_op jit(solution)/shard_map/ppermute | solution.py:559
  75.6 17.7 %collective-permute-start.28 = (bf16[544,512]{1,0:T(8,128)(2,1)S(1)}, bf16[544,512]{1,0:T(8,128)(2,1)S(1)}, u32[]{:S(2)}, u32[]{:S(2)}) collective-permute-start(bf16[544,512]{1,0:T(8,128)(2,1)S(1)} %get-tuple-element.57), channel_id=1, source_target_pairs={{8,4},{9,5},{10,6},{11,7},{4,8},{5,9},{6,10},{7,11},{24,20},{25,21... | collective-permute-start | bytes 1671176 | tf_op jit(solution)/shard_map/ppermute | solution.py:559
  79.7 13.6 %collective-permute-start.19 = (bf16[512,512]{1,0:T(8,128)(2,1)S(1)}, bf16[512,512]{1,0:T(8,128)(2,1)S(1)}, u32[]{:S(2)}, u32[]{:S(2)}) collective-permute-start(bf16[512,512]{1,0:T(8,128)(2,1)S(1)} %get-tuple-element.46), channel_id=1, source_target_pairs={{0,2},{1,3},{2,0},{3,1},{4,6},{5,7},{6,4},{7,5},{8,10},{9,11},{10,... | collective-permute-start | bytes 1572872 | tf_op jit(solution)/shard_map/ppermute | solution.py:556
  81.3 14.8 %collective-permute-start.17 = (bf16[256,1024]{1,0:T(8,128)(2,1)S(1)}, bf16[256,1024]{1,0:T(8,128)(2,1)S(1)}, u32[]{:S(2)}, u32[]{:S(2)}) collective-permute-start(bf16[256,1024]{1,0:T(8,128)(2,1)S(1)} %choose.5.refs_1_.refs_5_.refs_10_), channel_id=1, source_target_pairs={{0,16},{16,0},{1,17},{17,1},{2,18},{18,2},{3,19},{19,3},{4,20},{20... | collective-permute-start | bytes 1572872 | tf_op jit(solution)/shard_map/ppermute | solution.py:564
  82.8 19.4 %collective-permute-start.25 = (bf16[256,512]{1,0:T(8,128)(2,1)S(1)}, bf16[256,512]{1,0:T(8,128)(2,1)S(1)}, u32[]{:S(2)}, u32[]{:S(2)}) collective-permute-start(bf16[256,512]{1,0:T(8,128)(2,1)S(1)} %get-tuple-element.52), channel_id=1, source_target_pairs={{0,1},{1,0},{2,3},{3,2},{4,5},{5,4},{6,7},{7,6},{8,9},{9,8},{10,11... | collective-permute-start | bytes 786440 | tf_op jit(solution)/shard_map/ppermute | solution.py:556
  93.3 9.8 %collective-permute-start.26 = (bf16[256,512]{1,0:T(8,128)(2,1)S(1)}, bf16[256,512]{1,0:T(8,128)(2,1)S(1)}, u32[]{:S(2)}, u32[]{:S(2)}) collective-permute-start(bf16[256,512]{1,0:T(8,128)(2,1)S(1)} %slice.27), channel_id=1, source_target_pairs={{0,1},{1,0},{2,3},{3,2},{4,5},{5,4},{6,7},{7,6},{8,9},{9,8},{10,11... | collective-permute-start | bytes 786440 | tf_op jit(solution)/shard_map/ppermute | solution.py:556
  94.0 6.0 %collective-permute-start.30 = (bf16[32,512]{1,0:T(8,128)(2,1)S(1)}, bf16[32,512]{1,0:T(8,128)(2,1)S(1)}, u32[]{:S(2)}, u32[]{:S(2)}) collective-permute-start(bf16[32,512]{1,0:T(8,128)(2,1)S(1)} %get-tuple-element.60.refs_0_), channel_id=1, source_target_pairs={{0,4},{1,5},{2,6},{3,7},{4,8},{5,9},{6,10},{7,11},{8,12},{9,13},{1... | collective-permute-start | bytes 98312 | tf_op jit(solution)/shard_map/ppermute | solution.py:559
  95.0 6.6 %collective-permute-start.31 = (bf16[32,512]{1,0:T(8,128)(2,1)S(1)}, bf16[32,512]{1,0:T(8,128)(2,1)S(1)}, u32[]{:S(2)}, u32[]{:S(2)}) collective-permute-start(bf16[32,512]{1,0:T(8,128)(2,1)S(1)} %get-tuple-element.60.refs_0_), channel_id=1, source_target_pairs={{0,8},{1,9},{2,10},{3,11},{4,12},{5,13},{6,14},{7,15},{8,0},{9,1},... | collective-permute-start | bytes 98312 | tf_op jit(solution)/shard_map/ppermute | solution.py:559
  96.1 5.5 %collective-permute-start.32 = (bf16[32,512]{1,0:T(8,128)(2,1)S(1)}, bf16[32,512]{1,0:T(8,128)(2,1)S(1)}, u32[]{:S(2)}, u32[]{:S(2)}) collective-permute-start(bf16[32,512]{1,0:T(8,128)(2,1)S(1)} %get-tuple-element.60.refs_0_), channel_id=1, source_target_pairs={{0,12},{1,13},{2,14},{3,15},{4,0},{5,1},{6,2},{7,3},{8,4},{9,5},{1... | collective-permute-start | bytes 98312 | tf_op jit(solution)/shard_map/ppermute | solution.py:559
  100.0 12.1 %collective-permute-start.21 = (bf16[512,256]{1,0:T(8,128)(2,1)S(1)}, bf16[512,256]{1,0:T(8,128)(2,1)S(1)}, u32[]{:S(2)}, u32[]{:S(2)}) collective-permute-start(bf16[512,256]{1,0:T(8,128)(2,1)S(1)} %get-tuple-element.50), channel_id=1, source_target_pairs={{0,2},{1,3},{2,0},{3,1},{4,6},{5,7},{6,4},{7,5},{8,10},{9,11},{10,... | collective-permute-start | bytes 786440 | tf_op jit(solution)/shard_map/ppermute | solution.py:556
  101.6 12.6 %collective-permute-start.23 = (bf16[256,512]{1,0:T(8,128)(2,1)S(1)}, bf16[256,512]{1,0:T(8,128)(2,1)S(1)}, u32[]{:S(2)}, u32[]{:S(2)}) collective-permute-start(bf16[256,512]{1,0:T(8,128)(2,1)S(1)} %get-tuple-element.51), channel_id=1, source_target_pairs={{0,1},{1,0},{2,3},{3,2},{4,5},{5,4},{6,7},{7,6},{8,9},{9,8},{10,11... | collective-permute-start | bytes 786440 | tf_op jit(solution)/shard_map/ppermute | solution.py:556
  101.7 12.6 %collective-permute-start.24 = (bf16[256,512]{1,0:T(8,128)(2,1)S(1)}, bf16[256,512]{1,0:T(8,128)(2,1)S(1)}, u32[]{:S(2)}, u32[]{:S(2)}) collective-permute-start(bf16[256,512]{1,0:T(8,128)(2,1)S(1)} %slice.26), channel_id=1, source_target_pairs={{0,1},{1,0},{2,3},{3,2},{4,5},{5,4},{6,7},{7,6},{8,9},{9,8},{10,11... | collective-permute-start | bytes 786440 | tf_op jit(solution)/shard_map/ppermute | solution.py:556
  102.2 9.9 %collective-permute-start.34 = (bf16[128,512]{1,0:T(8,128)(2,1)S(1)}, bf16[128,512]{1,0:T(8,128)(2,1)S(1)}, u32[]{:S(2)}, u32[]{:S(2)}) collective-permute-start(bf16[128,512]{1,0:T(8,128)(2,1)S(1)} %quarter.1.q0), channel_id=1, source_target_pairs={{0,2},{1,3},{2,0},{3,1},{4,6},{5,7},{6,4},{7,5},{8,10},{9,11},{10,... | collective-permute-start | bytes 393224 | tf_op jit(solution)/shard_map/ppermute | solution.py:556
  103.1 13.4 %collective-permute-start.29 = (bf16[256,512]{1,0:T(8,128)(2,1)S(1)}, bf16[256,512]{1,0:T(8,128)(2,1)S(1)}, u32[]{:S(2)}, u32[]{:S(2)}) collective-permute-start(bf16[256,512]{1,0:T(8,128)(2,1)S(1)} %get-tuple-element.59), channel_id=1, source_target_pairs={{0,2},{1,3},{2,0},{3,1},{4,6},{5,7},{6,4},{7,5},{8,10},{9,11},{10,... | collective-permute-start | bytes 786440 | tf_op jit(solution)/shard_map/ppermute | solution.py:556
  112.1 4.4 %collective-permute-start.33 = (bf16[128,512]{1,0:T(8,128)(2,1)S(1)}, bf16[128,512]{1,0:T(8,128)(2,1)S(1)}, u32[]{:S(2)}, u32[]{:S(2)}) collective-permute-start(bf16[128,512]{1,0:T(8,128)(2,1)S(1)} %quarter.1.q0), channel_id=1, source_target_pairs={{0,1},{1,0},{2,3},{3,2},{4,5},{5,4},{6,7},{7,6},{8,9},{9,8},{10,11... | collective-permute-start | bytes 393224 | tf_op jit(solution)/shard_map/ppermute | solution.py:556
  112.1 4.4 %collective-permute-start.35 = (bf16[128,512]{1,0:T(8,128)(2,1)S(1)}, bf16[128,512]{1,0:T(8,128)(2,1)S(1)}, u32[]{:S(2)}, u32[]{:S(2)}) collective-permute-start(bf16[128,512]{1,0:T(8,128)(2,1)S(1)} %collective-permute-done.34.q2), channel_id=1, source_target_pairs={{0,1},{1,0},{2,3},{3,2},{4,5},{5,4},{6,7},{7,6},{8,9},{9,8},{10,11... | collective-permute-start | bytes 393224 | tf_op jit(solution)/shard_map/ppermute | solution.py:556
  114.2 3.6 %collective-permute-start.20 = (bf16[256,256]{1,0:T(8,128)(2,1)S(1)}, bf16[256,256]{1,0:T(8,128)(2,1)S(1)}, u32[]{:S(2)}, u32[]{:S(2)}) collective-permute-start(bf16[256,256]{1,0:T(8,128)(2,1)S(1)} %get-tuple-element.49), channel_id=1, source_target_pairs={{0,1},{1,0},{2,3},{3,2},{4,5},{5,4},{6,7},{7,6},{8,9},{9,8},{10,11... | collective-permute-start | bytes 393224 | tf_op jit(solution)/shard_map/ppermute | solution.py:556
  114.3 3.5 %collective-permute-start.22 = (bf16[256,256]{1,0:T(8,128)(2,1)S(1)}, bf16[256,256]{1,0:T(8,128)(2,1)S(1)}, u32[]{:S(2)}, u32[]{:S(2)}) collective-permute-start(bf16[256,256]{1,0:T(8,128)(2,1)S(1)} %slice.25), channel_id=1, source_target_pairs={{0,1},{1,0},{2,3},{3,2},{4,5},{5,4},{6,7},{7,6},{8,9},{9,8},{10,11... | collective-permute-start | bytes 393224 | tf_op jit(solution)/shard_map/ppermute | solution.py:556

commit v3 on v2

--- a/solution.py
+++ b/solution.py
@@ -17,13 +17,17 @@
 adapter_scale = 2.0
 VMEM_BYTES = 24 << 20
 
-COST_DOWN = 6
-COST_SPREAD = 40
-COST_MM = 3
-COST_PLACE = 1
-COST_LAST = 15
+COST_DOWN = 1
+COST_SPREAD = 2.0
+COST_CHOOSE = 40.0
+COST_MM = 3.0
+COST_PLACE = 1.0
+COST_HAND = 30
+COST_DOWN_END = 10.0
+COST_TWIN = 10.0
+COST_LAST = 10
 COST_OWN = 40
-COST_TERM = 4
+COST_TERM = 4.0
 
 F32 = jnp.float32
 BF16 = jnp.bfloat16
@@ -64,56 +68,28 @@
     return result
 
 
-def first_kernel(split, frozen, maps, g, h, part, packed, h_in, h_out, sems):
-    half, depth = frozen.shape[0] // split, frozen.shape[1]
-    width = maps.shape[1]
-    at = pl.multiple_of(lax.axis_index("groups") % split * half, half)
-    load = pltpu.make_async_copy(h, h_in, sems.at[0])
-    copies = [
-        pltpu.make_async_copy(g, packed.at[:, :depth], sems.at[1]),
-        pltpu.make_async_copy(frozen.at[pl.ds(at, half)], part.at[:, :depth], sems.at[2]),
-    ]
-    for i in range(split):
-        cols = slice(depth + i * width, depth + (i + 1) * width)
-        rows = slice(i * half, (i + 1) * half)
-        copies.append(pltpu.make_async_copy(maps.at[rows], part.at[:, cols], sems.at[3 + i]))
-    load.start()
-    for copy in copies:
-        copy.start()
-    load.wait()
-    h_out[...] = jnp.concatenate([h_in[...].T] * HIDDEN_COPIES, axis=1)
-    copies.append(pltpu.make_async_copy(h_out, packed.at[:, depth:], sems.at[5]))
-    copies[-1].start()
-    for copy in copies:
-        copy.wait()
-
-
-def first_sent(split, frozen, maps, g, h):
-    half, depth = frozen.shape[0] // split, frozen.shape[1]
-    rows = g.shape[0]
-    part = (half, depth + split * maps.shape[1])
-    packed = (rows, depth + HIDDEN_COPIES * ADAPTER_RANK)
-    return pl.pallas_call(
-        functools.partial(first_kernel, split),
-        out_shape=(jax.ShapeDtypeStruct(part, BF16), jax.ShapeDtypeStruct(packed, BF16)),
-        in_specs=[HBM] * 4,
-        out_specs=[ANY, ANY],
-        scratch_shapes=[
-            pltpu.VMEM(h.shape, BF16),
-            pltpu.VMEM((rows, HIDDEN_COPIES * ADAPTER_RANK), BF16),
-            pltpu.SemaphoreType.DMA((6,)),
-        ],
-        compiler_params=params(8 << 20),
-        cost_estimate=cost(1),
-        name="first_sent",
-    )(frozen, maps, g, h)
+def hidden_kernel(h, after, out):
+    del after
+    out[...] = jnp.concatenate([h[...].T] * HIDDEN_COPIES, axis=1)
+
+
+def hidden_pair(h, after):
+    return pl.pallas_call(
+        hidden_kernel,
+        out_shape=jax.ShapeDtypeStruct((h.shape[1], HIDDEN_COPIES * h.shape[0]), BF16),
+        in_specs=[VMEM, ANY],
+        out_specs=VMEM,
+        compiler_params=params(2 << 20),
+        cost_estimate=cost(0.1),
+        name="hidden_pair",
+    )(h, after)
 
 
 def hold_kernel(*refs):
     del refs
 
 
-def hold(x, *after):
+def hold(x, *after, microseconds=0):
     return pl.pallas_call(
         hold_kernel,
         out_shape=jax.ShapeDtypeStruct(x.shape, x.dtype),
@@ -121,7 +97,7 @@
         out_specs=ANY,
         input_output_aliases={0: 0},
         compiler_params=params(1 << 20),
-        cost_estimate=cost(0),
+        cost_estimate=cost(microseconds),
         name="hold",
     )(x, *after)
 
@@ -182,7 +158,7 @@
 
 
 def spread_kernel(members, b, *refs):
-    gs, spread, up = refs[:INNER], refs[INNER], refs[INNER + 1]
+    gs, spread, up = refs[:INNER], refs[-2], refs[-1]
     width, depth = b.shape
     rows = gs[0].shape[0]
     planes, piece, per = up.shape
@@ -206,7 +182,7 @@
         up[t] = total[row : row + piece, col : col + per]
 
 
-def spread_rows(members, b, gs, per, planes):
+def spread_rows(members, b, gs, per, planes, after):
     rows, (width, depth) = gs[0].shape[0], b.shape
     return pl.pallas_call(
         spread_kernel,
@@ -214,12 +190,12 @@
             jax.ShapeDtypeStruct((INNER, rows, width), BF16),
             jax.ShapeDtypeStruct((planes, width * depth // (INNER * planes * per), per), BF16),
         ),
-        in_specs=[SMEM] + [VMEM] * (1 + INNER),
+        in_specs=[SMEM] + [VMEM] * (1 + INNER) + [ANY] * len(after),
         out_specs=[VMEM, VMEM],
         compiler_params=params(8 << 20),
         cost_estimate=cost(COST_SPREAD),
         name="spread_rows",
-    )(members, b, *gs)
+    )(members, b, *gs, *after)
 
 
 def on_choice(turn, options, act):
@@ -309,7 +285,7 @@
     on_choice(turn, options, fetch)
 
 
-def choose(turn, options, parts, depth, after):
+def choose(turn, options, parts, depth, after, microseconds):
     half = parts[0].shape[0]
     return pl.pallas_call(
         functools.partial(choose_kernel, turn, options),
@@ -318,7 +294,7 @@
         out_specs=VMEM,
         scratch_shapes=[pltpu.SemaphoreType.DMA],
         compiler_params=params(4 << 20),
-        cost_estimate=cost(1),
+        cost_estimate=cost(microseconds),
         name="choose",
     )(*parts, *after)
 
@@ -459,8 +435,8 @@
     )(*came, keep, got, up, *after)
 
 
-def quarter_kernel(*refs):
-    pieces, out = refs[:-1], refs[-1]
+def quarter_kernel(n_after, *refs):
+    pieces, out = refs[: -1 - n_after], refs[-1]
     planes = len(pieces)
     rows, per = pieces[0].shape
     across = out.shape[1] // per
@@ -472,20 +448,36 @@
         out[row, col] = piece[...]
 
 
-def quarter(pieces, shape):
-    return pl.pallas_call(
-        quarter_kernel,
+def quarter(pieces, shape, after):
+    return pl.pallas_call(
+        functools.partial(quarter_kernel, len(after)),
         out_shape=jax.ShapeDtypeStruct(shape, BF16),
-        in_specs=[VMEM] * len(pieces),
+        in_specs=[VMEM] * len(pieces) + [ANY] * len(after),
         out_specs=VMEM,
         compiler_params=params(2 << 20),
         cost_estimate=cost(1),
         name="quarter",
-    )(*pieces)
-
-
-def finish_kernel(kept, other, q0, q1, q2, q3, down, up):
-    down[...] = (kept[...] + other[...].astype(F32)).T
+    )(*pieces, *after)
+
+
+def finish_down_kernel(kept, other, *refs):
+    refs[-1][...] = (kept[...] + other[...].astype(F32)).T
+
+
+def finish_down(kept, other, after):
+    return pl.pallas_call(
+        finish_down_kernel,
+        out_shape=jax.ShapeDtypeStruct(kept.shape[::-1], F32),
+        in_specs=[VMEM] * 2 + [ANY] * len(after),
+        out_specs=VMEM,
+        compiler_params=params(4 << 20),
+        cost_estimate=cost(COST_DOWN_END),
+        name="finish_down",
+    )(kept, other, *after)
+
+
+def finish_up_kernel(q0, q1, q2, q3, after, up):
+    del after
     rows, cols = q0.shape
     _, q = where_am_i()
     for j, part in enumerate((q0, q1, q2, q3)):
@@ -494,20 +486,17 @@
         up[row, col] = part[...].astype(F32)
 
 
-def finish(kept, other, quarters):
+def finish_up(quarters, after):
     rows, cols = quarters[0].shape
     return pl.pallas_call(
-        finish_kernel,
-        out_shape=(
-            jax.ShapeDtypeStruct(kept.shape[::-1], F32),
-            jax.ShapeDtypeStruct((2 * rows, 2 * cols), F32),
-        ),
-        in_specs=[VMEM] * 6,
-        out_specs=[VMEM] * 2,
-        compiler_params=params(6 << 20),
+        finish_up_kernel,
+        out_shape=jax.ShapeDtypeStruct((2 * rows, 2 * cols), F32),
+        in_specs=[VMEM] * 4 + [ANY],
+        out_specs=VMEM,
+        compiler_params=params(4 << 20),
         cost_estimate=cost(1),
-        name="finish",
-    )(kept, other, *quarters)
+        name="finish_up",
+    )(*quarters, *after)
 
 
 def source(turn, z, planes):
@@ -576,7 +565,7 @@
 
     came = {}
 
-    def add_on(k, after):
+    def add_on(k, keep, got, up, after):
         links = [l for l in (0, 1) if edges(k, l, planes)]
         got_before = [came[k + 1, 1 - l] for l in links if (k + 1, 1 - l) in came]
         flags = [(l, (k + 1, 1 - l) in came) for l in links]
@@ -588,7 +577,8 @@
     at = lax.axis_index("groups") % split * unit
     maps = [down_maps[i * unit : (i + 1) * unit] for i in range(split)]
     part = jnp.concatenate([lax.dynamic_slice_in_dim(frozen, at, unit), *maps], axis=1)
-    packed = jnp.concatenate([output_gradient] + [hidden] * HIDDEN_COPIES, axis=1)
+    hidden = hidden_pair(hidden.T, part)
+    packed = jnp.concatenate([output_gradient, hidden], axis=1)
     held[0, 0] = held[0, 1] = part
     g2 = inner(packed, 2)
     pass_on(1)
@@ -598,7 +588,6 @@
     g2 = hold(g2, send)
     g3 = inner(g2, 1)
     gs = [packed, g1, g2, g3]
-    spread, up = spread_rows(members, up_maps, gs, per, planes)
 
     out_shape = jax.ShapeDtypeStruct(tokens.shape, BF16)
 
@@ -615,7 +604,7 @@
         options = sorted({source(turn, p, planes) for p in range(planes)})
         return options, [held[o] for o in options]
 
-    def multiply(k, after):
+    def multiply(k, spread, after):
         sources, plan = [], []
 
         def add(x):
@@ -641,10 +630,9 @@
         pieces[k] = blocks[0], inner(blocks[1], 1), inner(blocks[2], 2)
         return blocks[0]
 
-    def hand_on(k, after):
+    def hand_on(k, *after, microseconds=0):
         own, core, across = pieces[k]
-        if after is not None:
-            across = hold(across, after)
+        across = hold(across, *after, microseconds=microseconds)
         pieces[k] = own, core, across, inner(across[rows:], 1)
         return across
 
@@ -654,33 +642,39 @@
         waits = [held[k, l] for l in (0, 1) if (k, l) in held]
         waits += [theirs[k - 1]] if k - 1 in theirs else []
         waits += [came[planes - k + 1, l] for l in (0, 1) if (planes - k + 1, l) in came]
-        mine[k] = choose(k, options, parts, depth, waits + [last, token])
+        price = COST_CHOOSE if k == 1 else 1
+        mine[k] = choose(k, options, parts, depth, waits + [last, token], price)
         pass_on(k + 1)
         if split > 1:
             theirs[k] = twin(mine[k])
-        summed = add_on(planes - k, [mine[k]])
+        if k == 1:
+            spread, up = spread_rows(members, up_maps, gs, per, planes, [mine[1]])
+        summed = add_on(planes - k, keep, got, up, [mine[k]])
         across = hand_on(k - 1, summed) if k > 1 else summed
-        last = multiply(k, [across])
+        last = multiply(k, spread, [across])
         if k > 1:
             result, token = place(plans[k - 1], pieces[k - 1], result, out_shape, [last])
+    if planes - 1 in theirs:
+        theirs[planes - 1] = last = hold(theirs[planes - 1], last, microseconds=COST_TWIN)
     if planes > 1:
-        last = hand_on(planes - 1, last)
-    last = multiply(planes, [last])
-    if planes > 1:
-        result, token = place(plans[planes - 1], pieces[planes - 1], result, out_shape, [last])
+        last = hand_on(planes - 1, last, token)
     came_last = [came[1, l] for l in (0, 1) if (1, l) in came]
-    down_send, down_kept, piece = totals(came_last, keep, got, up, [])
+    last = multiply(planes, spread, [last])
+    down_send, down_kept, piece = totals(came_last, keep, got, up, [last])
     other = inner(down_send, 2)
     moved = [
         along(piece, [(s, (s + k) % planes) for s in range(planes)]) for k in range(1, planes)
     ]
-    mine_up = quarter([piece, *moved], (width // 2, depth // 2))
+    if planes > 1:
+        result, token = place(plans[planes - 1], pieces[planes - 1], result, out_shape, [last])
+    mine_up = quarter([piece, *moved], (width // 2, depth // 2), [token])
     over_y = inner(mine_up, 2)
+    down_grad = finish_down(down_kept, other, [mine_up])
     quarters = [mine_up, inner(mine_up, 1), over_y, inner(over_y, 1)]
     if planes in plans:
-        hand_on(planes, None)
+        hand_on(planes, microseconds=COST_HAND)
         result, token = place(plans[planes], pieces[planes], result, out_shape, [], COST_LAST)
-    down_grad, up_grad = finish(down_kept, other, quarters)
+    up_grad = finish_up(quarters, [token])
     return result, down_grad, up_grad
 
 

time: 120 us -> 114 us (0.950)
  waiting for transfers between devices: 43.8 us -> 38.5 us
  starting transfers between devices: 44.3 us -> 46.6 us
  local copies, waits for them, and re-layouts: 5.55 us -> 3.81 us
    ppermute x20, waiting for transfers between devices: 27.7 us -> 17.2 us  [inner(): return lax.ppermute(x, 'dp', [(i, i ^ bit) for i in range(n)])]
    ppermute x3, waiting for transfers between devices: 13.6 us -> 18.8 us  [twin(): return lax.ppermute(x, 'groups', [(i, i ^ 1) for i in range(groups)])]
    pallas_call x4, Pallas kernels: 5.88 us -> 4.15 us  [place(): pl.pallas_call(functools.partial(place_kernel, plan), out_shape=(shape, j...]
    unnamed x13 -> x14, local copies, waits for them, and re-layouts: 3.13 us -> 1.44 us
    concatenate x1 -> x0, local copies, waits for them, and re-layouts: 1.26 us -> none  [local(): jnp.concatenate([output_gradient] + [hidden] * HIDDEN_COPIES, axis=1)]
  transfers between devices with their start and end apart: 36 -> 36, of which waited for: 11 -> 13; matrix products, arithmetic and copies ran while one was open for 1% -> 0% of each run, Pallas kernels for 19% -> 20%
where the time goes in v3:
time: 114 us
  starting transfers between devices  46.6 us (41%)
  waiting for transfers between devices  38.5 us (34%)
  Pallas kernels  23.6 us (21%)
  local copies, waits for them, and re-layouts  3.81 us (3%)
    ppermute x13, starting transfers between devices, along(): lax.ppermute(x, 'dp', [(s * INNER + i, t * INNER + i) for s, t in pairs f...  28.9 us
    ppermute x3, waiting for transfers between devices, twin(): return lax.ppermute(x, 'groups', [(i, i ^ 1) for i in range(groups)])  18.8 us
    ppermute x20, waiting for transfers between devices, inner(): return lax.ppermute(x, 'dp', [(i, i ^ bit) for i in range(n)])  17.2 us
    ppermute x20, starting transfers between devices, inner(): return lax.ppermute(x, 'dp', [(i, i ^ bit) for i in range(n)])  13 us
    pallas_call x4, Pallas kernels, product(): pl.pallas_call(functools.partial(product_kernel, plan, len(sources)), out...  7.05 us
    pallas_call x1, Pallas kernels, down_partials(): pl.pallas_call(down_kernel, out_shape=(shape, shape), in_specs=[SMEM] + [...  5.9 us
    ppermute x3, starting transfers between devices, twin(): return lax.ppermute(x, 'groups', [(i, i ^ 1) for i in range(groups)])  4.66 us
    pallas_call x4, Pallas kernels, place(): pl.pallas_call(functools.partial(place_kernel, plan), out_shape=(shape, j...  4.15 us
  transfers between devices with their start and end apart: 36, of which 13 were waited for; matrix products, arithmetic and copies ran while one was open for 0% of the time, Pallas kernels for 20%

profile of v3, /device:TPU:0, one launch (start us, length us, event | category | flops | bytes accessed | tf_op | source)
XLA Modules:
  0.0 113.8 jit_solution(14062124466873427818)
XLA Ops:
  0.7 1.1 fusion
  1.8 1.2 %constant_dynamic-slice_fusion = bf16[256,1024]{1,0:T(8,128)(2,1)S(1)} fusion(bf16[512,1024]{1,0:T(8,128)(2,1)} %refs_5_.1, s32[]{:T(128)S(6)} %select_n.11), kind=kLoop, calls=%fused_computation.2 | loop fusion | bytes 1048580 | tf_op jit(solution)/shard_map/dynamic_slice | solution.py:579
  3.0 0.8 collective-permute-start.4
  3.9 5.9 %collective-permute-start.3 = (bf16[256,1536]{1,0:T(8,128)(2,1)S(1)}, bf16[256,1536]{1,0:T(8,128)(2,1)S(1)}, u32[]{:S(2)}, u32[]{:S(2)}) collective-permute-start(bf16[256,1536]{1,0:T(8,128)(2,1)S(1)} %pad_maximum_fusion.after), channel_id=1, source_target_pairs={{0,4},{1,5},{2,6},{3,7},{4,0},{5,1},{6,2},{7,3},{8,12},{9,13},{10,... | collective-permute-start | bytes 2359304 | tf_op jit(solution)/shard_map/ppermute | solution.py:548
  9.8 0.8 copy-done.5
  10.5 0.1 hidden_pair.1
  10.7 0.1 collective-permute-start
  10.8 1.6 %collective-permute-start.1 = (bf16[256,1152]{1,0:T(8,128)(2,1)S(1)}, bf16[256,1152]{1,0:T(8,128)(2,1)S(1)}, u32[]{:S(2)}, u32[]{:S(2)}) collective-permute-start(bf16[256,1152]{1,0:T(8,128)(2,1)S(1)} %pad_maximum_fusion.1.refs_0_.refs_1_), channel_id=1, source_target_pairs={{0,2},{1,3},{2,0},{3,1},{4,6},{5,7},{6,4},{7,5},{8,10},{9,11},{10,... | collective-permute-start | bytes 1769480 | tf_op jit(solution)/shard_map/ppermute | solution.py:545
  12.4 0.4 collective-permute-done.after.refs_1_.refs_2_
  12.8 0.7 copy-done.6
  13.5 5.9 %down_partials.1 = (bf16[8,256,512]{2,1,0:T(8,128)(2,1)S(1)}, bf16[8,256,512]{2,1,0:T(8,128)(2,1)S(1)}) custom-call(s32[32]{0:T(128)S(1)} %copy-done.6, bf16[256,1024]{1,0:T(8,128)(2,1)S(1)} %copy-done.1, bf16[256,1024]{1,0:T(8,128)(2,1)S(1)} %copy-done.2, bf16[256,8192]{1,0:T(8,128)(2,1)S(1)} %copy-done, ...), custom_call_target="tpu_custom_call" | custom-call | flops 1100000000 | bytes 3300000 | tf_op jit(solution)/shard_map/down_partials/pallas_call | solution.py:141
  19.4 0.2 collective-permute-start.8
  19.6 7.0 %collective-permute-done.1.refs_0_ = bf16[256,1152]{1,0:T(8,128)(2,1)S(1)} collective-permute-done((bf16[256,1152]{1,0:T(8,128)(2,1)S(1)}, bf16[256,1152]{1,0:T(8,128)(2,1)S(1)}, u32[]{:S(2)}, u32[]{:S(2)}) %collective-permute-start.1) | collective-permute-done | bytes 589856 | tf_op jit(solution)/shard_map/ppermute | solution.py:545
  26.6 0.5 collective-permute-done.3.refs_0_.refs_1_
  27.1 0.7 collective-permute-start.5
  27.8 1.3 %collective-permute-start.6 = (bf16[256,1536]{1,0:T(8,128)(2,1)S(1)}, bf16[256,1536]{1,0:T(8,128)(2,1)S(1)}, u32[]{:S(2)}, u32[]{:S(2)}) collective-permute-start(bf16[256,1536]{1,0:T(8,128)(2,1)S(1)} %hold.13.refs_0_.refs_7_.refs_5_), channel_id=1, source_target_pairs={{4,0},{5,1},{6,2},{7,3},{8,12},{9,13},{10,14},{11,15},{20,16},{21,... | collective-permute-start | bytes 2359304 | tf_op jit(solution)/shard_map/ppermute | solution.py:548
  29.1 1.5 %spread_rows.1 = (bf16[4,256,256]{2,1,0:T(8,128)(2,1)S(1)}, bf16[4,32,512]{2,1,0:T(8,128)(2,1)S(1)}) custom-call(s32[32]{0:T(128)S(1)} %copy-done.6, bf16[256,1024]{1,0:T(8,128)(2,1)S(1)} %copy-done.2, bf16[256,1152]{1,0:T(8,128)(2,1)S(1)} %pad_maximum_fusion.1.refs_0_.refs_1_, bf16[256,1152]{1,0:T(8,128)(2,1)S(1)} %collective-permute-done.after.refs_1_.refs_2_, ...), custom_call_target="tpu_custom_call" | custom-call | flops 2200000000 | bytes 6600000 | tf_op jit(solution)/shard_map/spread_rows/pallas_call | solution.py:187
  30.6 0.3 running_sums.3.refs_9_
  31.0 5.5 %collective-permute-start.9 = (bf16[544,512]{1,0:T(8,128)(2,1)S(1)}, bf16[544,512]{1,0:T(8,128)(2,1)S(1)}, u32[]{:S(2)}, u32[]{:S(2)}) collective-permute-start(bf16[544,512]{1,0:T(8,128)(2,1)S(1)} %running_sums.3.refs_9_), channel_id=1, source_target_pairs={{0,4},{1,5},{2,6},{3,7},{12,8},{13,9},{14,10},{15,11},{16,20},{17,... | collective-permute-start | bytes 1671176 | tf_op jit(solution)/shard_map/ppermute | solution.py:548
  36.5 1.6 %collective-permute-start.7 = (bf16[256,1024]{1,0:T(8,128)(2,1)S(1)}, bf16[256,1024]{1,0:T(8,128)(2,1)S(1)}, u32[]{:S(2)}, u32[]{:S(2)}) collective-permute-start(bf16[256,1024]{1,0:T(8,128)(2,1)S(1)} %choose.3.refs_4_.refs_1_.refs_3_.refs_8_), channel_id=1, source_target_pairs={{0,16},{16,0},{1,17},{17,1},{2,18},{18,2},{3,19},{19,3},{4,20},{20... | collective-permute-start | bytes 1572872 | tf_op jit(solution)/shard_map/ppermute | solution.py:553
  38.0 2.6 %product.4 = (bf16[256,768]{1,0:T(8,128)(2,1)S(1)}, bf16[256,768]{1,0:T(8,128)(2,1)S(1)}, bf16[512,768]{1,0:T(8,128)(2,1)S(1)}) custom-call(bf16[4,256,256]{2,1,0:T(8,128)(2,1)S(1)} %get-tuple-element.35.refs_0_, bf16[256,1152]{1,0:T(8,128)(2,1)S(1)} %pad_maximum_fusion.1.refs_0_.refs_1_, bf16[256,1152]{1,0:T(8,128)(2,1)S(1)} %collective-permute-done.after.refs_1_.refs_2_, ...), custom_call_target="tpu_custom_call" | custom-call | flops 3300000000 | bytes 9900000 | tf_op jit(solution)/shard_map/product/pallas_call | solution.py:262
  40.7 1.6 %collective-permute-start.14 = (bf16[512,768]{1,0:T(8,128)(2,1)S(1)}, bf16[512,768]{1,0:T(8,128)(2,1)S(1)}, u32[]{:S(2)}, u32[]{:S(2)}) collective-permute-start(bf16[512,768]{1,0:T(8,128)(2,1)S(1)} %get-tuple-element.41), channel_id=1, source_target_pairs={{0,2},{1,3},{2,0},{3,1},{4,6},{5,7},{6,4},{7,5},{8,10},{9,11},{10,... | collective-permute-start | bytes 2359304 | tf_op jit(solution)/shard_map/ppermute | solution.py:545
  42.3 6.8 %collective-permute-done.7.refs_4_.refs_6_ = bf16[256,1024]{1,0:T(8,128)(2,1)S(1)} collective-permute-done((bf16[256,1024]{1,0:T(8,128)(2,1)S(1)}, bf16[256,1024]{1,0:T(8,128)(2,1)S(1)}, u32[]{:S(2)}, u32[]{:S(2)}) %collective-permute-start.7) | collective-permute-done | bytes 524320 | tf_op jit(solution)/shard_map/ppermute | solution.py:553
  49.1 0.1 collective-permute-done.6.refs_1_.refs_2_.refs_0_
  49.3 1.3 %collective-permute-start.10 = (bf16[256,1536]{1,0:T(8,128)(2,1)S(1)}, bf16[256,1536]{1,0:T(8,128)(2,1)S(1)}, u32[]{:S(2)}, u32[]{:S(2)}) collective-permute-start(bf16[256,1536]{1,0:T(8,128)(2,1)S(1)} %hold.14.refs_0_.refs_8_.refs_5_), channel_id=1, source_target_pairs={{4,0},{5,1},{6,2},{7,3},{8,12},{9,13},{10,14},{11,15},{20,16},{21,... | collective-permute-start | bytes 2359304 | tf_op jit(solution)/shard_map/ppermute | solution.py:548
  50.6 0.8 running_sums.4
  51.4 0.7 collective-permute-start.13
  52.1 6.8 %collective-permute-start.12 = (bf16[544,512]{1,0:T(8,128)(2,1)S(1)}, bf16[544,512]{1,0:T(8,128)(2,1)S(1)}, u32[]{:S(2)}, u32[]{:S(2)}) collective-permute-start(bf16[544,512]{1,0:T(8,128)(2,1)S(1)} %get-tuple-element.39.refs_1_), channel_id=1, source_target_pairs={{0,4},{1,5},{2,6},{3,7},{12,8},{13,9},{14,10},{15,11},{16,20},{17,... | collective-permute-start | bytes 1671176 | tf_op jit(solution)/shard_map/ppermute | solution.py:548
  58.9 1.6 %collective-permute-start.11 = (bf16[256,1024]{1,0:T(8,128)(2,1)S(1)}, bf16[256,1024]{1,0:T(8,128)(2,1)S(1)}, u32[]{:S(2)}, u32[]{:S(2)}) collective-permute-start(bf16[256,1024]{1,0:T(8,128)(2,1)S(1)} %choose.4.refs_1_.refs_4_.refs_9_), channel_id=1, source_target_pairs={{0,16},{16,0},{1,17},{17,1},{2,18},{18,2},{3,19},{19,3},{4,20},{20... | collective-permute-start | bytes 1572872 | tf_op jit(solution)/shard_map/ppermute | solution.py:553
  60.5 1.6 %product.5 = (bf16[256,512]{1,0:T(8,128)(2,1)S(1)}, bf16[256,512]{1,0:T(8,128)(2,1)S(1)}, bf16[512,512]{1,0:T(8,128)(2,1)S(1)}) custom-call(bf16[4,256,256]{2,1,0:T(8,128)(2,1)S(1)} %get-tuple-element.35.refs_0_, bf16[256,1152]{1,0:T(8,128)(2,1)S(1)} %pad_maximum_fusion.1.refs_0_.refs_1_, bf16[256,1152]{1,0:T(8,128)(2,1)S(1)} %collective-permute-done.after.refs_1_.refs_2_, ...), custom_call_target="tpu_custom_call" | custom-call | flops 3300000000 | bytes 9900000 | tf_op jit(solution)/shard_map/product/pallas_call | solution.py:262
  62.2 1.6 %collective-permute-start.18 = (bf16[512,512]{1,0:T(8,128)(2,1)S(1)}, bf16[512,512]{1,0:T(8,128)(2,1)S(1)}, u32[]{:S(2)}, u32[]{:S(2)}) collective-permute-start(bf16[512,512]{1,0:T(8,128)(2,1)S(1)} %get-tuple-element.45), channel_id=1, source_target_pairs={{0,2},{1,3},{2,0},{3,1},{4,6},{5,7},{6,4},{7,5},{8,10},{9,11},{10,... | collective-permute-start | bytes 1572872 | tf_op jit(solution)/shard_map/ppermute | solution.py:545
  63.8 1.2 %place.4 = (bf16[256,8192]{1,0:T(8,128)(2,1)}, f32[8,128]{1,0:T(8,128)S(1)}) custom-call(bf16[256,768]{1,0:T(8,128)(2,1)S(1)} %get-tuple-element.38.refs_6_.own, bf16[256,768]{1,0:T(8,128)(2,1)S(1)} %collective-permute-done.15.core, bf16[512,768]{1,0:T(8,128)(2,1)S(1)} %hold.16.refs_10_.across, bf16[256,768]{1,0:T(8,128)(2,1)S(1)} %collective-permute-done.16.both, ...), custom_call_target="tpu_custom_call" | custom-call | flops 1100000000 | bytes 3300000 | tf_op jit(solution)/shard_map/place/pallas_call | solution.py:323
  65.0 7.3 %collective-permute-done.11.refs_3_.refs_7_ = bf16[256,1024]{1,0:T(8,128)(2,1)S(1)} collective-permute-done((bf16[256,1024]{1,0:T(8,128)(2,1)S(1)}, bf16[256,1024]{1,0:T(8,128)(2,1)S(1)}, u32[]{:S(2)}, u32[]{:S(2)}) %collective-permute-start.11) | collective-permute-done | bytes 524320 | tf_op jit(solution)/shard_map/ppermute | solution.py:553
  72.4 0.1 choose.5.refs_1_.refs_5_.refs_10_
  72.5 1.5 %collective-permute-start.17 = (bf16[256,1024]{1,0:T(8,128)(2,1)S(1)}, bf16[256,1024]{1,0:T(8,128)(2,1)S(1)}, u32[]{:S(2)}, u32[]{:S(2)}) collective-permute-start(bf16[256,1024]{1,0:T(8,128)(2,1)S(1)} %choose.5.refs_1_.refs_5_.refs_10_), channel_id=1, source_target_pairs={{0,16},{16,0},{1,17},{17,1},{2,18},{18,2},{3,19},{19,3},{4,20},{20... | collective-permute-start | bytes 1572872 | tf_op jit(solution)/shard_map/ppermute | solution.py:553
  74.0 0.9 running_sums.5
  74.9 0.9 collective-permute-start.27
  75.8 0.7 collective-permute-done.18.refs_0_
  76.7 1.8 %product.6 = (bf16[256,512]{1,0:T(8,128)(2,1)S(1)}, bf16[256,512]{1,0:T(8,128)(2,1)S(1)}, bf16[512,512]{1,0:T(8,128)(2,1)S(1)}) custom-call(bf16[4,256,256]{2,1,0:T(8,128)(2,1)S(1)} %get-tuple-element.35.refs_0_, bf16[256,1152]{1,0:T(8,128)(2,1)S(1)} %pad_maximum_fusion.1.refs_0_.refs_1_, bf16[256,1152]{1,0:T(8,128)(2,1)S(1)} %collective-permute-done.after.refs_1_.refs_2_, ...), custom_call_target="tpu_custom_call" | custom-call | flops 3300000000 | bytes 9900000 | tf_op jit(solution)/shard_map/product/pallas_call | solution.py:262
  78.5 0.5 collective-permute-start.25
  79.0 1.5 %collective-permute-start.19 = (bf16[512,512]{1,0:T(8,128)(2,1)S(1)}, bf16[512,512]{1,0:T(8,128)(2,1)S(1)}, u32[]{:S(2)}, u32[]{:S(2)}) collective-permute-start(bf16[512,512]{1,0:T(8,128)(2,1)S(1)} %get-tuple-element.48), channel_id=1, source_target_pairs={{0,2},{1,3},{2,0},{3,1},{4,6},{5,7},{6,4},{7,5},{8,10},{9,11},{10,... | collective-permute-start | bytes 1572872 | tf_op jit(solution)/shard_map/ppermute | solution.py:545
  80.6 0.7 collective-permute-start.28
  81.2 1.1 place.5
  82.3 4.6 %collective-permute-done.17.refs_0_ = bf16[256,1024]{1,0:T(8,128)(2,1)S(1)} collective-permute-done((bf16[256,1024]{1,0:T(8,128)(2,1)S(1)}, bf16[256,1024]{1,0:T(8,128)(2,1)S(1)}, u32[]{:S(2)}, u32[]{:S(2)}) %collective-permute-start.17) | collective-permute-done | bytes 524320 | tf_op jit(solution)/shard_map/ppermute | solution.py:553
  86.9 6.1 %collective-permute-done.19.refs_0_ = bf16[512,512]{1,0:T(8,128)(2,1)S(1)} collective-permute-done((bf16[512,512]{1,0:T(8,128)(2,1)S(1)}, bf16[512,512]{1,0:T(8,128)(2,1)S(1)}, u32[]{:S(2)}, u32[]{:S(2)}) %collective-permute-start.19) | collective-permute-done | bytes 524320 | tf_op jit(solution)/shard_map/ppermute | solution.py:545
  93.0 0.9 product.7
  93.9 0.1 collective-permute-start.22
  94.0 0.5 collective-permute-start.26
  94.5 1.5 %collective-permute-start.23 = (bf16[512,256]{1,0:T(8,128)(2,1)S(1)}, bf16[512,256]{1,0:T(8,128)(2,1)S(1)}, u32[]{:S(2)}, u32[]{:S(2)}) collective-permute-start(bf16[512,256]{1,0:T(8,128)(2,1)S(1)} %get-tuple-element.54), channel_id=1, source_target_pairs={{0,2},{1,3},{2,0},{3,1},{4,6},{5,7},{6,4},{7,5},{8,10},{9,11},{10,... | collective-permute-start | bytes 786440 | tf_op jit(solution)/shard_map/ppermute | solution.py:545
  96.0 0.6 totals.1
  96.7 2.1 %collective-permute-start.32 = (bf16[32,512]{1,0:T(8,128)(2,1)S(1)}, bf16[32,512]{1,0:T(8,128)(2,1)S(1)}, u32[]{:S(2)}, u32[]{:S(2)}) collective-permute-start(bf16[32,512]{1,0:T(8,128)(2,1)S(1)} %get-tuple-element.62.refs_0_), channel_id=1, source_target_pairs={{0,12},{1,13},{2,14},{3,15},{4,0},{5,1},{6,2},{7,3},{8,4},{9,5},{1... | collective-permute-start | bytes 98312 | tf_op jit(solution)/shard_map/ppermute | solution.py:548
  98.7 1.2 %collective-permute-start.31 = (bf16[32,512]{1,0:T(8,128)(2,1)S(1)}, bf16[32,512]{1,0:T(8,128)(2,1)S(1)}, u32[]{:S(2)}, u32[]{:S(2)}) collective-permute-start(bf16[32,512]{1,0:T(8,128)(2,1)S(1)} %get-tuple-element.62.refs_0_), channel_id=1, source_target_pairs={{0,8},{1,9},{2,10},{3,11},{4,12},{5,13},{6,14},{7,15},{8,0},{9,1},... | collective-permute-start | bytes 98312 | tf_op jit(solution)/shard_map/ppermute | solution.py:548
  99.9 1.1 collective-permute-start.30
  101.1 1.0 place.6
  102.1 1.6 %collective-permute-start.29 = (bf16[256,512]{1,0:T(8,128)(2,1)S(1)}, bf16[256,512]{1,0:T(8,128)(2,1)S(1)}, u32[]{:S(2)}, u32[]{:S(2)}) collective-permute-start(bf16[256,512]{1,0:T(8,128)(2,1)S(1)} %get-tuple-element.61), channel_id=1, source_target_pairs={{0,2},{1,3},{2,0},{3,1},{4,6},{5,7},{6,4},{7,5},{8,10},{9,11},{10,... | collective-permute-start | bytes 786440 | tf_op jit(solution)/shard_map/ppermute | solution.py:545
  103.7 1.9 %collective-permute-done.30.refs_1_ = bf16[32,512]{1,0:T(8,128)(2,1)S(1)} collective-permute-done((bf16[32,512]{1,0:T(8,128)(2,1)S(1)}, bf16[32,512]{1,0:T(8,128)(2,1)S(1)}, u32[]{:S(2)}, u32[]{:S(2)}) %collective-permute-start.30) | collective-permute-done | bytes 32800 | tf_op jit(solution)/shard_map/ppermute | solution.py:548
  105.7 1.6 %collective-permute-start.34 = (bf16[128,512]{1,0:T(8,128)(2,1)S(1)}, bf16[128,512]{1,0:T(8,128)(2,1)S(1)}, u32[]{:S(2)}, u32[]{:S(2)}) collective-permute-start(bf16[128,512]{1,0:T(8,128)(2,1)S(1)} %quarter.1.refs_0_.q0), channel_id=1, source_target_pairs={{0,2},{1,3},{2,0},{3,1},{4,6},{5,7},{6,4},{7,5},{8,10},{9,11},{10,... | collective-permute-start | bytes 393224 | tf_op jit(solution)/shard_map/ppermute | solution.py:545
  107.3 0.6 collective-permute-start.24
  107.9 2.1 %collective-permute-done.29.other = bf16[256,512]{1,0:T(8,128)(2,1)S(1)} collective-permute-done((bf16[256,512]{1,0:T(8,128)(2,1)S(1)}, bf16[256,512]{1,0:T(8,128)(2,1)S(1)}, u32[]{:S(2)}, u32[]{:S(2)}) %collective-permute-start.29) | collective-permute-done | bytes 262176 | tf_op jit(solution)/shard_map/ppermute | solution.py:545
  109.9 1.0 finish_down.1
  110.9 0.4 collective-permute-done.34.q2
  111.4 0.8 place.7
  112.2 0.5 collective-permute-done.35.q3
  112.7 1.1 finish_up.1
  (62 shorter events, 0.6 us)
Async XLA Ops:
  0.6 10.0 %copy-start.1 = (bf16[256,1024]{1,0:T(8,128)(2,1)S(1)}, bf16[256,1024]{1,0:T(8,128)(2,1)}, u32[]{:S(2)}) copy-start(bf16[256,1024]{1,0:T(8,128)(2,1)} %g.1) | copy-start | bytes 1572868
  0.7 12.1 %copy-start.2 = (bf16[256,1024]{1,0:T(8,128)(2,1)S(1)}, bf16[256,1024]{1,0:T(8,128)(2,1)}, u32[]{:S(2)}) copy-start(bf16[256,1024]{1,0:T(8,128)(2,1)} %b.3) | copy-start | bytes 1572868
  1.7 11.1 %copy-start = (bf16[256,8192]{1,0:T(8,128)(2,1)S(1)}, bf16[256,8192]{1,0:T(8,128)(2,1)}, u32[]{:S(2)}) copy-start(bf16[256,8192]{1,0:T(8,128)(2,1)} %tokens.1) | copy-start | bytes 12582916
  3.0 23.5 %collective-permute-start.4 = (bf16[256,1536]{1,0:T(8,128)(2,1)S(1)}, bf16[256,1536]{1,0:T(8,128)(2,1)S(1)}, u32[]{:S(2)}, u32[]{:S(2)}) collective-permute-start(bf16[256,1536]{1,0:T(8,128)(2,1)S(1)} %pad_maximum_fusion.after), channel_id=1, source_target_pairs={{4,8},{5,9},{6,10},{7,11},{8,4},{9,5},{10,6},{11,7},{20,24},{21,25... | collective-permute-start | bytes 2359304 | tf_op jit(solution)/shard_map/ppermute | solution.py:548
  3.9 23.1 %collective-permute-start.3 = (bf16[256,1536]{1,0:T(8,128)(2,1)S(1)}, bf16[256,1536]{1,0:T(8,128)(2,1)S(1)}, u32[]{:S(2)}, u32[]{:S(2)}) collective-permute-start(bf16[256,1536]{1,0:T(8,128)(2,1)S(1)} %pad_maximum_fusion.after), channel_id=1, source_target_pairs={{0,4},{1,5},{2,6},{3,7},{4,0},{5,1},{6,2},{7,3},{8,12},{9,13},{10,... | collective-permute-start | bytes 2359304 | tf_op jit(solution)/shard_map/ppermute | solution.py:548
  9.8 0.8 copy-start.5
  10.7 2.1 %collective-permute-start = (bf16[256,1152]{1,0:T(8,128)(2,1)S(1)}, bf16[256,1152]{1,0:T(8,128)(2,1)S(1)}, u32[]{:S(2)}, u32[]{:S(2)}) collective-permute-start(bf16[256,1152]{1,0:T(8,128)(2,1)S(1)} %pad_maximum_fusion.1.refs_0_.refs_1_), channel_id=1, source_target_pairs={{0,1},{1,0},{2,3},{3,2},{4,5},{5,4},{6,7},{7,6},{8,9},{9,8},{10,11... | collective-permute-start | bytes 1769480 | tf_op jit(solution)/shard_map/ppermute | solution.py:545
  10.8 15.7 %collective-permute-start.1 = (bf16[256,1152]{1,0:T(8,128)(2,1)S(1)}, bf16[256,1152]{1,0:T(8,128)(2,1)S(1)}, u32[]{:S(2)}, u32[]{:S(2)}) collective-permute-start(bf16[256,1152]{1,0:T(8,128)(2,1)S(1)} %pad_maximum_fusion.1.refs_0_.refs_1_), channel_id=1, source_target_pairs={{0,2},{1,3},{2,0},{3,1},{4,6},{5,7},{6,4},{7,5},{8,10},{9,11},{10,... | collective-permute-start | bytes 1769480 | tf_op jit(solution)/shard_map/ppermute | solution.py:545
  12.8 0.7 copy-start.6
  19.4 11.2 %collective-permute-start.8 = (bf16[8,256,512]{2,1,0:T(8,128)(2,1)S(1)}, bf16[8,256,512]{2,1,0:T(8,128)(2,1)S(1)}, u32[]{:S(2)}, u32[]{:S(2)}) collective-permute-start(bf16[8,256,512]{2,1,0:T(8,128)(2,1)S(1)} %get-tuple-element.34.refs_1_.refs_3_.refs_4_.refs_7_), channel_id=1, source_target_pairs={{0,1},{1,0},{2,3},{3,2},{4,5},{5,4},{6,7},{7,6},{8,9},{9,8},{10,11... | collective-permute-start | bytes 6291464 | tf_op jit(solution)/shard_map/ppermute | solution.py:545
  26.6 2.6 %collective-permute-start.2 = (bf16[256,1152]{1,0:T(8,128)(2,1)S(1)}, bf16[256,1152]{1,0:T(8,128)(2,1)S(1)}, u32[]{:S(2)}, u32[]{:S(2)}) collective-permute-start(bf16[256,1152]{1,0:T(8,128)(2,1)S(1)} %hold.11.refs_2_.refs_3_), channel_id=1, source_target_pairs={{0,1},{1,0},{2,3},{3,2},{4,5},{5,4},{6,7},{7,6},{8,9},{9,8},{10,11... | collective-permute-start | bytes 1769480 | tf_op jit(solution)/shard_map/ppermute | solution.py:545
  27.1 22.0 %collective-permute-start.5 = (bf16[256,1536]{1,0:T(8,128)(2,1)S(1)}, bf16[256,1536]{1,0:T(8,128)(2,1)S(1)}, u32[]{:S(2)}, u32[]{:S(2)}) collective-permute-start(bf16[256,1536]{1,0:T(8,128)(2,1)S(1)} %hold.12.refs_7_.refs_5_), channel_id=1, source_target_pairs={{4,8},{5,9},{6,10},{7,11},{8,4},{9,5},{10,6},{11,7},{20,24},{21,25... | collective-permute-start | bytes 2359304 | tf_op jit(solution)/shard_map/ppermute | solution.py:548
  27.8 21.4 %collective-permute-start.6 = (bf16[256,1536]{1,0:T(8,128)(2,1)S(1)}, bf16[256,1536]{1,0:T(8,128)(2,1)S(1)}, u32[]{:S(2)}, u32[]{:S(2)}) collective-permute-start(bf16[256,1536]{1,0:T(8,128)(2,1)S(1)} %hold.13.refs_0_.refs_7_.refs_5_), channel_id=1, source_target_pairs={{4,0},{5,1},{6,2},{7,3},{8,12},{9,13},{10,14},{11,15},{20,16},{21,... | collective-permute-start | bytes 2359304 | tf_op jit(solution)/shard_map/ppermute | solution.py:548
  30.6 7.4 %copy-start.3 = (bf16[512,256]{1,0:T(8,128)(2,1)S(1)}, bf16[512,256]{1,0:T(8,128)(2,1)}, u32[]{:S(2)}) copy-start(bf16[512,256]{1,0:T(8,128)(2,1)} %refs_6_.1) | copy-start | bytes 786436
  30.6 7.4 %copy-start.4 = (bf16[512,1024]{1,0:T(8,128)(2,1)S(1)}, bf16[512,1024]{1,0:T(8,128)(2,1)}, u32[]{:S(2)}) copy-start(bf16[512,1024]{1,0:T(8,128)(2,1)} %refs_5_.1) | copy-start | bytes 3145732
  31.0 18.2 %collective-permute-start.9 = (bf16[544,512]{1,0:T(8,128)(2,1)S(1)}, bf16[544,512]{1,0:T(8,128)(2,1)S(1)}, u32[]{:S(2)}, u32[]{:S(2)}) collective-permute-start(bf16[544,512]{1,0:T(8,128)(2,1)S(1)} %running_sums.3.refs_9_), channel_id=1, source_target_pairs={{0,4},{1,5},{2,6},{3,7},{12,8},{13,9},{14,10},{15,11},{16,20},{17,... | collective-permute-start | bytes 1671176 | tf_op jit(solution)/shard_map/ppermute | solution.py:548
  36.5 12.6 %collective-permute-start.7 = (bf16[256,1024]{1,0:T(8,128)(2,1)S(1)}, bf16[256,1024]{1,0:T(8,128)(2,1)S(1)}, u32[]{:S(2)}, u32[]{:S(2)}) collective-permute-start(bf16[256,1024]{1,0:T(8,128)(2,1)S(1)} %choose.3.refs_4_.refs_1_.refs_3_.refs_8_), channel_id=1, source_target_pairs={{0,16},{16,0},{1,17},{17,1},{2,18},{18,2},{3,19},{19,3},{4,20},{20... | collective-permute-start | bytes 1572872 | tf_op jit(solution)/shard_map/ppermute | solution.py:553
  40.7 18.2 %collective-permute-start.14 = (bf16[512,768]{1,0:T(8,128)(2,1)S(1)}, bf16[512,768]{1,0:T(8,128)(2,1)S(1)}, u32[]{:S(2)}, u32[]{:S(2)}) collective-permute-start(bf16[512,768]{1,0:T(8,128)(2,1)S(1)} %get-tuple-element.41), channel_id=1, source_target_pairs={{0,2},{1,3},{2,0},{3,1},{4,6},{5,7},{6,4},{7,5},{8,10},{9,11},{10,... | collective-permute-start | bytes 2359304 | tf_op jit(solution)/shard_map/ppermute | solution.py:545
  49.1 11.3 %collective-permute-start.15 = (bf16[256,768]{1,0:T(8,128)(2,1)S(1)}, bf16[256,768]{1,0:T(8,128)(2,1)S(1)}, u32[]{:S(2)}, u32[]{:S(2)}) collective-permute-start(bf16[256,768]{1,0:T(8,128)(2,1)S(1)} %get-tuple-element.43), channel_id=1, source_target_pairs={{0,1},{1,0},{2,3},{3,2},{4,5},{5,4},{6,7},{7,6},{8,9},{9,8},{10,11... | collective-permute-start | bytes 1179656 | tf_op jit(solution)/shard_map/ppermute | solution.py:545
  49.3 23.1 %collective-permute-start.10 = (bf16[256,1536]{1,0:T(8,128)(2,1)S(1)}, bf16[256,1536]{1,0:T(8,128)(2,1)S(1)}, u32[]{:S(2)}, u32[]{:S(2)}) collective-permute-start(bf16[256,1536]{1,0:T(8,128)(2,1)S(1)} %hold.14.refs_0_.refs_8_.refs_5_), channel_id=1, source_target_pairs={{4,0},{5,1},{6,2},{7,3},{8,12},{9,13},{10,14},{11,15},{20,16},{21,... | collective-permute-start | bytes 2359304 | tf_op jit(solution)/shard_map/ppermute | solution.py:548
  51.4 21.0 %collective-permute-start.13 = (bf16[544,512]{1,0:T(8,128)(2,1)S(1)}, bf16[544,512]{1,0:T(8,128)(2,1)S(1)}, u32[]{:S(2)}, u32[]{:S(2)}) collective-permute-start(bf16[544,512]{1,0:T(8,128)(2,1)S(1)} %get-tuple-element.40), channel_id=1, source_target_pairs={{8,4},{9,5},{10,6},{11,7},{4,8},{5,9},{6,10},{7,11},{24,20},{25,21... | collective-permute-start | bytes 1671176 | tf_op jit(solution)/shard_map/ppermute | solution.py:548
  52.1 20.3 %collective-permute-start.12 = (bf16[544,512]{1,0:T(8,128)(2,1)S(1)}, bf16[544,512]{1,0:T(8,128)(2,1)S(1)}, u32[]{:S(2)}, u32[]{:S(2)}) collective-permute-start(bf16[544,512]{1,0:T(8,128)(2,1)S(1)} %get-tuple-element.39.refs_1_), channel_id=1, source_target_pairs={{0,4},{1,5},{2,6},{3,7},{12,8},{13,9},{14,10},{15,11},{16,20},{17,... | collective-permute-start | bytes 1671176 | tf_op jit(solution)/shard_map/ppermute | solution.py:548
  58.9 13.5 %collective-permute-start.11 = (bf16[256,1024]{1,0:T(8,128)(2,1)S(1)}, bf16[256,1024]{1,0:T(8,128)(2,1)S(1)}, u32[]{:S(2)}, u32[]{:S(2)}) collective-permute-start(bf16[256,1024]{1,0:T(8,128)(2,1)S(1)} %choose.4.refs_1_.refs_4_.refs_9_), channel_id=1, source_target_pairs={{0,16},{16,0},{1,17},{17,1},{2,18},{18,2},{3,19},{19,3},{4,20},{20... | collective-permute-start | bytes 1572872 | tf_op jit(solution)/shard_map/ppermute | solution.py:553
  60.5 1.8 %collective-permute-start.16 = (bf16[256,768]{1,0:T(8,128)(2,1)S(1)}, bf16[256,768]{1,0:T(8,128)(2,1)S(1)}, u32[]{:S(2)}, u32[]{:S(2)}) collective-permute-start(bf16[256,768]{1,0:T(8,128)(2,1)S(1)} %slice.24), channel_id=1, source_target_pairs={{0,1},{1,0},{2,3},{3,2},{4,5},{5,4},{6,7},{7,6},{8,9},{9,8},{10,11... | collective-permute-start | bytes 1179656 | tf_op jit(solution)/shard_map/ppermute | solution.py:545
  62.2 14.3 %collective-permute-start.18 = (bf16[512,512]{1,0:T(8,128)(2,1)S(1)}, bf16[512,512]{1,0:T(8,128)(2,1)S(1)}, u32[]{:S(2)}, u32[]{:S(2)}) collective-permute-start(bf16[512,512]{1,0:T(8,128)(2,1)S(1)} %get-tuple-element.45), channel_id=1, source_target_pairs={{0,2},{1,3},{2,0},{3,1},{4,6},{5,7},{6,4},{7,5},{8,10},{9,11},{10,... | collective-permute-start | bytes 1572872 | tf_op jit(solution)/shard_map/ppermute | solution.py:545
  72.4 6.7 %collective-permute-start.20 = (bf16[256,512]{1,0:T(8,128)(2,1)S(1)}, bf16[256,512]{1,0:T(8,128)(2,1)S(1)}, u32[]{:S(2)}, u32[]{:S(2)}) collective-permute-start(bf16[256,512]{1,0:T(8,128)(2,1)S(1)} %get-tuple-element.49), channel_id=1, source_target_pairs={{0,1},{1,0},{2,3},{3,2},{4,5},{5,4},{6,7},{7,6},{8,9},{9,8},{10,11... | collective-permute-start | bytes 786440 | tf_op jit(solution)/shard_map/ppermute | solution.py:545
  72.5 14.4 %collective-permute-start.17 = (bf16[256,1024]{1,0:T(8,128)(2,1)S(1)}, bf16[256,1024]{1,0:T(8,128)(2,1)S(1)}, u32[]{:S(2)}, u32[]{:S(2)}) collective-permute-start(bf16[256,1024]{1,0:T(8,128)(2,1)S(1)} %choose.5.refs_1_.refs_5_.refs_10_), channel_id=1, source_target_pairs={{0,16},{16,0},{1,17},{17,1},{2,18},{18,2},{3,19},{19,3},{4,20},{20... | collective-permute-start | bytes 1572872 | tf_op jit(solution)/shard_map/ppermute | solution.py:553
  74.9 21.1 %collective-permute-start.27 = (bf16[544,512]{1,0:T(8,128)(2,1)S(1)}, bf16[544,512]{1,0:T(8,128)(2,1)S(1)}, u32[]{:S(2)}, u32[]{:S(2)}) collective-permute-start(bf16[544,512]{1,0:T(8,128)(2,1)S(1)} %get-tuple-element.46.refs_1_), channel_id=1, source_target_pairs={{4,0},{5,1},{6,2},{7,3},{0,4},{1,5},{2,6},{3,7},{12,8},{13,9},{14,... | collective-permute-start | bytes 1671176 | tf_op jit(solution)/shard_map/ppermute | solution.py:548
  76.6 4.0 %collective-permute-start.21 = (bf16[256,512]{1,0:T(8,128)(2,1)S(1)}, bf16[256,512]{1,0:T(8,128)(2,1)S(1)}, u32[]{:S(2)}, u32[]{:S(2)}) collective-permute-start(bf16[256,512]{1,0:T(8,128)(2,1)S(1)} %slice.25), channel_id=1, source_target_pairs={{0,1},{1,0},{2,3},{3,2},{4,5},{5,4},{6,7},{7,6},{8,9},{9,8},{10,11... | collective-permute-start | bytes 786440 | tf_op jit(solution)/shard_map/ppermute | solution.py:545
  78.5 20.2 %collective-permute-start.25 = (bf16[256,512]{1,0:T(8,128)(2,1)S(1)}, bf16[256,512]{1,0:T(8,128)(2,1)S(1)}, u32[]{:S(2)}, u32[]{:S(2)}) collective-permute-start(bf16[256,512]{1,0:T(8,128)(2,1)S(1)} %get-tuple-element.55), channel_id=1, source_target_pairs={{0,1},{1,0},{2,3},{3,2},{4,5},{5,4},{6,7},{7,6},{8,9},{9,8},{10,11... | collective-permute-start | bytes 786440 | tf_op jit(solution)/shard_map/ppermute | solution.py:545
  79.0 13.9 %collective-permute-start.19 = (bf16[512,512]{1,0:T(8,128)(2,1)S(1)}, bf16[512,512]{1,0:T(8,128)(2,1)S(1)}, u32[]{:S(2)}, u32[]{:S(2)}) collective-permute-start(bf16[512,512]{1,0:T(8,128)(2,1)S(1)} %get-tuple-element.48), channel_id=1, source_target_pairs={{0,2},{1,3},{2,0},{3,1},{4,6},{5,7},{6,4},{7,5},{8,10},{9,11},{10,... | collective-permute-start | bytes 1572872 | tf_op jit(solution)/shard_map/ppermute | solution.py:545
  80.6 13.9 %collective-permute-start.28 = (bf16[544,512]{1,0:T(8,128)(2,1)S(1)}, bf16[544,512]{1,0:T(8,128)(2,1)S(1)}, u32[]{:S(2)}, u32[]{:S(2)}) collective-permute-start(bf16[544,512]{1,0:T(8,128)(2,1)S(1)} %get-tuple-element.59), channel_id=1, source_target_pairs={{8,4},{9,5},{10,6},{11,7},{4,8},{5,9},{6,10},{7,11},{24,20},{25,21... | collective-permute-start | bytes 1671176 | tf_op jit(solution)/shard_map/ppermute | solution.py:548
  93.9 17.4 %collective-permute-start.22 = (bf16[256,256]{1,0:T(8,128)(2,1)S(1)}, bf16[256,256]{1,0:T(8,128)(2,1)S(1)}, u32[]{:S(2)}, u32[]{:S(2)}) collective-permute-start(bf16[256,256]{1,0:T(8,128)(2,1)S(1)} %get-tuple-element.53), channel_id=1, source_target_pairs={{0,1},{1,0},{2,3},{3,2},{4,5},{5,4},{6,7},{7,6},{8,9},{9,8},{10,11... | collective-permute-start | bytes 393224 | tf_op jit(solution)/shard_map/ppermute | solution.py:545
  94.0 5.9 %collective-permute-start.26 = (bf16[256,512]{1,0:T(8,128)(2,1)S(1)}, bf16[256,512]{1,0:T(8,128)(2,1)S(1)}, u32[]{:S(2)}, u32[]{:S(2)}) collective-permute-start(bf16[256,512]{1,0:T(8,128)(2,1)S(1)} %slice.27), channel_id=1, source_target_pairs={{0,1},{1,0},{2,3},{3,2},{4,5},{5,4},{6,7},{7,6},{8,9},{9,8},{10,11... | collective-permute-start | bytes 786440 | tf_op jit(solution)/shard_map/ppermute | solution.py:545
  94.5 12.8 %collective-permute-start.23 = (bf16[512,256]{1,0:T(8,128)(2,1)S(1)}, bf16[512,256]{1,0:T(8,128)(2,1)S(1)}, u32[]{:S(2)}, u32[]{:S(2)}) collective-permute-start(bf16[512,256]{1,0:T(8,128)(2,1)S(1)} %get-tuple-element.54), channel_id=1, source_target_pairs={{0,2},{1,3},{2,0},{3,1},{4,6},{5,7},{6,4},{7,5},{8,10},{9,11},{10,... | collective-permute-start | bytes 786440 | tf_op jit(solution)/shard_map/ppermute | solution.py:545
  96.7 5.4 %collective-permute-start.32 = (bf16[32,512]{1,0:T(8,128)(2,1)S(1)}, bf16[32,512]{1,0:T(8,128)(2,1)S(1)}, u32[]{:S(2)}, u32[]{:S(2)}) collective-permute-start(bf16[32,512]{1,0:T(8,128)(2,1)S(1)} %get-tuple-element.62.refs_0_), channel_id=1, source_target_pairs={{0,12},{1,13},{2,14},{3,15},{4,0},{5,1},{6,2},{7,3},{8,4},{9,5},{1... | collective-permute-start | bytes 98312 | tf_op jit(solution)/shard_map/ppermute | solution.py:548
  98.7 5.0 %collective-permute-start.31 = (bf16[32,512]{1,0:T(8,128)(2,1)S(1)}, bf16[32,512]{1,0:T(8,128)(2,1)S(1)}, u32[]{:S(2)}, u32[]{:S(2)}) collective-permute-start(bf16[32,512]{1,0:T(8,128)(2,1)S(1)} %get-tuple-element.62.refs_0_), channel_id=1, source_target_pairs={{0,8},{1,9},{2,10},{3,11},{4,12},{5,13},{6,14},{7,15},{8,0},{9,1},... | collective-permute-start | bytes 98312 | tf_op jit(solution)/shard_map/ppermute | solution.py:548
  99.9 5.7 %collective-permute-start.30 = (bf16[32,512]{1,0:T(8,128)(2,1)S(1)}, bf16[32,512]{1,0:T(8,128)(2,1)S(1)}, u32[]{:S(2)}, u32[]{:S(2)}) collective-permute-start(bf16[32,512]{1,0:T(8,128)(2,1)S(1)} %get-tuple-element.62.refs_0_), channel_id=1, source_target_pairs={{0,4},{1,5},{2,6},{3,7},{4,8},{5,9},{6,10},{7,11},{8,12},{9,13},{1... | collective-permute-start | bytes 98312 | tf_op jit(solution)/shard_map/ppermute | solution.py:548
  102.1 7.8 %collective-permute-start.29 = (bf16[256,512]{1,0:T(8,128)(2,1)S(1)}, bf16[256,512]{1,0:T(8,128)(2,1)S(1)}, u32[]{:S(2)}, u32[]{:S(2)}) collective-permute-start(bf16[256,512]{1,0:T(8,128)(2,1)S(1)} %get-tuple-element.61), channel_id=1, source_target_pairs={{0,2},{1,3},{2,0},{3,1},{4,6},{5,7},{6,4},{7,5},{8,10},{9,11},{10,... | collective-permute-start | bytes 786440 | tf_op jit(solution)/shard_map/ppermute | solution.py:545
  105.7 5.7 %collective-permute-start.34 = (bf16[128,512]{1,0:T(8,128)(2,1)S(1)}, bf16[128,512]{1,0:T(8,128)(2,1)S(1)}, u32[]{:S(2)}, u32[]{:S(2)}) collective-permute-start(bf16[128,512]{1,0:T(8,128)(2,1)S(1)} %quarter.1.refs_0_.q0), channel_id=1, source_target_pairs={{0,2},{1,3},{2,0},{3,1},{4,6},{5,7},{6,4},{7,5},{8,10},{9,11},{10,... | collective-permute-start | bytes 393224 | tf_op jit(solution)/shard_map/ppermute | solution.py:545
  107.3 4.9 %collective-permute-start.33 = (bf16[128,512]{1,0:T(8,128)(2,1)S(1)}, bf16[128,512]{1,0:T(8,128)(2,1)S(1)}, u32[]{:S(2)}, u32[]{:S(2)}) collective-permute-start(bf16[128,512]{1,0:T(8,128)(2,1)S(1)} %quarter.1.refs_0_.q0), channel_id=1, source_target_pairs={{0,1},{1,0},{2,3},{3,2},{4,5},{5,4},{6,7},{7,6},{8,9},{9,8},{10,11... | collective-permute-start | bytes 393224 | tf_op jit(solution)/shard_map/ppermute | solution.py:545
  107.3 4.1 %collective-permute-start.24 = (bf16[256,256]{1,0:T(8,128)(2,1)S(1)}, bf16[256,256]{1,0:T(8,128)(2,1)S(1)}, u32[]{:S(2)}, u32[]{:S(2)}) collective-permute-start(bf16[256,256]{1,0:T(8,128)(2,1)S(1)} %slice.26), channel_id=1, source_target_pairs={{0,1},{1,0},{2,3},{3,2},{4,5},{5,4},{6,7},{7,6},{8,9},{9,8},{10,11... | collective-permute-start | bytes 393224 | tf_op jit(solution)/shard_map/ppermute | solution.py:545
  111.3 1.3 %collective-permute-start.35 = (bf16[128,512]{1,0:T(8,128)(2,1)S(1)}, bf16[128,512]{1,0:T(8,128)(2,1)S(1)}, u32[]{:S(2)}, u32[]{:S(2)}) collective-permute-start(bf16[128,512]{1,0:T(8,128)(2,1)S(1)} %collective-permute-done.34.q2), channel_id=1, source_target_pairs={{0,1},{1,0},{2,3},{3,2},{4,5},{5,4},{6,7},{7,6},{8,9},{9,8},{10,11... | collective-permute-start | bytes 393224 | tf_op jit(solution)/shard_map/ppermute | solution.py:545
